TPU v7x, 768 devices: a whole 4x8x12 slice. The times are simulated.
768 devices in a mesh: row: 8 (over y), col: 96 (over z, x, core).
Axes of the slice: x: 4, y: 8, z: 12, core: 2. Of those that a mesh axis runs over, the one named last changes fastest.
Arguments:
- image_mantissa: bfloat16 [6144, 1536], P(('row', 'col')), may hold values from -4 to 4
- image_exponent: int32 [6144], P(('row', 'col')), may hold values from -2 to 2
- text_mantissa: bfloat16 [6144, 1536], P(('col', 'row')), may hold values from -4 to 4
- text_exponent: int32 [6144], P(('col', 'row')), may hold values from -2 to 2
- positive: int32 [6144], P('row'), may hold values from 0 to 6143, each once
- logit_scale: float32 [1], replicated, may hold values from 4 to 16
- logit_bias: float32 [1], replicated, may hold values from -4 to -1
Outputs:
- image_grad: float32 [6144, 1536], P(('row', 'col'))
- text_grad: float32 [6144, 1536], P(('col', 'row'))
Inputs may be any that keep to these rules, and one draw needn't show every extreme that they name: positive is a permutation of the 6144 text indices.
All inputs are finite; a program needn't handle non-finite values.
Results may differ from a plain program's by a relative error of at most 0.0041.
Values may be sent and summed in bfloat16 or wider, within the bound.
No kernel may reach another device: no remote copies, remote signals or barrier semaphores. Data moves between devices by JAX's collectives and lax.ppermute only.
A program may use at most 32 MiB of HBM per device.

v0:
```python
import jax
import jax.numpy as jnp
from jax import lax
from jax.sharding import PartitionSpec as P

epsilon = 1e-06


def unit_rows(mantissa, exponent):
    scaled = mantissa.astype(jnp.float32) * jnp.exp2(exponent.astype(jnp.float32))[:, None]
    norm = jnp.sqrt(jnp.sum(scaled * scaled, axis=1, keepdims=True) + epsilon)
    unit = scaled / norm
    return (norm, unit, unit.astype(jnp.bfloat16))


def shards(
    image_mantissa, image_exponent, text_mantissa, text_exponent, positive, logit_scale, logit_bias
):
    image_norm, image_unit, image_half = unit_rows(image_mantissa, image_exponent)
    text_norm, text_unit, text_half = unit_rows(text_mantissa, text_exponent)
    factor = logit_scale[0]
    offset = logit_bias[0]
    all_texts = lax.all_gather(text_half, "row", axis=0, tiled=True)
    text_width = all_texts.shape[0]
    text_ids = lax.axis_index("col") * text_width + jnp.arange(text_width, dtype=jnp.int32)
    images = lax.all_gather(image_half, "col", axis=0, tiled=True)
    logits = factor * jnp.dot(images, all_texts.T, preferred_element_type=jnp.float32) + offset
    label_sign = jnp.where(positive[:, None] == text_ids[None, :], 1.0, -1.0).astype(jnp.float32)
    margin = label_sign * logits
    weights = (-label_sign * jax.nn.sigmoid(-margin)).astype(jnp.bfloat16)
    weight_block = weights
    unit_grad_text = lax.psum_scatter(
        factor * jnp.dot(weight_block.T, images, preferred_element_type=jnp.float32),
        "row",
        scatter_dimension=0,
        tiled=True,
    )
    weight_block = weights
    unit_grad_image = lax.psum_scatter(
        factor * jnp.dot(weight_block, all_texts, preferred_element_type=jnp.float32),
        "col",
        scatter_dimension=0,
        tiled=True,
    )
    image_grad = (
        unit_grad_image - image_unit * jnp.sum(image_unit * unit_grad_image, axis=1, keepdims=True)
    ) / image_norm
    text_grad = (
        unit_grad_text - text_unit * jnp.sum(text_unit * unit_grad_text, axis=1, keepdims=True)
    ) / text_norm
    return (image_grad, text_grad)


def solution(mesh):
    placed = (
        P(("row", "col"), None),
        P(("row", "col")),
        P(("col", "row"), None),
        P(("col", "row")),
        P("row"),
        P(),
        P(),
    )
    return jax.shard_map(
        shards,
        mesh=mesh,
        in_specs=placed,
        out_specs=(P(("row", "col"), None), P(("col", "row"), None)),
        check_vma=False,
    )
```

profile of v0, /device:TPU:6, one launch (start us, length us, event | category | flops | bytes accessed | tf_op | source)
XLA Modules:
  0.0 406.4 jit_solution(2788818732152545761)
XLA Ops:
  7.2 0.0 all-gather.2.cloned.1.call-start
  7.2 0.7 multiply_exponential_fusion.1
  7.9 0.9 multiply_reduce_fusion.3
  8.8 1.4 fusion.9
  10.2 0.0 all-gather.2.cloned.1.call-update
  10.3 0.0 reduce-scatter.5.cloned.1.call-start
  11.6 0.7 multiply_exponential_fusion
  12.3 0.9 multiply_reduce_fusion.2
  13.2 0.8 fusion.10
  14.1 26.3 %all_gather.7 = bf16[64,1536]{1,0:T(8,128)(2,1)S(1)} all-gather(bf16[8,1536]{1,0:T(8,128)(2,1)S(1)} %fusion.10), channel_id=1, replica_groups=mesh['row'=8,'col'=96] {'row'}, dimensions={0}, use_global_device_ids=true | all-gather | bytes 221184 | tf_op jit(solution)/shard_map/all_gather | solution.py:23
  40.3 94.5 %all-gather.2.cloned.1.call-done = bf16[768,1536]{1,0:T(8,128)(2,1)} async-done(((bf16[8,1536]{1,0:T(8,128)(2,1)}), bf16[768,1536]{1,0:T(8,128)(2,1)}) %all-gather.2.cloned.1.call-update) | async-done | bytes 2359312 | tf_op jit(solution)/shard_map/all_gather | solution.py:26
  134.8 0.0 copy-start
  134.8 2.7 fusion.6
  137.5 0.0 copy-done
  137.5 1.3 convolution_multiply_fusion.1
  138.8 0.0 reduce-scatter.5.cloned.1.call-update
  138.8 0.0 reduce-scatter.3.cloned.1.call-start
  138.9 2.9 convolution_multiply_fusion
  141.8 0.0 copy-start.1
  141.8 0.0 copy-start.2
  141.8 0.0 reduce-scatter.3.cloned.1.call-update
  141.8 36.2 %reduce-scatter.5.cloned.1.call-done = f32[8,1536]{1,0:T(8,128)} async-done(((f32[64,1536]{1,0:T(8,128)}), f32[8,1536]{1,0:T(8,128)}) %reduce-scatter.5.cloned.1.call-update) | async-done | bytes 49168 | tf_op jit(solution)/shard_map/reduce_scatter | solution.py:32
  178.0 0.0 copy-done.1
  178.0 1.0 multiply_reduce_fusion
  179.0 1.5 subtract_divide_fusion
  180.5 216.9 %reduce-scatter.3.cloned.1.call-done = f32[8,1536]{1,0:T(8,128)} async-done(((f32[768,1536]{1,0:T(8,128)}), f32[8,1536]{1,0:T(8,128)}) %reduce-scatter.3.cloned.1.call-update) | async-done | bytes 49168 | tf_op jit(solution)/shard_map/reduce_scatter | solution.py:39
  397.3 0.0 copy-done.2
  397.3 1.0 multiply_reduce_fusion.1
  398.3 1.5 subtract_divide_fusion.1
  (3 shorter events, 0.0 us)
Async XLA Ops:
  7.2 127.6 %all-gather.2.cloned.1.call-start = ((), (), s32[]{:S(2)}) async-start(), calls=%async_computation.2 | async-start | bytes 2383872 | tf_op jit(solution)/shard_map/all_gather | solution.py:26
  10.3 167.7 %reduce-scatter.5.cloned.1.call-start = ((), (), s32[]{:S(2)}) async-start(), calls=%async_computation.4 | async-start | bytes 442368 | tf_op jit(solution)/shard_map/reduce_scatter | solution.py:32
  134.8 2.7 copy-start
  138.8 258.5 %reduce-scatter.3.cloned.1.call-start = ((), (), s32[]{:S(2)}) async-start(), calls=%async_computation.3 | async-start | bytes 4767744 | tf_op jit(solution)/shard_map/reduce_scatter | solution.py:39
  141.8 36.2 %copy-start.1 = (bf16[8,1536]{1,0:T(8,128)(2,1)S(1)}, bf16[8,1536]{1,0:T(8,128)(2,1)}, u32[]{:S(2)}) copy-start(bf16[8,1536]{1,0:T(8,128)(2,1)} %param.9) | copy-start | bytes 73732
  141.8 255.5 %copy-start.2 = (bf16[8,1536]{1,0:T(8,128)(2,1)S(1)}, bf16[8,1536]{1,0:T(8,128)(2,1)}, u32[]{:S(2)}) copy-start(bf16[8,1536]{1,0:T(8,128)(2,1)} %param.7) | copy-start | bytes 73732
Sparse Core Ops, SparseCore 0:
  12.2 122.5 all-gather.1
  138.9 38.9 reduce-scatter.4
  184.2 213.1 reduce-scatter.2
where the time goes:
time: 408 us; the launch traced here: 406 us
  waiting for transfers between devices  348 us (85%)
  blocking collectives  26.3 us (6%)
  between operations  15.1 us (4%)
  other arithmetic  10.5 us (3%)
  matrix products  6.9 us (2%)
    reduce_scatter x1, waiting for transfers between devices, shards(): lax.psum_scatter(factor * jnp.dot(weight_block, all_texts, preferred_elem...  217 us
    all_gather x1, waiting for transfers between devices, shards(): images = lax.all_gather(image_half, 'col', axis=0, tiled=True)  94.5 us
    reduce_scatter x1, waiting for transfers between devices, shards(): lax.psum_scatter(factor * jnp.dot(weight_block.T, images, preferred_eleme...  36.2 us
    all_gather x1, blocking collectives, shards(): all_texts = lax.all_gather(text_half, 'row', axis=0, tiled=True)  26.3 us
  transfers between devices with their start and end apart: 3, of which 3 were waited for; matrix products, arithmetic and copies ran while one was open for 2% of the time, Pallas kernels for 0%

commit v1 on v0

v1 whole, which is shorter than its diff:
```python
import jax
import jax.numpy as jnp
from jax import lax
from jax.sharding import Mesh, PartitionSpec as P

epsilon = 1e-06
AXES = ("y", "z", "x", "core")
NY, NZ, NX, NC = 8, 12, 4, 2
R = 8
f32 = jnp.float32
bf16 = jnp.bfloat16


def unit_rows(mantissa, exponent):
    scaled = mantissa.astype(f32) * jnp.exp2(exponent.astype(f32))[:, None]
    norm = jnp.sqrt(jnp.sum(scaled * scaled, axis=1, keepdims=True) + epsilon)
    unit = scaled / norm
    return (norm, unit, unit.astype(bf16))


def exchange(blocks, axis):
    return lax.all_to_all(blocks, axis, split_axis=0, concat_axis=0, tiled=True)


def spread(block, axis, n):
    return exchange(jnp.broadcast_to(block[None], (n,) + block.shape), axis)


def tangent(unit_grad, unit, norm):
    return (unit_grad - unit * jnp.sum(unit * unit_grad, axis=1, keepdims=True)) / norm


def shards(
    image_mantissa, image_exponent, text_mantissa, text_exponent, positive, logit_scale, logit_bias
):
    d = image_mantissa.shape[1]
    image_norm, image_unit, image_half = unit_rows(image_mantissa, image_exponent)
    text_norm, text_unit, text_half = unit_rows(text_mantissa, text_exponent)
    factor = logit_scale[0]
    offset = logit_bias[0]
    z, x, c = lax.axis_index("z"), lax.axis_index("x"), lax.axis_index("core")

    images = spread(image_half, "z", NZ).reshape(NZ * R, d)
    images = lax.all_gather(images, "core", axis=0, tiled=True)
    texts = spread(text_half, "y", NY).reshape(NY * R, d)
    texts = lax.all_gather(texts, "x", axis=0, tiled=True)

    place = positive.reshape(NZ, NX, NC, R)
    place = lax.dynamic_index_in_dim(place, x, axis=1, keepdims=False)
    place = place.transpose(1, 0, 2).reshape(NC * NZ * R)
    xs = jnp.arange(NX, dtype=jnp.int32)[:, None]
    yr = jnp.arange(NY * R, dtype=jnp.int32)[None, :]
    text_ids = (((z * NX + xs) * NC + c) * (NY * R) + yr).reshape(NX * NY * R)

    logits = factor * jnp.dot(images, texts.T, preferred_element_type=f32) + offset
    label_sign = jnp.where(place[:, None] == text_ids[None, :], 1.0, -1.0).astype(f32)
    weights = (-label_sign * jax.nn.sigmoid(-label_sign * logits)).astype(bf16)

    part = factor * jnp.dot(weights, texts, preferred_element_type=f32)
    part = exchange(part.reshape(NC, NZ * R, d), "core").sum(axis=0).astype(bf16)
    part = exchange(part.reshape(NZ, R, d), "z")
    unit_grad_image = part.astype(f32).sum(axis=0)

    part = (factor * jnp.dot(weights.T, images, preferred_element_type=f32)).astype(bf16)
    part = exchange(part.reshape(NX, NY * R, d), "x").astype(f32).sum(axis=0).astype(bf16)
    part = exchange(part.reshape(NY, R, d), "y")
    unit_grad_text = part.astype(f32).sum(axis=0)

    return (
        tangent(unit_grad_image, image_unit, image_norm),
        tangent(unit_grad_text, text_unit, text_norm),
    )


def solution(mesh):
    fine = Mesh(mesh.devices.reshape(NY, NZ, NX, NC), AXES)
    image = ("y", "z", "x", "core")
    text = ("z", "x", "core", "y")
    return jax.shard_map(
        shards,
        mesh=fine,
        in_specs=(P(image, None), P(image), P(text, None), P(text), P("y"), P(), P()),
        out_specs=(P(image, None), P(text, None)),
        check_vma=False,
    )
```

time: 408 us -> 120 us (0.29)
  the two profiles are of different devices: /device:TPU:6 before, /device:TPU:64 now
where the time goes in v1:
time: 120 us
  waiting for transfers between devices  45.2 us (38%)
  starting transfers between devices  38.4 us (32%)
  blocking collectives  21.6 us (18%)
  other arithmetic  8.48 us (7%)
  matrix products  2.03 us (2%)
  between operations  2.03 us (2%)
  local copies, waits for them, and re-layouts  1.73 us (1%)
    all_to_all x5, waiting for transfers between devices, exchange(): return lax.all_to_all(blocks, axis, split_axis=0, concat_axis=0, tiled=True)  45.2 us
    all_to_all x5, starting transfers between devices, exchange(): return lax.all_to_all(blocks, axis, split_axis=0, concat_axis=0, tiled=True)  38.4 us
    all_gather x1, blocking collectives, shards(): texts = lax.all_gather(texts, 'x', axis=0, tiled=True)  14.7 us
    all_to_all x1, blocking collectives, exchange(): return lax.all_to_all(blocks, axis, split_axis=0, concat_axis=0, tiled=True)  4.68 us
  transfers between devices with their start and end apart: 5, of which 4 were waited for; matrix products, arithmetic and copies ran while one was open for 5% of the time, Pallas kernels for 0%

profile of v1, /device:TPU:64, one launch (start us, length us, event | category | flops | bytes accessed | tf_op | source)
XLA Modules:
  0.0 119.5 jit_solution(15429286479996197102)
XLA Ops:
  0.6 0.0 copy-start.2
  0.6 0.7 multiply_exponential_fusion
  1.3 0.9 multiply_reduce_fusion.2
  2.3 0.8 fusion.12
  3.1 0.7 broadcast_in_dim.13
  3.8 7.1 %all-to-all-start.1 = ((bf16[8,8,1536]{2,1,0:T(8,128)(2,1)}), bf16[8,8,1536]{2,1,0:T(8,128)(2,1)S(1)}, u32[]{:S(2)}, u32[]{:S(2)}) async-start(bf16[8,8,1536]{2,1,0:T(8,128)(2,1)} %broadcast_in_dim.13), calls=%async_computation.1 | async-start | bytes 393216 | tf_op jit(solution)/shard_map/all_to_all | solution.py:22
  10.9 0.7 multiply_exponential_fusion.1
  11.5 0.9 multiply_reduce_fusion.3
  12.5 0.8 fusion.11
  13.3 8.0 %all-to-all-done.1 = bf16[8,8,1536]{2,1,0:T(8,128)(2,1)S(1)} async-done(((bf16[8,8,1536]{2,1,0:T(8,128)(2,1)}), bf16[8,8,1536]{2,1,0:T(8,128)(2,1)S(1)}, u32[]{:S(2)}, u32[]{:S(2)}) %all-to-all-start.1) | async-done | bytes 196640 | tf_op jit(solution)/shard_map/all_to_all | solution.py:22
  21.3 0.7 broadcast_in_dim.12
  22.1 14.8 %all-to-all-start = ((bf16[12,8,1536]{2,1,0:T(8,128)(2,1)}), bf16[12,8,1536]{2,1,0:T(8,128)(2,1)S(1)}, u32[]{:S(2)}, u32[]{:S(2)}) async-start(bf16[12,8,1536]{2,1,0:T(8,128)(2,1)} %broadcast_in_dim.12), calls=%async_computation | async-start | bytes 589824 | tf_op jit(solution)/shard_map/all_to_all | solution.py:22
  38.1 0.1 iota_add_fusion
  38.2 0.1 add.79
  38.3 0.0 copy-done.2
  38.3 0.1 reshape.69
  38.5 0.1 eq.15
  38.6 14.7 %all_gather.7 = bf16[256,1536]{1,0:T(8,128)(2,1)S(1)} all-gather(bf16[64,1536]{1,0:T(8,128)(2,1)S(1)} %bitcast.27), channel_id=1, replica_groups=mesh['y'=8,'z'=12,'x'=4,'core'=2] {'x'}, dimensions={0}, use_global_device_ids=true | all-gather | bytes 983040 | tf_op jit(solution)/shard_map/all_gather | solution.py:46
  53.3 0.0 all-to-all-done
  53.3 2.2 %all_gather.6 = bf16[192,1536]{1,0:T(8,128)(2,1)S(1)} all-gather(bf16[96,1536]{1,0:T(8,128)(2,1)S(1)} %bitcast.26), channel_id=1, replica_groups=mesh['y'=8,'z'=12,'x'=4,'core'=2] {'core'}, dimensions={0}, use_global_device_ids=true | all-gather | bytes 884736 | tf_op jit(solution)/shard_map/all_gather | solution.py:44
  55.5 0.4 fusion.8
  55.9 1.3 %fusion = bf16[256,1536]{1,0:T(8,128)(2,1)} fusion(bf16[192,256]{1,0:T(8,128)(2,1)S(1)} %fusion.8, bf16[192,1536]{1,0:T(8,128)(2,1)S(1)} %all_gather.6, f32[]{:T(128)} %bitcast.23), kind=kOutput, calls=%fused_computation.2 | convolution fusion | flops 151781376 | bytes 1474564 | tf_op jit(solution)/shard_map/dot_general | solution.py:64
  57.2 0.3 convolution_multiply_fusion.1
  57.5 4.7 %all_to_all.30 = f32[2,96,1536]{2,1,0:T(8,128)S(1)} all-to-all(f32[2,96,1536]{2,1,0:T(8,128)S(1)} %bitcast.25), channel_id=1, replica_groups=mesh['y'=8,'z'=12,'x'=4,'core'=2] {'core'}, dimensions={0} | all-to-all | bytes 2359296 | tf_op jit(solution)/shard_map/all_to_all | solution.py:22
  62.2 3.5 %all-to-all-start.4 = ((bf16[4,64,1536]{2,1,0:T(8,128)(2,1)}), bf16[4,64,1536]{2,1,0:T(8,128)(2,1)S(1)}, u32[]{:S(2)}, u32[]{:S(2)}) async-start(bf16[4,64,1536]{2,1,0:T(8,128)(2,1)} %bitcast.9), calls=%async_computation.4 | async-start | bytes 1572864 | tf_op jit(solution)/shard_map/all_to_all | solution.py:22
  65.7 0.8 reduce_sum.77
  66.6 0.0 copy-start
  66.6 12.0 %all-to-all-done.4 = bf16[4,64,1536]{2,1,0:T(8,128)(2,1)S(1)} async-done(((bf16[4,64,1536]{2,1,0:T(8,128)(2,1)}), bf16[4,64,1536]{2,1,0:T(8,128)(2,1)S(1)}, u32[]{:S(2)}, u32[]{:S(2)}) %all-to-all-start.4) | async-done | bytes 786464 | tf_op jit(solution)/shard_map/all_to_all | solution.py:22
  78.6 9.6 %all-to-all-start.3 = ((bf16[12,8,1536]{2,1,0:T(8,128)(2,1)}), bf16[12,8,1536]{2,1,0:T(8,128)(2,1)S(1)}, u32[]{:S(2)}, u32[]{:S(2)}) async-start(bf16[12,8,1536]{2,1,0:T(8,128)(2,1)} %bitcast.13), calls=%async_computation.3 | async-start | bytes 589824 | tf_op jit(solution)/shard_map/all_to_all | solution.py:22
  88.2 0.0 copy-start.1
  88.2 0.8 reduce_sum.80
  89.0 15.3 %all-to-all-done.3 = bf16[12,8,1536]{2,1,0:T(8,128)(2,1)S(1)} async-done(((bf16[12,8,1536]{2,1,0:T(8,128)(2,1)}), bf16[12,8,1536]{2,1,0:T(8,128)(2,1)S(1)}, u32[]{:S(2)}, u32[]{:S(2)}) %all-to-all-start.3) | async-done | bytes 294944 | tf_op jit(solution)/shard_map/all_to_all | solution.py:22
  104.3 3.4 %all-to-all-start.5 = ((bf16[8,8,1536]{2,1,0:T(8,128)(2,1)}), bf16[8,8,1536]{2,1,0:T(8,128)(2,1)S(1)}, u32[]{:S(2)}, u32[]{:S(2)}) async-start(bf16[8,8,1536]{2,1,0:T(8,128)(2,1)} %bitcast.10), calls=%async_computation.5 | async-start | bytes 393216 | tf_op jit(solution)/shard_map/all_to_all | solution.py:22
  107.8 0.0 copy-done
  107.8 0.2 multiply_reduce_fusion.1
  108.0 0.7 subtract_divide_fusion.1
  108.7 9.9 %all-to-all-done.5 = bf16[8,8,1536]{2,1,0:T(8,128)(2,1)S(1)} async-done(((bf16[8,8,1536]{2,1,0:T(8,128)(2,1)}), bf16[8,8,1536]{2,1,0:T(8,128)(2,1)S(1)}, u32[]{:S(2)}, u32[]{:S(2)}) %all-to-all-start.5) | async-done | bytes 196640 | tf_op jit(solution)/shard_map/all_to_all | solution.py:22
  118.6 0.0 copy-done.1
  118.6 0.2 multiply_reduce_fusion
  118.8 0.7 subtract_divide_fusion
  (7 shorter events, 0.1 us)
Async XLA Ops:
  0.6 37.7 %copy-start.2 = (s32[768]{0:T(1024)S(1)}, s32[768]{0:T(1024)}, u32[]{:S(2)}) copy-start(s32[768]{0:T(1024)} %param.11) | copy-start | bytes 9220
  3.8 17.6 %all-to-all-start.1 = ((bf16[8,8,1536]{2,1,0:T(8,128)(2,1)}), bf16[8,8,1536]{2,1,0:T(8,128)(2,1)S(1)}, u32[]{:S(2)}, u32[]{:S(2)}) async-start(bf16[8,8,1536]{2,1,0:T(8,128)(2,1)} %broadcast_in_dim.13), calls=%async_computation.1 | async-start | bytes 393216 | tf_op jit(solution)/shard_map/all_to_all | solution.py:22
  22.1 31.2 %all-to-all-start = ((bf16[12,8,1536]{2,1,0:T(8,128)(2,1)}), bf16[12,8,1536]{2,1,0:T(8,128)(2,1)S(1)}, u32[]{:S(2)}, u32[]{:S(2)}) async-start(bf16[12,8,1536]{2,1,0:T(8,128)(2,1)} %broadcast_in_dim.12), calls=%async_computation | async-start | bytes 589824 | tf_op jit(solution)/shard_map/all_to_all | solution.py:22
  62.2 16.3 %all-to-all-start.4 = ((bf16[4,64,1536]{2,1,0:T(8,128)(2,1)}), bf16[4,64,1536]{2,1,0:T(8,128)(2,1)S(1)}, u32[]{:S(2)}, u32[]{:S(2)}) async-start(bf16[4,64,1536]{2,1,0:T(8,128)(2,1)} %bitcast.9), calls=%async_computation.4 | async-start | bytes 1572864 | tf_op jit(solution)/shard_map/all_to_all | solution.py:22
  66.6 41.2 %copy-start = (bf16[8,1536]{1,0:T(8,128)(2,1)S(1)}, bf16[8,1536]{1,0:T(8,128)(2,1)}, u32[]{:S(2)}) copy-start(bf16[8,1536]{1,0:T(8,128)(2,1)} %param.7) | copy-start | bytes 73732
  78.6 25.8 %all-to-all-start.3 = ((bf16[12,8,1536]{2,1,0:T(8,128)(2,1)}), bf16[12,8,1536]{2,1,0:T(8,128)(2,1)S(1)}, u32[]{:S(2)}, u32[]{:S(2)}) async-start(bf16[12,8,1536]{2,1,0:T(8,128)(2,1)} %bitcast.13), calls=%async_computation.3 | async-start | bytes 589824 | tf_op jit(solution)/shard_map/all_to_all | solution.py:22
  88.2 30.4 %copy-start.1 = (bf16[8,1536]{1,0:T(8,128)(2,1)S(1)}, bf16[8,1536]{1,0:T(8,128)(2,1)}, u32[]{:S(2)}) copy-start(bf16[8,1536]{1,0:T(8,128)(2,1)} %param.9) | copy-start | bytes 73732
  104.3 14.2 %all-to-all-start.5 = ((bf16[8,8,1536]{2,1,0:T(8,128)(2,1)}), bf16[8,8,1536]{2,1,0:T(8,128)(2,1)S(1)}, u32[]{:S(2)}, u32[]{:S(2)}) async-start(bf16[8,8,1536]{2,1,0:T(8,128)(2,1)} %bitcast.10), calls=%async_computation.5 | async-start | bytes 393216 | tf_op jit(solution)/shard_map/all_to_all | solution.py:22

commit v2 on v1

--- a/solution.py
+++ b/solution.py
@@ -26,6 +26,10 @@
     return exchange(jnp.broadcast_to(block[None], (n,) + block.shape), axis)
 
 
+def shift(block, axis, n, k):
+    return lax.ppermute(block, axis, [(i, (i + k) % n) for i in range(n)])
+
+
 def tangent(unit_grad, unit, norm):
     return (unit_grad - unit * jnp.sum(unit * unit_grad, axis=1, keepdims=True)) / norm
 
@@ -34,36 +38,41 @@
     image_mantissa, image_exponent, text_mantissa, text_exponent, positive, logit_scale, logit_bias
 ):
     d = image_mantissa.shape[1]
+    text_norm, text_unit, text_half = unit_rows(text_mantissa, text_exponent)
     image_norm, image_unit, image_half = unit_rows(image_mantissa, image_exponent)
-    text_norm, text_unit, text_half = unit_rows(text_mantissa, text_exponent)
     factor = logit_scale[0]
     offset = logit_bias[0]
     z, x, c = lax.axis_index("z"), lax.axis_index("x"), lax.axis_index("core")
 
+    texts = spread(text_half, "y", NY).reshape(NY * R, d)
     images = spread(image_half, "z", NZ).reshape(NZ * R, d)
-    images = lax.all_gather(images, "core", axis=0, tiled=True)
-    texts = spread(text_half, "y", NY).reshape(NY * R, d)
-    texts = lax.all_gather(texts, "x", axis=0, tiled=True)
+    texts = jnp.concatenate([texts] + [shift(texts, "x", NX, k) for k in range(1, NX)], axis=0)
+    texts = jnp.concatenate([texts, shift(texts, "core", NC, 1)], axis=0)
 
-    place = positive.reshape(NZ, NX, NC, R)
-    place = lax.dynamic_index_in_dim(place, x, axis=1, keepdims=False)
-    place = place.transpose(1, 0, 2).reshape(NC * NZ * R)
-    xs = jnp.arange(NX, dtype=jnp.int32)[:, None]
-    yr = jnp.arange(NY * R, dtype=jnp.int32)[None, :]
-    text_ids = (((z * NX + xs) * NC + c) * (NY * R) + yr).reshape(NX * NY * R)
+    place = positive.reshape(NZ, NX * NC, R)
+    place = lax.dynamic_index_in_dim(place, x * NC + c, axis=1, keepdims=False).reshape(NZ * R)
+    cs = (c + jnp.arange(NC, dtype=jnp.int32)[:, None, None]) % NC
+    xs = (x + NX - jnp.arange(NX, dtype=jnp.int32)[None, :, None]) % NX
+    yr = jnp.arange(NY * R, dtype=jnp.int32)[None, None, :]
+    text_ids = (((z * NX + xs) * NC + cs) * (NY * R) + yr).reshape(NC * NX * NY * R)
 
     logits = factor * jnp.dot(images, texts.T, preferred_element_type=f32) + offset
     label_sign = jnp.where(place[:, None] == text_ids[None, :], 1.0, -1.0).astype(f32)
     weights = (-label_sign * jax.nn.sigmoid(-label_sign * logits)).astype(bf16)
 
-    part = factor * jnp.dot(weights, texts, preferred_element_type=f32)
-    part = exchange(part.reshape(NC, NZ * R, d), "core").sum(axis=0).astype(bf16)
+    near = NX * NY * R
+    far_part = (factor * jnp.dot(weights[:, near:].T, images, preferred_element_type=f32)).astype(bf16)
+    far_part = shift(far_part, "core", NC, 1)
+    part = (factor * jnp.dot(weights, texts, preferred_element_type=f32)).astype(bf16)
     part = exchange(part.reshape(NZ, R, d), "z")
     unit_grad_image = part.astype(f32).sum(axis=0)
 
-    part = (factor * jnp.dot(weights.T, images, preferred_element_type=f32)).astype(bf16)
-    part = exchange(part.reshape(NX, NY * R, d), "x").astype(f32).sum(axis=0).astype(bf16)
-    part = exchange(part.reshape(NY, R, d), "y")
+    own = factor * jnp.dot(weights[:, :near].T, images, preferred_element_type=f32)
+    own = (own + far_part.astype(f32)).astype(bf16).reshape(NX, NY * R, d)
+    total = own[0].astype(f32)
+    for k in range(1, NX):
+        total = total + shift(own[k], "x", NX, -k).astype(f32)
+    part = exchange(total.astype(bf16).reshape(NY, R, d), "y")
     unit_grad_text = part.astype(f32).sum(axis=0)
 
     return (

time: 120 us -> 105 us (0.88)
  the two profiles are of different devices: /device:TPU:64 before, /device:TPU:6 now
where the time goes in v2:
time: 105 us; the launch traced here: 104 us
  starting transfers between devices  55.6 us (53%)
  waiting for transfers between devices  34.1 us (32%)
  other arithmetic  7.74 us (7%)
  matrix products  2.52 us (2%)
  between operations  2.23 us (2%)
  local copies, waits for them, and re-layouts  1.86 us (2%)
    all_to_all x4, starting transfers between devices, exchange(): return lax.all_to_all(blocks, axis, split_axis=0, concat_axis=0, tiled=True)  35.1 us
    all_to_all x4, waiting for transfers between devices, exchange(): return lax.all_to_all(blocks, axis, split_axis=0, concat_axis=0, tiled=True)  25.3 us
    ppermute x8, starting transfers between devices, shift(): return lax.ppermute(block, axis, [(i, (i + k) % n) for i in range(n)])  20.5 us
    ppermute x8, waiting for transfers between devices, shift(): return lax.ppermute(block, axis, [(i, (i + k) % n) for i in range(n)])  8.8 us
  transfers between devices with their start and end apart: 12, of which 6 were waited for; matrix products, arithmetic and copies ran while one was open for 5% of the time, Pallas kernels for 0%

profile of v2, /device:TPU:6, one launch (start us, length us, event | category | flops | bytes accessed | tf_op | source)
XLA Modules:
  0.0 104.0 jit_solution(15606437517372982365)
XLA Ops:
  0.6 0.7 multiply_exponential_fusion
  1.3 0.9 multiply_reduce_fusion.2
  2.3 0.8 fusion.24
  3.1 0.7 broadcast_in_dim.13
  3.8 7.1 %all-to-all-start.1 = ((bf16[8,8,1536]{2,1,0:T(8,128)(2,1)}), bf16[8,8,1536]{2,1,0:T(8,128)(2,1)S(1)}, u32[]{:S(2)}, u32[]{:S(2)}) async-start(bf16[8,8,1536]{2,1,0:T(8,128)(2,1)} %broadcast_in_dim.13), calls=%async_computation.1 | async-start | bytes 393216 | tf_op jit(solution)/shard_map/all_to_all | solution.py:22
  10.9 0.7 multiply_exponential_fusion.1
  11.5 0.9 multiply_reduce_fusion.3
  13.8 0.1 add_multiply_fusion
  13.9 0.8 fusion.23
  14.7 6.6 %all-to-all-done.1 = bf16[8,8,1536]{2,1,0:T(8,128)(2,1)S(1)} async-done(((bf16[8,8,1536]{2,1,0:T(8,128)(2,1)}), bf16[8,8,1536]{2,1,0:T(8,128)(2,1)S(1)}, u32[]{:S(2)}, u32[]{:S(2)}) %all-to-all-start.1) | async-done | bytes 196640 | tf_op jit(solution)/shard_map/all_to_all | solution.py:22
  21.3 0.7 broadcast_in_dim.12
  22.1 15.2 %all-to-all-start = ((bf16[12,8,1536]{2,1,0:T(8,128)(2,1)}), bf16[12,8,1536]{2,1,0:T(8,128)(2,1)S(1)}, u32[]{:S(2)}, u32[]{:S(2)}) async-start(bf16[12,8,1536]{2,1,0:T(8,128)(2,1)} %broadcast_in_dim.12), calls=%async_computation | async-start | bytes 589824 | tf_op jit(solution)/shard_map/all_to_all | solution.py:22
  37.2 2.4 %collective-permute-start = (bf16[64,1536]{1,0:T(8,128)(2,1)S(1)}, bf16[64,1536]{1,0:T(8,128)(2,1)S(1)}, u32[]{:S(2)}, u32[]{:S(2)}) collective-permute-start(bf16[64,1536]{1,0:T(8,128)(2,1)S(1)} %bitcast.23), channel_id=1, source_target_pairs={{0,2},{2,4},{4,6},{6,0},{1,3},{3,5},{5,7},{7,1},{8,10},{10,12},{12... | collective-permute-start | bytes 589832 | tf_op jit(solution)/shard_map/ppermute | solution.py:30
  39.6 4.3 %collective-permute-start.1 = (bf16[64,1536]{1,0:T(8,128)(2,1)S(1)}, bf16[64,1536]{1,0:T(8,128)(2,1)S(1)}, u32[]{:S(2)}, u32[]{:S(2)}) collective-permute-start(bf16[64,1536]{1,0:T(8,128)(2,1)S(1)} %bitcast.24), channel_id=1, source_target_pairs={{0,4},{2,6},{4,0},{6,2},{1,5},{3,7},{5,1},{7,3},{8,12},{10,14},{12... | collective-permute-start | bytes 589832 | tf_op jit(solution)/shard_map/ppermute | solution.py:30
  44.0 1.9 %collective-permute-start.2 = (bf16[64,1536]{1,0:T(8,128)(2,1)S(1)}, bf16[64,1536]{1,0:T(8,128)(2,1)S(1)}, u32[]{:S(2)}, u32[]{:S(2)}) collective-permute-start(bf16[64,1536]{1,0:T(8,128)(2,1)S(1)} %bitcast.25), channel_id=1, source_target_pairs={{0,6},{2,0},{4,2},{6,4},{1,7},{3,1},{5,3},{7,5},{8,14},{10,8},{12,... | collective-permute-start | bytes 589832 | tf_op jit(solution)/shard_map/ppermute | solution.py:30
  45.9 0.1 iota_add_fusion
  46.0 0.1 add.144
  46.0 0.1 reshape.144
  46.2 0.1 eq.19
  46.3 4.4 %collective-permute-done.1 = bf16[64,1536]{1,0:T(8,128)(2,1)S(1)} collective-permute-done((bf16[64,1536]{1,0:T(8,128)(2,1)S(1)}, bf16[64,1536]{1,0:T(8,128)(2,1)S(1)}, u32[]{:S(2)}, u32[]{:S(2)}) %collective-permute-start.1) | collective-permute-done | bytes 196640 | tf_op jit(solution)/shard_map/ppermute | solution.py:30
  50.6 2.3 %collective-permute-done.2 = bf16[64,1536]{1,0:T(8,128)(2,1)S(1)} collective-permute-done((bf16[64,1536]{1,0:T(8,128)(2,1)S(1)}, bf16[64,1536]{1,0:T(8,128)(2,1)S(1)}, u32[]{:S(2)}, u32[]{:S(2)}) %collective-permute-start.2) | collective-permute-done | bytes 196640 | tf_op jit(solution)/shard_map/ppermute | solution.py:30
  52.9 0.1 pad_maximum_fusion
  53.0 1.9 %collective-permute-start.3 = (bf16[256,1536]{1,0:T(8,128)(2,1)S(1)}, bf16[256,1536]{1,0:T(8,128)(2,1)S(1)}, u32[]{:S(2)}, u32[]{:S(2)}) collective-permute-start(bf16[256,1536]{1,0:T(8,128)(2,1)S(1)} %pad_maximum_fusion), channel_id=1, source_target_pairs={{0,1},{1,0},{2,3},{3,2},{4,5},{5,4},{6,7},{7,6},{8,9},{9,8},{10,11... | collective-permute-start | bytes 2359304 | tf_op jit(solution)/shard_map/ppermute | solution.py:30
  55.0 2.2 %collective-permute-done.3 = bf16[256,1536]{1,0:T(8,128)(2,1)S(1)} collective-permute-done((bf16[256,1536]{1,0:T(8,128)(2,1)S(1)}, bf16[256,1536]{1,0:T(8,128)(2,1)S(1)}, u32[]{:S(2)}, u32[]{:S(2)}) %collective-permute-start.3) | collective-permute-done | bytes 786464 | tf_op jit(solution)/shard_map/ppermute | solution.py:30
  57.1 0.1 constant_dynamic-update-slice_fusion
  57.2 0.7 fusion.10
  57.9 0.4 fusion
  58.3 2.0 %collective-permute-start.4 = (bf16[256,1536]{1,0:T(8,128)(2,1)S(1)}, bf16[256,1536]{1,0:T(8,128)(2,1)S(1)}, u32[]{:S(2)}, u32[]{:S(2)}) collective-permute-start(bf16[256,1536]{1,0:T(8,128)(2,1)S(1)} %fusion), channel_id=1, source_target_pairs={{0,1},{1,0},{2,3},{3,2},{4,5},{5,4},{6,7},{7,6},{8,9},{9,8},{10,11... | collective-permute-start | bytes 2359304 | tf_op jit(solution)/shard_map/ppermute | solution.py:30
  60.3 1.1 %fusion.2 = bf16[12,8,1536]{2,1,0:T(8,128)(2,1)} fusion(bf16[96,512]{1,0:T(8,128)(2,1)S(1)} %fusion.10, bf16[512,1536]{1,0:T(8,128)(2,1)S(1)} %constant_dynamic-update-slice_fusion, f32[]{:T(128)} %bitcast.18), kind=kOutput, calls=%fused_computation.5 | convolution fusion | flops 151289856 | bytes 1966084 | tf_op jit(solution)/shard_map/dot_general | solution.py:66
  61.4 9.5 %all-to-all-start.2 = ((bf16[12,8,1536]{2,1,0:T(8,128)(2,1)}), bf16[12,8,1536]{2,1,0:T(8,128)(2,1)S(1)}, u32[]{:S(2)}, u32[]{:S(2)}) async-start(bf16[12,8,1536]{2,1,0:T(8,128)(2,1)} %fusion.2), calls=%async_computation.2 | async-start | bytes 589824 | tf_op jit(solution)/shard_map/all_to_all | solution.py:22
  70.9 0.0 collective-permute-done.4
  70.9 0.0 copy-start
  70.9 0.4 add_convert_fusion
  71.3 0.0 copy-start.1
  71.4 2.5 %collective-permute-start.7 = (bf16[64,1536]{1,0:T(8,128)(2,1)S(1)}, bf16[64,1536]{1,0:T(8,128)(2,1)S(1)}, u32[]{:S(2)}, u32[]{:S(2)}) collective-permute-start(bf16[64,1536]{1,0:T(8,128)(2,1)S(1)} %get-tuple-element.3), channel_id=1, source_target_pairs={{0,2},{2,4},{4,6},{6,0},{1,3},{3,5},{5,7},{7,1},{8,10},{10,12},{12... | collective-permute-start | bytes 589832 | tf_op jit(solution)/shard_map/ppermute | solution.py:30
  73.8 2.7 %collective-permute-start.6 = (bf16[64,1536]{1,0:T(8,128)(2,1)S(1)}, bf16[64,1536]{1,0:T(8,128)(2,1)S(1)}, u32[]{:S(2)}, u32[]{:S(2)}) collective-permute-start(bf16[64,1536]{1,0:T(8,128)(2,1)S(1)} %get-tuple-element.4), channel_id=1, source_target_pairs={{0,4},{2,6},{4,0},{6,2},{1,5},{3,7},{5,1},{7,3},{8,12},{10,14},{12... | collective-permute-start | bytes 589832 | tf_op jit(solution)/shard_map/ppermute | solution.py:30
  76.5 2.8 %collective-permute-start.5 = (bf16[64,1536]{1,0:T(8,128)(2,1)S(1)}, bf16[64,1536]{1,0:T(8,128)(2,1)S(1)}, u32[]{:S(2)}, u32[]{:S(2)}) collective-permute-start(bf16[64,1536]{1,0:T(8,128)(2,1)S(1)} %get-tuple-element.2), channel_id=1, source_target_pairs={{0,6},{2,0},{4,2},{6,4},{1,7},{3,1},{5,3},{7,5},{8,14},{10,8},{12,... | collective-permute-start | bytes 589832 | tf_op jit(solution)/shard_map/ppermute | solution.py:30
  79.3 8.9 %all-to-all-done.2 = bf16[12,8,1536]{2,1,0:T(8,128)(2,1)S(1)} async-done(((bf16[12,8,1536]{2,1,0:T(8,128)(2,1)}), bf16[12,8,1536]{2,1,0:T(8,128)(2,1)S(1)}, u32[]{:S(2)}, u32[]{:S(2)}) %all-to-all-start.2) | async-done | bytes 294944 | tf_op jit(solution)/shard_map/all_to_all | solution.py:22
  88.3 0.2 multiply_reduce_fusion.1
  88.5 0.0 collective-permute-done.7
  88.5 0.0 collective-permute-done.6
  88.5 0.0 collective-permute-done.5
  88.5 0.8 fusion.14
  89.3 3.4 %all-to-all-start.3 = ((bf16[8,8,1536]{2,1,0:T(8,128)(2,1)}), bf16[8,8,1536]{2,1,0:T(8,128)(2,1)S(1)}, u32[]{:S(2)}, u32[]{:S(2)}) async-start(bf16[8,8,1536]{2,1,0:T(8,128)(2,1)} %fusion.14), calls=%async_computation.3 | async-start | bytes 393216 | tf_op jit(solution)/shard_map/all_to_all | solution.py:22
  92.7 0.7 subtract_divide_fusion.1
  93.4 9.7 %all-to-all-done.3 = bf16[8,8,1536]{2,1,0:T(8,128)(2,1)S(1)} async-done(((bf16[8,8,1536]{2,1,0:T(8,128)(2,1)}), bf16[8,8,1536]{2,1,0:T(8,128)(2,1)S(1)}, u32[]{:S(2)}, u32[]{:S(2)}) %all-to-all-start.3) | async-done | bytes 196640 | tf_op jit(solution)/shard_map/all_to_all | solution.py:22
  103.1 0.2 multiply_reduce_fusion
  103.3 0.7 subtract_divide_fusion
  (18 shorter events, 0.3 us)
Async XLA Ops:
  0.6 45.4 %copy-start.2 = (s32[768]{0:T(1024)S(1)}, s32[768]{0:T(1024)}, u32[]{:S(2)}) copy-start(s32[768]{0:T(1024)} %param.11) | copy-start | bytes 9220
  3.8 17.6 %all-to-all-start.1 = ((bf16[8,8,1536]{2,1,0:T(8,128)(2,1)}), bf16[8,8,1536]{2,1,0:T(8,128)(2,1)S(1)}, u32[]{:S(2)}, u32[]{:S(2)}) async-start(bf16[8,8,1536]{2,1,0:T(8,128)(2,1)} %broadcast_in_dim.13), calls=%async_computation.1 | async-start | bytes 393216 | tf_op jit(solution)/shard_map/all_to_all | solution.py:22
  22.1 35.1 %all-to-all-start = ((bf16[12,8,1536]{2,1,0:T(8,128)(2,1)}), bf16[12,8,1536]{2,1,0:T(8,128)(2,1)S(1)}, u32[]{:S(2)}, u32[]{:S(2)}) async-start(bf16[12,8,1536]{2,1,0:T(8,128)(2,1)} %broadcast_in_dim.12), calls=%async_computation | async-start | bytes 589824 | tf_op jit(solution)/shard_map/all_to_all | solution.py:22
  37.2 9.0 %collective-permute-start = (bf16[64,1536]{1,0:T(8,128)(2,1)S(1)}, bf16[64,1536]{1,0:T(8,128)(2,1)S(1)}, u32[]{:S(2)}, u32[]{:S(2)}) collective-permute-start(bf16[64,1536]{1,0:T(8,128)(2,1)S(1)} %bitcast.23), channel_id=1, source_target_pairs={{0,2},{2,4},{4,6},{6,0},{1,3},{3,5},{5,7},{7,1},{8,10},{10,12},{12... | collective-permute-start | bytes 589832 | tf_op jit(solution)/shard_map/ppermute | solution.py:30
  39.6 11.0 %collective-permute-start.1 = (bf16[64,1536]{1,0:T(8,128)(2,1)S(1)}, bf16[64,1536]{1,0:T(8,128)(2,1)S(1)}, u32[]{:S(2)}, u32[]{:S(2)}) collective-permute-start(bf16[64,1536]{1,0:T(8,128)(2,1)S(1)} %bitcast.24), channel_id=1, source_target_pairs={{0,4},{2,6},{4,0},{6,2},{1,5},{3,7},{5,1},{7,3},{8,12},{10,14},{12... | collective-permute-start | bytes 589832 | tf_op jit(solution)/shard_map/ppermute | solution.py:30
  44.0 8.9 %collective-permute-start.2 = (bf16[64,1536]{1,0:T(8,128)(2,1)S(1)}, bf16[64,1536]{1,0:T(8,128)(2,1)S(1)}, u32[]{:S(2)}, u32[]{:S(2)}) collective-permute-start(bf16[64,1536]{1,0:T(8,128)(2,1)S(1)} %bitcast.25), channel_id=1, source_target_pairs={{0,6},{2,0},{4,2},{6,4},{1,7},{3,1},{5,3},{7,5},{8,14},{10,8},{12,... | collective-permute-start | bytes 589832 | tf_op jit(solution)/shard_map/ppermute | solution.py:30
  53.0 4.2 %collective-permute-start.3 = (bf16[256,1536]{1,0:T(8,128)(2,1)S(1)}, bf16[256,1536]{1,0:T(8,128)(2,1)S(1)}, u32[]{:S(2)}, u32[]{:S(2)}) collective-permute-start(bf16[256,1536]{1,0:T(8,128)(2,1)S(1)} %pad_maximum_fusion), channel_id=1, source_target_pairs={{0,1},{1,0},{2,3},{3,2},{4,5},{5,4},{6,7},{7,6},{8,9},{9,8},{10,11... | collective-permute-start | bytes 2359304 | tf_op jit(solution)/shard_map/ppermute | solution.py:30
  58.3 12.7 %collective-permute-start.4 = (bf16[256,1536]{1,0:T(8,128)(2,1)S(1)}, bf16[256,1536]{1,0:T(8,128)(2,1)S(1)}, u32[]{:S(2)}, u32[]{:S(2)}) collective-permute-start(bf16[256,1536]{1,0:T(8,128)(2,1)S(1)} %fusion), channel_id=1, source_target_pairs={{0,1},{1,0},{2,3},{3,2},{4,5},{5,4},{6,7},{7,6},{8,9},{9,8},{10,11... | collective-permute-start | bytes 2359304 | tf_op jit(solution)/shard_map/ppermute | solution.py:30
  61.4 26.8 %all-to-all-start.2 = ((bf16[12,8,1536]{2,1,0:T(8,128)(2,1)}), bf16[12,8,1536]{2,1,0:T(8,128)(2,1)S(1)}, u32[]{:S(2)}, u32[]{:S(2)}) async-start(bf16[12,8,1536]{2,1,0:T(8,128)(2,1)} %fusion.2), calls=%async_computation.2 | async-start | bytes 589824 | tf_op jit(solution)/shard_map/all_to_all | solution.py:22
  70.9 17.3 %copy-start = (bf16[8,1536]{1,0:T(8,128)(2,1)S(1)}, bf16[8,1536]{1,0:T(8,128)(2,1)}, u32[]{:S(2)}) copy-start(bf16[8,1536]{1,0:T(8,128)(2,1)} %param.7) | copy-start | bytes 73732
  71.3 31.8 %copy-start.1 = (bf16[8,1536]{1,0:T(8,128)(2,1)S(1)}, bf16[8,1536]{1,0:T(8,128)(2,1)}, u32[]{:S(2)}) copy-start(bf16[8,1536]{1,0:T(8,128)(2,1)} %param.9) | copy-start | bytes 73732
  71.4 17.1 %collective-permute-start.7 = (bf16[64,1536]{1,0:T(8,128)(2,1)S(1)}, bf16[64,1536]{1,0:T(8,128)(2,1)S(1)}, u32[]{:S(2)}, u32[]{:S(2)}) collective-permute-start(bf16[64,1536]{1,0:T(8,128)(2,1)S(1)} %get-tuple-element.3), channel_id=1, source_target_pairs={{0,2},{2,4},{4,6},{6,0},{1,3},{3,5},{5,7},{7,1},{8,10},{10,12},{12... | collective-permute-start | bytes 589832 | tf_op jit(solution)/shard_map/ppermute | solution.py:30
  73.8 14.6 %collective-permute-start.6 = (bf16[64,1536]{1,0:T(8,128)(2,1)S(1)}, bf16[64,1536]{1,0:T(8,128)(2,1)S(1)}, u32[]{:S(2)}, u32[]{:S(2)}) collective-permute-start(bf16[64,1536]{1,0:T(8,128)(2,1)S(1)} %get-tuple-element.4), channel_id=1, source_target_pairs={{0,4},{2,6},{4,0},{6,2},{1,5},{3,7},{5,1},{7,3},{8,12},{10,14},{12... | collective-permute-start | bytes 589832 | tf_op jit(solution)/shard_map/ppermute | solution.py:30
  76.5 12.0 %collective-permute-start.5 = (bf16[64,1536]{1,0:T(8,128)(2,1)S(1)}, bf16[64,1536]{1,0:T(8,128)(2,1)S(1)}, u32[]{:S(2)}, u32[]{:S(2)}) collective-permute-start(bf16[64,1536]{1,0:T(8,128)(2,1)S(1)} %get-tuple-element.2), channel_id=1, source_target_pairs={{0,6},{2,0},{4,2},{6,4},{1,7},{3,1},{5,3},{7,5},{8,14},{10,8},{12,... | collective-permute-start | bytes 589832 | tf_op jit(solution)/shard_map/ppermute | solution.py:30
  89.3 13.8 %all-to-all-start.3 = ((bf16[8,8,1536]{2,1,0:T(8,128)(2,1)}), bf16[8,8,1536]{2,1,0:T(8,128)(2,1)S(1)}, u32[]{:S(2)}, u32[]{:S(2)}) async-start(bf16[8,8,1536]{2,1,0:T(8,128)(2,1)} %fusion.14), calls=%async_computation.3 | async-start | bytes 393216 | tf_op jit(solution)/shard_map/all_to_all | solution.py:22

commit v3 on v2

v3 whole, which is shorter than its diff:
```python
import jax
import jax.numpy as jnp
from jax import lax
from jax.experimental import pallas as pl
from jax.experimental.pallas import tpu as pltpu
from jax.sharding import Mesh, PartitionSpec as P

epsilon = 1e-06
AXES = ("y", "z", "x", "core")
NY, NZ, NX, NC = 8, 12, 4, 2
R = 8
f32 = jnp.float32
bf16 = jnp.bfloat16


def prologue_kernel(mantissa_ref, exponent_ref, out_ref, unit_ref, norm_ref):
    row = lax.broadcasted_iota(jnp.int32, (R, 1), 0)
    exponent = jnp.zeros((R, 1), jnp.int32)
    for r in range(R):
        exponent = jnp.where(row == r, exponent_ref[r], exponent)
    scaled = mantissa_ref[...].astype(f32) * jnp.exp2(exponent.astype(f32))
    norm = jnp.sqrt(jnp.sum(scaled * scaled, axis=1, keepdims=True) + epsilon)
    unit = scaled / norm
    norm_ref[...] = norm
    unit_ref[...] = unit
    half = unit.astype(bf16)
    for k in range(out_ref.shape[0]):
        out_ref[k] = half


def prologue(mantissa, exponent, copies):
    return pl.pallas_call(
        prologue_kernel,
        out_shape=(
            jax.ShapeDtypeStruct((copies,) + mantissa.shape, bf16),
            jax.ShapeDtypeStruct(mantissa.shape, f32),
            jax.ShapeDtypeStruct((R, 1), f32),
        ),
        in_specs=[
            pl.BlockSpec(memory_space=pltpu.VMEM),
            pl.BlockSpec(memory_space=pltpu.SMEM),
        ],
        out_specs=(pl.BlockSpec(memory_space=pltpu.VMEM),) * 3,
    )(mantissa, exponent)


def exchange(blocks, axis):
    return lax.all_to_all(blocks, axis, split_axis=0, concat_axis=0, tiled=True)


def shift(block, axis, n, k):
    return lax.ppermute(block, axis, [(i, (i + k) % n) for i in range(n)])


def product(a, b):
    return jnp.dot(a, b, preferred_element_type=f32)


def tangent(unit_grad, unit, norm):
    return (unit_grad - unit * jnp.sum(unit * unit_grad, axis=1, keepdims=True)) / norm


def shards(
    image_mantissa, image_exponent, text_mantissa, text_exponent, positive, logit_scale, logit_bias
):
    d = image_mantissa.shape[1]
    factor = logit_scale[0]
    offset = logit_bias[0]
    z, x, c = lax.axis_index("z"), lax.axis_index("x"), lax.axis_index("core")
    half_rows = NY * R
    near_rows = NX * half_rows

    place = positive.reshape(NZ, NX * NC, R)
    place = lax.dynamic_index_in_dim(place, x * NC + c, axis=1, keepdims=False).reshape(NZ * R)
    place = place - z * (NC * near_rows)
    place = jnp.where((place >= 0) & (place < NC * near_rows), place, -1)

    text_send, text_unit, text_norm = prologue(text_mantissa, text_exponent, NY)
    image_mantissa, place = lax.optimization_barrier((image_mantissa, place))
    image_send, image_unit, image_norm = prologue(image_mantissa, image_exponent, NZ)
    near_texts = lax.all_gather(exchange(text_send, "y").reshape(half_rows, d), "x", axis=0, tiled=True)
    far_texts = shift(near_texts, "core", NC, 1)
    images = exchange(image_send, "z").reshape(NZ * R, d)

    column = jnp.arange(near_rows, dtype=jnp.int32)[None, :]

    def weigh(texts, core):
        logits = factor * product(images, texts.T) + offset
        target = (column // half_rows) * (NC * half_rows) + core * half_rows + column % half_rows
        label_sign = jnp.where(place[:, None] == target, 1.0, -1.0).astype(f32)
        return (-label_sign * jax.nn.sigmoid(-label_sign * logits)).astype(bf16)

    far_weights = weigh(far_texts, 1 - c)
    far_part = (factor * product(far_weights.T, images)).astype(bf16)
    far_part = shift(far_part, "core", NC, 1)
    near_weights = weigh(near_texts, c)
    part = (factor * (product(near_weights, near_texts) + product(far_weights, far_texts))).astype(bf16)
    image_parts = exchange(part.reshape(NZ, R, d), "z")
    unit_grad_image = image_parts.astype(f32).sum(axis=0)

    near_part = factor * product(near_weights.T, images)
    near_part = (near_part + far_part.astype(f32)).astype(bf16).reshape(NX, half_rows, d)
    total = lax.dynamic_index_in_dim(near_part, x, axis=0, keepdims=False).astype(f32)
    for k in range(1, NX):
        block = lax.dynamic_index_in_dim(near_part, (x + k) % NX, axis=0, keepdims=False)
        total = total + shift(block, "x", NX, k).astype(f32)
    total = total.astype(bf16).reshape(NY, R, d)
    total, unit_grad_image = lax.optimization_barrier((total, unit_grad_image))
    unit_grad_text = exchange(total, "y").astype(f32).sum(axis=0)

    return (
        tangent(unit_grad_image, image_unit, image_norm),
        tangent(unit_grad_text, text_unit, text_norm),
    )


def solution(mesh):
    fine = Mesh(mesh.devices.reshape(NY, NZ, NX, NC), AXES)
    image = ("y", "z", "x", "core")
    text = ("z", "x", "core", "y")
    return jax.shard_map(
        shards,
        mesh=fine,
        in_specs=(P(image, None), P(image), P(text, None), P(text), P("y"), P(), P()),
        out_specs=(P(image, None), P(text, None)),
        check_vma=False,
    )
```

time: 105 us -> 102 us (0.971)
  blocking collectives: 0 us -> 13.3 us
  waiting for transfers between devices: 34.1 us -> 25.6 us
  starting transfers between devices: 55.6 us -> 48.4 us
  other arithmetic: 7.74 us -> 2.79 us
  Pallas kernels: 0 us -> 3.26 us
  matrix products: 2.52 us -> 3.69 us
    all_gather x0 -> x1, blocking collectives: none -> 13.3 us  [shards(): lax.all_gather(exchange(text_send, 'y').reshape(half_rows, d), 'x', axis=...]
    ppermute x8 -> x5, starting transfers between devices: 20.5 us -> 13.2 us  [shift(): return lax.ppermute(block, axis, [(i, (i + k) % n) for i in range(n)])]
    ppermute x8 -> x5, waiting for transfers between devices: 8.8 us -> 1.5 us  [shift(): return lax.ppermute(block, axis, [(i, (i + k) % n) for i in range(n)])]
    pallas_call x0 -> x2, Pallas kernels: none -> 3.26 us  [prologue(): pl.pallas_call(prologue_kernel, out_shape=(jax.ShapeDtypeStruct((copies,)...]
    reduce_sum x4 -> x2, other arithmetic: 1.94 us -> 0.07 us  [the longest x1 0.04 us: shards(): unit_grad_image = image_parts.astype(f32).sum(axis=0)]
    convert_element_type x2 -> x0, other arithmetic: 1.63 us -> none  [unit_rows(): return (norm, unit, unit.astype(bf16))]
    broadcast_in_dim x2 -> x0, local copies, waits for them, and re-layouts: 1.41 us -> none  [spread(): return exchange(jnp.broadcast_to(block[None], (n,) + block.shape), axis)]
    exp2 x2 -> x0, other arithmetic: 1.33 us -> none  [unit_rows(): scaled = mantissa.astype(f32) * jnp.exp2(exponent.astype(f32))[:, None]]
  transfers between devices with their start and end apart: 12 -> 9, of which waited for: 6 -> 5; matrix products, arithmetic and copies ran while one was open for 5% -> 4% of each run, Pallas kernels for 0% -> 2%
where the time goes in v3:
time: 102 us; the launch traced here: 100 us
  starting transfers between devices  48.4 us (47%)
  waiting for transfers between devices  25.6 us (25%)
  blocking collectives  13.3 us (13%)
  matrix products  3.69 us (4%)
  Pallas kernels  3.26 us (3%)
  other arithmetic  2.79 us (3%)
  between operations  2.19 us (2%)
    all_to_all x4, starting transfers between devices, exchange(): return lax.all_to_all(blocks, axis, split_axis=0, concat_axis=0, tiled=True)  35.3 us
    all_to_all x4, waiting for transfers between devices, exchange(): return lax.all_to_all(blocks, axis, split_axis=0, concat_axis=0, tiled=True)  24.1 us
    all_gather x1, blocking collectives, shards(): lax.all_gather(exchange(text_send, 'y').reshape(half_rows, d), 'x', axis=...  13.3 us
    ppermute x5, starting transfers between devices, shift(): return lax.ppermute(block, axis, [(i, (i + k) % n) for i in range(n)])  13.2 us
    dot_general x6, matrix products, product(): return jnp.dot(a, b, preferred_element_type=f32)  3.69 us
    pallas_call x2, Pallas kernels, prologue(): pl.pallas_call(prologue_kernel, out_shape=(jax.ShapeDtypeStruct((copies,)...  3.26 us
  transfers between devices with their start and end apart: 9, of which 5 were waited for; matrix products, arithmetic and copies ran while one was open for 4% of the time, Pallas kernels for 2%

profile of v3, /device:TPU:6, one launch (start us, length us, event | category | flops | bytes accessed | tf_op | source)
XLA Modules:
  0.0 100.2 jit_solution(4108903761242302360)
XLA Ops:
  0.6 1.6 %shard_map.87 = (bf16[8,8,1536]{2,1,0:T(8,128)(2,1)}, f32[8,1536]{1,0:T(8,128)}, f32[8,1]{1,0:T(8,128)}) custom-call(bf16[8,1536]{1,0:T(8,128)(2,1)} %mantissa_ref.2, s32[8]{0:T(128)} %exponent_ref.3), custom_call_target="tpu_custom_call" | custom-call | tf_op jit(solution)/shard_map/pallas_call | solution.py:32
  2.2 7.1 %all-to-all-start.1 = ((bf16[8,8,1536]{2,1,0:T(8,128)(2,1)}), bf16[8,8,1536]{2,1,0:T(8,128)(2,1)S(1)}, u32[]{:S(2)}, u32[]{:S(2)}) async-start(bf16[8,8,1536]{2,1,0:T(8,128)(2,1)} %get-tuple-element.15), calls=%async_computation.1 | async-start | bytes 393216 | tf_op jit(solution)/shard_map/all_to_all | solution.py:48
  9.3 0.8 reshape.93
  10.2 0.1 sub.30
  10.3 1.6 %shard_map.86 = (bf16[12,8,1536]{2,1,0:T(8,128)(2,1)}, f32[8,1536]{1,0:T(8,128)}, f32[8,1]{1,0:T(8,128)}) custom-call(bf16[8,1536]{1,0:T(8,128)(2,1)} %mantissa_ref.1, s32[8]{0:T(128)} %exponent_ref.2), custom_call_target="tpu_custom_call" | custom-call | tf_op jit(solution)/shard_map/pallas_call | solution.py:32
  11.9 7.9 %all-to-all-done.1 = bf16[8,8,1536]{2,1,0:T(8,128)(2,1)S(1)} async-done(((bf16[8,8,1536]{2,1,0:T(8,128)(2,1)}), bf16[8,8,1536]{2,1,0:T(8,128)(2,1)S(1)}, u32[]{:S(2)}, u32[]{:S(2)}) %all-to-all-start.1) | async-done | bytes 196640 | tf_op jit(solution)/shard_map/all_to_all | solution.py:48
  19.8 15.2 %all-to-all-start = ((bf16[12,8,1536]{2,1,0:T(8,128)(2,1)}), bf16[12,8,1536]{2,1,0:T(8,128)(2,1)S(1)}, u32[]{:S(2)}, u32[]{:S(2)}) async-start(bf16[12,8,1536]{2,1,0:T(8,128)(2,1)} %get-tuple-element.14), calls=%async_computation | async-start | bytes 589824 | tf_op jit(solution)/shard_map/all_to_all | solution.py:48
  35.0 13.3 %all_gather.3 = bf16[256,1536]{1,0:T(8,128)(2,1)S(1)} all-gather(bf16[64,1536]{1,0:T(8,128)(2,1)S(1)} %bitcast.43), channel_id=1, replica_groups=mesh['y'=8,'z'=12,'x'=4,'core'=2] {'x'}, dimensions={0}, use_global_device_ids=true | all-gather | bytes 983040 | tf_op jit(solution)/shard_map/all_gather | solution.py:81
  48.3 1.9 %collective-permute-start = (bf16[256,1536]{1,0:T(8,128)(2,1)S(1)}, bf16[256,1536]{1,0:T(8,128)(2,1)S(1)}, u32[]{:S(2)}, u32[]{:S(2)}) collective-permute-start(bf16[256,1536]{1,0:T(8,128)(2,1)S(1)} %all_gather.3), channel_id=1, source_target_pairs={{0,1},{1,0},{2,3},{3,2},{4,5},{5,4},{6,7},{7,6},{8,9},{9,8},{10,11... | collective-permute-start | bytes 2359304 | tf_op jit(solution)/shard_map/ppermute | solution.py:52
  51.5 0.0 all-to-all-done
  51.5 0.9 collective-permute-done
  52.5 0.4 fusion.18
  52.9 1.3 %fusion = bf16[256,1536]{1,0:T(8,128)(2,1)} fusion(bf16[96,256]{1,0:T(8,128)(2,1)S(1)} %fusion.18, f32[]{:T(128)} %bitcast.37, bf16[12,8,1536]{2,1,0:T(8,128)(2,1)S(1)} %all-to-all-done), kind=kOutput, calls=%fused_computation.2 | convolution fusion | flops 76283904 | bytes 1130500 | tf_op jit(solution)/shard_map/dot_general | solution.py:56
  54.1 2.0 %collective-permute-start.1 = (bf16[256,1536]{1,0:T(8,128)(2,1)}, bf16[256,1536]{1,0:T(8,128)(2,1)S(1)}, u32[]{:S(2)}, u32[]{:S(2)}) collective-permute-start(bf16[256,1536]{1,0:T(8,128)(2,1)} %fusion), channel_id=1, source_target_pairs={{0,1},{1,0},{2,3},{3,2},{4,5},{5,4},{6,7},{7,6},{8,9},{9,8},{10,11... | collective-permute-start | bytes 2359304 | tf_op jit(solution)/shard_map/ppermute | solution.py:52
  56.2 0.4 fusion.19
  56.6 0.3 fusion.31
  56.8 1.0 fusion.3
  57.8 9.6 %all-to-all-start.2 = ((bf16[12,8,1536]{2,1,0:T(8,128)(2,1)}), bf16[12,8,1536]{2,1,0:T(8,128)(2,1)S(1)}, u32[]{:S(2)}, u32[]{:S(2)}) async-start(bf16[12,8,1536]{2,1,0:T(8,128)(2,1)} %fusion.3), calls=%async_computation.2 | async-start | bytes 589824 | tf_op jit(solution)/shard_map/all_to_all | solution.py:48
  67.5 0.0 collective-permute-done.1
  67.5 0.4 add_convert_fusion
  67.9 0.0 copy-start.2
  67.9 0.0 copy-start.3
  67.9 0.1 dynamic-slice_bitcast_fusion.2
  68.0 3.5 %collective-permute-start.2 = (bf16[64,1536]{1,0:T(8,128)(2,1)S(1)}, bf16[64,1536]{1,0:T(8,128)(2,1)S(1)}, u32[]{:S(2)}, u32[]{:S(2)}) collective-permute-start(bf16[64,1536]{1,0:T(8,128)(2,1)S(1)} %get-tuple-element.22), channel_id=1, source_target_pairs={{0,2},{2,4},{4,6},{6,0},{1,3},{3,5},{5,7},{7,1},{8,10},{10,12},{12... | collective-permute-start | bytes 589832 | tf_op jit(solution)/shard_map/ppermute | solution.py:52
  71.5 2.3 %collective-permute-start.4 = (bf16[64,1536]{1,0:T(8,128)(2,1)S(1)}, bf16[64,1536]{1,0:T(8,128)(2,1)S(1)}, u32[]{:S(2)}, u32[]{:S(2)}) collective-permute-start(bf16[64,1536]{1,0:T(8,128)(2,1)S(1)} %get-tuple-element.23), channel_id=1, source_target_pairs={{0,6},{2,0},{4,2},{6,4},{1,7},{3,1},{5,3},{7,5},{8,14},{10,8},{12,... | collective-permute-start | bytes 589832 | tf_op jit(solution)/shard_map/ppermute | solution.py:52
  73.8 3.4 %collective-permute-start.3 = (bf16[64,1536]{1,0:T(8,128)(2,1)S(1)}, bf16[64,1536]{1,0:T(8,128)(2,1)S(1)}, u32[]{:S(2)}, u32[]{:S(2)}) collective-permute-start(bf16[64,1536]{1,0:T(8,128)(2,1)S(1)} %get-tuple-element.24), channel_id=1, source_target_pairs={{0,4},{2,6},{4,0},{6,2},{1,5},{3,7},{5,1},{7,3},{8,12},{10,14},{12... | collective-permute-start | bytes 589832 | tf_op jit(solution)/shard_map/ppermute | solution.py:52
  77.2 0.0 copy-done.2
  77.2 0.1 reduce.2
  77.3 0.0 copy-done.3
  77.3 0.1 reduce.1
  77.4 0.0 copy-start.1
  77.5 7.3 %all-to-all-done.2 = bf16[12,8,1536]{2,1,0:T(8,128)(2,1)S(1)} async-done(((bf16[12,8,1536]{2,1,0:T(8,128)(2,1)}), bf16[12,8,1536]{2,1,0:T(8,128)(2,1)S(1)}, u32[]{:S(2)}, u32[]{:S(2)}) %all-to-all-start.2) | async-done | bytes 294944 | tf_op jit(solution)/shard_map/all_to_all | solution.py:48
  84.8 0.0 copy-start
  84.8 0.0 collective-permute-done.2
  84.8 0.6 collective-permute-done.4
  85.4 0.0 collective-permute-done.3
  85.4 0.8 fusion.27
  86.2 3.4 %all-to-all-start.3 = ((bf16[8,8,1536]{2,1,0:T(8,128)(2,1)}), bf16[8,8,1536]{2,1,0:T(8,128)(2,1)S(1)}, u32[]{:S(2)}, u32[]{:S(2)}) async-start(bf16[8,8,1536]{2,1,0:T(8,128)(2,1)} %fusion.27), calls=%async_computation.3 | async-start | bytes 393216 | tf_op jit(solution)/shard_map/all_to_all | solution.py:48
  89.6 0.0 copy-done.1
  89.6 0.1 multiply_reduce_fusion.1
  89.7 0.7 subtract_divide_fusion.1
  90.4 8.9 %all-to-all-done.3 = bf16[8,8,1536]{2,1,0:T(8,128)(2,1)S(1)} async-done(((bf16[8,8,1536]{2,1,0:T(8,128)(2,1)}), bf16[8,8,1536]{2,1,0:T(8,128)(2,1)S(1)}, u32[]{:S(2)}, u32[]{:S(2)}) %all-to-all-start.3) | async-done | bytes 196640 | tf_op jit(solution)/shard_map/all_to_all | solution.py:48
  99.4 0.0 copy-done
  99.4 0.1 multiply_reduce_fusion
  99.5 0.7 subtract_divide_fusion
  (6 shorter events, 0.1 us)
Async XLA Ops:
  2.2 17.6 %all-to-all-start.1 = ((bf16[8,8,1536]{2,1,0:T(8,128)(2,1)}), bf16[8,8,1536]{2,1,0:T(8,128)(2,1)S(1)}, u32[]{:S(2)}, u32[]{:S(2)}) async-start(bf16[8,8,1536]{2,1,0:T(8,128)(2,1)} %get-tuple-element.15), calls=%async_computation.1 | async-start | bytes 393216 | tf_op jit(solution)/shard_map/all_to_all | solution.py:48
  19.8 31.7 %all-to-all-start = ((bf16[12,8,1536]{2,1,0:T(8,128)(2,1)}), bf16[12,8,1536]{2,1,0:T(8,128)(2,1)S(1)}, u32[]{:S(2)}, u32[]{:S(2)}) async-start(bf16[12,8,1536]{2,1,0:T(8,128)(2,1)} %get-tuple-element.14), calls=%async_computation | async-start | bytes 589824 | tf_op jit(solution)/shard_map/all_to_all | solution.py:48
  48.3 4.2 %collective-permute-start = (bf16[256,1536]{1,0:T(8,128)(2,1)S(1)}, bf16[256,1536]{1,0:T(8,128)(2,1)S(1)}, u32[]{:S(2)}, u32[]{:S(2)}) collective-permute-start(bf16[256,1536]{1,0:T(8,128)(2,1)S(1)} %all_gather.3), channel_id=1, source_target_pairs={{0,1},{1,0},{2,3},{3,2},{4,5},{5,4},{6,7},{7,6},{8,9},{9,8},{10,11... | collective-permute-start | bytes 2359304 | tf_op jit(solution)/shard_map/ppermute | solution.py:52
  54.1 13.3 %collective-permute-start.1 = (bf16[256,1536]{1,0:T(8,128)(2,1)}, bf16[256,1536]{1,0:T(8,128)(2,1)S(1)}, u32[]{:S(2)}, u32[]{:S(2)}) collective-permute-start(bf16[256,1536]{1,0:T(8,128)(2,1)} %fusion), channel_id=1, source_target_pairs={{0,1},{1,0},{2,3},{3,2},{4,5},{5,4},{6,7},{7,6},{8,9},{9,8},{10,11... | collective-permute-start | bytes 2359304 | tf_op jit(solution)/shard_map/ppermute | solution.py:52
  57.8 26.9 %all-to-all-start.2 = ((bf16[12,8,1536]{2,1,0:T(8,128)(2,1)}), bf16[12,8,1536]{2,1,0:T(8,128)(2,1)S(1)}, u32[]{:S(2)}, u32[]{:S(2)}) async-start(bf16[12,8,1536]{2,1,0:T(8,128)(2,1)} %fusion.3), calls=%async_computation.2 | async-start | bytes 589824 | tf_op jit(solution)/shard_map/all_to_all | solution.py:48
  67.9 9.3 %copy-start.2 = (f32[8,1]{1,0:T(8,128)S(1)}, f32[8,1]{1,0:T(8,128)}, u32[]{:S(2)}) copy-start(f32[8,1]{1,0:T(8,128)} %get-tuple-element.21) | copy-start | bytes 100
  67.9 9.4 %copy-start.3 = (f32[8,1]{1,0:T(8,128)S(1)}, f32[8,1]{1,0:T(8,128)}, u32[]{:S(2)}) copy-start(f32[8,1]{1,0:T(8,128)} %get-tuple-element.18) | copy-start | bytes 100
  68.0 16.8 %collective-permute-start.2 = (bf16[64,1536]{1,0:T(8,128)(2,1)S(1)}, bf16[64,1536]{1,0:T(8,128)(2,1)S(1)}, u32[]{:S(2)}, u32[]{:S(2)}) collective-permute-start(bf16[64,1536]{1,0:T(8,128)(2,1)S(1)} %get-tuple-element.22), channel_id=1, source_target_pairs={{0,2},{2,4},{4,6},{6,0},{1,3},{3,5},{5,7},{7,1},{8,10},{10,12},{12... | collective-permute-start | bytes 589832 | tf_op jit(solution)/shard_map/ppermute | solution.py:52
  71.5 13.9 %collective-permute-start.4 = (bf16[64,1536]{1,0:T(8,128)(2,1)S(1)}, bf16[64,1536]{1,0:T(8,128)(2,1)S(1)}, u32[]{:S(2)}, u32[]{:S(2)}) collective-permute-start(bf16[64,1536]{1,0:T(8,128)(2,1)S(1)} %get-tuple-element.23), channel_id=1, source_target_pairs={{0,6},{2,0},{4,2},{6,4},{1,7},{3,1},{5,3},{7,5},{8,14},{10,8},{12,... | collective-permute-start | bytes 589832 | tf_op jit(solution)/shard_map/ppermute | solution.py:52
  73.8 11.6 %collective-permute-start.3 = (bf16[64,1536]{1,0:T(8,128)(2,1)S(1)}, bf16[64,1536]{1,0:T(8,128)(2,1)S(1)}, u32[]{:S(2)}, u32[]{:S(2)}) collective-permute-start(bf16[64,1536]{1,0:T(8,128)(2,1)S(1)} %get-tuple-element.24), channel_id=1, source_target_pairs={{0,4},{2,6},{4,0},{6,2},{1,5},{3,7},{5,1},{7,3},{8,12},{10,14},{12... | collective-permute-start | bytes 589832 | tf_op jit(solution)/shard_map/ppermute | solution.py:52
  77.4 12.1 %copy-start.1 = (f32[8,1536]{1,0:T(8,128)S(1)}, f32[8,1536]{1,0:T(8,128)}, u32[]{:S(2)}) copy-start(f32[8,1536]{1,0:T(8,128)} %get-tuple-element.17) | copy-start | bytes 147460
  84.8 14.6 %copy-start = (f32[8,1536]{1,0:T(8,128)S(1)}, f32[8,1536]{1,0:T(8,128)}, u32[]{:S(2)}) copy-start(f32[8,1536]{1,0:T(8,128)} %get-tuple-element.20) | copy-start | bytes 147460
  86.2 13.2 %all-to-all-start.3 = ((bf16[8,8,1536]{2,1,0:T(8,128)(2,1)}), bf16[8,8,1536]{2,1,0:T(8,128)(2,1)S(1)}, u32[]{:S(2)}, u32[]{:S(2)}) async-start(bf16[8,8,1536]{2,1,0:T(8,128)(2,1)} %fusion.27), calls=%async_computation.3 | async-start | bytes 393216 | tf_op jit(solution)/shard_map/all_to_all | solution.py:48

commit v4 on v3

v4 whole, which is shorter than its diff:
```python
import jax
import jax.numpy as jnp
from jax import lax
from jax.experimental import pallas as pl
from jax.experimental.pallas import tpu as pltpu
from jax.sharding import Mesh, PartitionSpec as P

epsilon = 1e-06
AXES = ("y", "z", "x", "core")
NY, NZ, NX, NC = 8, 12, 4, 2
R = 8
f32 = jnp.float32
bf16 = jnp.bfloat16


def unit_rows(mantissa_ref, exponent_ref):
    row = lax.broadcasted_iota(jnp.int32, (R, 1), 0)
    exponent = jnp.zeros((R, 1), jnp.int32)
    for r in range(R):
        exponent = jnp.where(row == r, exponent_ref[r], exponent)
    scaled = mantissa_ref[...].astype(f32) * jnp.exp2(exponent.astype(f32))
    norm = jnp.sqrt(jnp.sum(scaled * scaled, axis=1, keepdims=True) + epsilon)
    return norm, scaled / norm


def text_kernel(mantissa_ref, exponent_ref, send_ref):
    _, unit = unit_rows(mantissa_ref, exponent_ref)
    half = unit.astype(bf16)
    for k in range(NY):
        send_ref[k] = half


def image_kernel(
    image_ref, image_exponent_ref, text_ref, text_exponent_ref, scale_ref, bias_ref,
    send_ref, image_unit_ref, image_gain_ref, text_unit_ref, text_gain_ref, scale_row_ref, bias_row_ref,
):
    norm, unit = unit_rows(image_ref, image_exponent_ref)
    half = unit.astype(bf16)
    for k in range(NZ):
        send_ref[k] = half
    factor = scale_ref[0]
    image_unit_ref[...] = unit
    image_gain_ref[...] = jnp.broadcast_to(factor / norm, unit.shape)
    norm, unit = unit_rows(text_ref, text_exponent_ref)
    text_unit_ref[...] = unit
    text_gain_ref[...] = jnp.broadcast_to(factor / norm, unit.shape)
    scale_row_ref[...] = jnp.full(scale_row_ref.shape, factor, f32)
    bias_row_ref[...] = jnp.full(bias_row_ref.shape, bias_ref[0], f32)


vmem = pl.BlockSpec(memory_space=pltpu.VMEM)
smem = pl.BlockSpec(memory_space=pltpu.SMEM)


def text_prologue(mantissa, exponent):
    return pl.pallas_call(
        text_kernel,
        out_shape=jax.ShapeDtypeStruct((NY,) + mantissa.shape, bf16),
        in_specs=[vmem, smem],
        out_specs=vmem,
    )(mantissa, exponent)


def image_prologue(image, image_exponent, text, text_exponent, scale, bias):
    d = image.shape[1]
    rows = jax.ShapeDtypeStruct((R, d), f32)
    row = jax.ShapeDtypeStruct((1, NX * NY * R), f32)
    return pl.pallas_call(
        image_kernel,
        out_shape=(
            jax.ShapeDtypeStruct((NZ, R, d), bf16), rows, rows, rows, rows, row, row,
        ),
        in_specs=[vmem, smem, vmem, smem, smem, smem],
        out_specs=(vmem,) * 7,
    )(image, image_exponent, text, text_exponent, scale, bias)


def exchange(blocks, axis):
    return lax.all_to_all(blocks, axis, split_axis=0, concat_axis=0, tiled=True)


def shift(block, axis, n, k):
    return lax.ppermute(block, axis, [(i, (i + k) % n) for i in range(n)])


def rows_at(array, start, size):
    starts = (start,) + (jnp.int32(0),) * (array.ndim - 1)
    return lax.dynamic_slice(array, starts, (size,) + array.shape[1:], allow_negative_indices=False)


def product(a, b):
    return jnp.dot(a, b, preferred_element_type=f32)


def tangent(unit_grad, unit, gain):
    return (unit_grad - unit * jnp.sum(unit * unit_grad, axis=1, keepdims=True)) * gain


def shards(
    image_mantissa, image_exponent, text_mantissa, text_exponent, positive, logit_scale, logit_bias
):
    d = image_mantissa.shape[1]
    z, x, c = lax.axis_index("z"), lax.axis_index("x"), lax.axis_index("core")
    half_rows = NY * R
    near_rows = NX * half_rows
    own = NZ * R

    place = positive.reshape(NZ, NX, NC, R).transpose(1, 2, 0, 3).reshape(NX, NC * own)
    place = rows_at(place, x, 1).reshape(NC * own)
    place = place - (z * (NC * near_rows) + c * half_rows)
    place = jnp.where((place >= 0) & (place < NC * near_rows), place, -1)

    text_send = text_prologue(text_mantissa, text_exponent)
    image_mantissa, place = lax.optimization_barrier((image_mantissa, place))
    image_send, image_unit, image_gain, text_unit, text_gain, scale, bias = image_prologue(
        image_mantissa, image_exponent, text_mantissa, text_exponent, logit_scale, logit_bias
    )
    texts = lax.all_gather(exchange(text_send, "y").reshape(half_rows, d), "x", axis=0, tiled=True)
    images = lax.all_gather(exchange(image_send, "z").reshape(own, d), "core", axis=0, tiled=True)

    column = jnp.arange(near_rows, dtype=jnp.int32)[None, :]
    target = (column // half_rows) * (NC * half_rows) + column % half_rows
    logits = scale * product(images, texts.T) + bias
    label_sign = jnp.where(place[:, None] == target, 1.0, -1.0).astype(f32)
    weights = (-label_sign * jax.nn.sigmoid(-label_sign * logits)).astype(bf16)

    far = rows_at(weights, (1 - c) * own, own)
    near = rows_at(weights, c * own, own)
    far = product(far, texts).astype(bf16)
    far, weights = lax.optimization_barrier((far, weights))
    far = shift(far, "core", NC, 1)

    part = product(weights.T, images).astype(bf16).reshape(NX, half_rows, d)
    blocks = [rows_at(part, (x + k) & (NX - 1), 1).reshape(half_rows, d) for k in range(NX)]
    opposite = shift(blocks[2], "x", NX, 2)

    near = lax.optimization_barrier(product(near, texts))
    image_part = (near + far.astype(f32)).astype(bf16)
    image_part, blocks[1], blocks[3] = lax.optimization_barrier((image_part, blocks[1], blocks[3]))
    image_parts = exchange(image_part.reshape(NZ, R, d), "z")
    unit_grad_image = image_parts.astype(f32).sum(axis=0)

    total = blocks[0].astype(f32) + opposite.astype(f32)
    total = total + shift(blocks[1], "x", NX, 1).astype(f32) + shift(blocks[3], "x", NX, 3).astype(f32)
    total = total.astype(bf16).reshape(NY, R, d)
    total, unit_grad_image = lax.optimization_barrier((total, unit_grad_image))
    unit_grad_text = exchange(total, "y").astype(f32).sum(axis=0)

    return (
        tangent(unit_grad_image, image_unit, image_gain),
        tangent(unit_grad_text, text_unit, text_gain),
    )


def solution(mesh):
    fine = Mesh(mesh.devices.reshape(NY, NZ, NX, NC), AXES)
    image = ("y", "z", "x", "core")
    text = ("z", "x", "core", "y")
    return jax.shard_map(
        shards,
        mesh=fine,
        in_specs=(P(image, None), P(image), P(text, None), P(text), P("y"), P(), P()),
        out_specs=(P(image, None), P(text, None)),
        check_vma=False,
    )
```

time: 102 us -> 98.7 us (0.968)
  the two profiles are of different devices: /device:TPU:6 before, /device:TPU:64 now
where the time goes in v4:
time: 98.7 us; the launch traced here: 97.9 us
  starting transfers between devices  45.8 us (46%)
  waiting for transfers between devices  24.1 us (24%)
  blocking collectives  16.9 us (17%)
  Pallas kernels  3.31 us (3%)
  other arithmetic  3.3 us (3%)
  between operations  2.1 us (2%)
  matrix products  1.35 us (1%)
  local copies, waits for them, and re-layouts  0.99 us (1%)
    all_to_all x4, starting transfers between devices, exchange(): return lax.all_to_all(blocks, axis, split_axis=0, concat_axis=0, tiled=True)  34.6 us
    all_to_all x4, waiting for transfers between devices, exchange(): return lax.all_to_all(blocks, axis, split_axis=0, concat_axis=0, tiled=True)  16.7 us
    all_gather x1, blocking collectives, shards(): lax.all_gather(exchange(text_send, 'y').reshape(half_rows, d), 'x', axis=...  14.7 us
    ppermute x4, starting transfers between devices, shift(): return lax.ppermute(block, axis, [(i, (i + k) % n) for i in range(n)])  11.2 us
    ppermute x4, waiting for transfers between devices, shift(): return lax.ppermute(block, axis, [(i, (i + k) % n) for i in range(n)])  7.33 us
    all_gather x1, blocking collectives, shards(): lax.all_gather(exchange(image_send, 'z').reshape(own, d), 'core', axis=0,...  2.22 us
  transfers between devices with their start and end apart: 8, of which 7 were waited for; matrix products, arithmetic and copies ran while one was open for 3% of the time, Pallas kernels for 2%

profile of v4, /device:TPU:64, one launch (start us, length us, event | category | flops | bytes accessed | tf_op | source)
XLA Modules:
  0.0 97.9 jit_solution(2041648316594279224)
XLA Ops:
  0.6 1.6 %shard_map.87 = bf16[8,8,1536]{2,1,0:T(8,128)(2,1)} custom-call(bf16[8,1536]{1,0:T(8,128)(2,1)} %mantissa_ref.1, s32[8]{0:T(128)} %exponent_ref.1), custom_call_target="tpu_custom_call" | custom-call | tf_op jit(solution)/shard_map/pallas_call | solution.py:56
  2.2 7.1 %all-to-all-start.1 = ((bf16[8,8,1536]{2,1,0:T(8,128)(2,1)}), bf16[8,8,1536]{2,1,0:T(8,128)(2,1)S(1)}, u32[]{:S(2)}, u32[]{:S(2)}) async-start(bf16[8,8,1536]{2,1,0:T(8,128)(2,1)} %shard_map.87), calls=%async_computation.1 | async-start | bytes 393216 | tf_op jit(solution)/shard_map/all_to_all | solution.py:79
  9.3 0.8 reshape.98
  10.2 0.1 reshape.99
  11.6 1.7 %shard_map.86 = (bf16[12,8,1536]{2,1,0:T(8,128)(2,1)}, f32[8,1536]{1,0:T(8,128)}, f32[8,1536]{1,0:T(8,128)}, f32[8,1536]{1,0:T(8,128)}, f32[8,1536]{1,0:T(8,128)}, /*index=5*/f32[1,256]{1,0:T(1,128)}, f32[1,256]{1,0:T(1,128)}) custom-call(bf16[8,1536]{1,0:T(8,128)(2,1)} %image_ref, s32[8]{0:T(128)} %image_exponent_ref.1, bf16[8,1536]{1,0:T(8,128)(2,1)} %mantissa_ref.1, ...), custom_call_target="tpu_custom_call" | custom-call | tf_op jit(solution)/shard_map/pallas_call | solution.py:68
  13.3 6.5 %all-to-all-done.1 = bf16[8,8,1536]{2,1,0:T(8,128)(2,1)S(1)} async-done(((bf16[8,8,1536]{2,1,0:T(8,128)(2,1)}), bf16[8,8,1536]{2,1,0:T(8,128)(2,1)S(1)}, u32[]{:S(2)}, u32[]{:S(2)}) %all-to-all-start.1) | async-done | bytes 196640 | tf_op jit(solution)/shard_map/all_to_all | solution.py:79
  19.8 14.8 %all-to-all-start = ((bf16[12,8,1536]{2,1,0:T(8,128)(2,1)}), bf16[12,8,1536]{2,1,0:T(8,128)(2,1)S(1)}, u32[]{:S(2)}, u32[]{:S(2)}) async-start(bf16[12,8,1536]{2,1,0:T(8,128)(2,1)} %get-tuple-element.21), calls=%async_computation | async-start | bytes 589824 | tf_op jit(solution)/shard_map/all_to_all | solution.py:79
  34.6 0.0 copy-start.4
  34.6 0.0 copy-start.5
  34.6 14.7 %all_gather.7 = bf16[256,1536]{1,0:T(8,128)(2,1)S(1)} all-gather(bf16[64,1536]{1,0:T(8,128)(2,1)S(1)} %bitcast.28), channel_id=1, replica_groups=mesh['y'=8,'z'=12,'x'=4,'core'=2] {'x'}, dimensions={0}, use_global_device_ids=true | all-gather | bytes 983040 | tf_op jit(solution)/shard_map/all_gather | solution.py:118
  49.3 0.0 all-to-all-done
  49.3 2.2 %all_gather.6 = bf16[192,1536]{1,0:T(8,128)(2,1)S(1)} all-gather(bf16[96,1536]{1,0:T(8,128)(2,1)S(1)} %bitcast.27), channel_id=1, replica_groups=mesh['y'=8,'z'=12,'x'=4,'core'=2] {'core'}, dimensions={0}, use_global_device_ids=true | all-gather | bytes 884736 | tf_op jit(solution)/shard_map/all_gather | solution.py:119
  51.6 0.0 copy-done.4
  51.6 0.0 copy-done.5
  51.6 0.4 fusion.7
  52.0 0.3 convolution_convert_fusion.1
  52.3 2.0 %collective-permute-start.1 = (bf16[96,1536]{1,0:T(8,128)(2,1)S(1)}, bf16[96,1536]{1,0:T(8,128)(2,1)S(1)}, u32[]{:S(2)}, u32[]{:S(2)}) collective-permute-start(bf16[96,1536]{1,0:T(8,128)(2,1)S(1)} %convolution_convert_fusion.1), channel_id=1, source_target_pairs={{0,1},{1,0},{2,3},{3,2},{4,5},{5,4},{6,7},{7,6},{8,9},{9,8},{10,11... | collective-permute-start | bytes 884744 | tf_op jit(solution)/shard_map/ppermute | solution.py:83
  54.3 0.4 convolution_convert_fusion
  54.7 0.3 fusion.12
  55.0 0.1 dynamic-slice_bitcast_fusion.2
  55.0 0.7 collective-permute-done.1
  55.8 0.8 add_convert_fusion
  56.5 9.3 %all-to-all-start.2 = ((bf16[12,8,1536]{2,1,0:T(8,128)(2,1)}), bf16[12,8,1536]{2,1,0:T(8,128)(2,1)S(1)}, u32[]{:S(2)}, u32[]{:S(2)}) async-start(bf16[12,8,1536]{2,1,0:T(8,128)(2,1)} %bitcast.12), calls=%async_computation.2 | async-start | bytes 589824 | tf_op jit(solution)/shard_map/all_to_all | solution.py:79
  65.9 3.4 %collective-permute-start = (bf16[64,1536]{1,0:T(8,128)(2,1)S(1)}, bf16[64,1536]{1,0:T(8,128)(2,1)S(1)}, u32[]{:S(2)}, u32[]{:S(2)}) collective-permute-start(bf16[64,1536]{1,0:T(8,128)(2,1)S(1)} %get-tuple-element.34), channel_id=1, source_target_pairs={{0,4},{2,6},{4,0},{6,2},{1,5},{3,7},{5,1},{7,3},{8,12},{10,14},{12... | collective-permute-start | bytes 589832 | tf_op jit(solution)/shard_map/ppermute | solution.py:83
  69.2 3.6 %collective-permute-start.3 = (bf16[64,1536]{1,0:T(8,128)(2,1)S(1)}, bf16[64,1536]{1,0:T(8,128)(2,1)S(1)}, u32[]{:S(2)}, u32[]{:S(2)}) collective-permute-start(bf16[64,1536]{1,0:T(8,128)(2,1)S(1)} %get-tuple-element.26), channel_id=1, source_target_pairs={{0,6},{2,0},{4,2},{6,4},{1,7},{3,1},{5,3},{7,5},{8,14},{10,8},{12,... | collective-permute-start | bytes 589832 | tf_op jit(solution)/shard_map/ppermute | solution.py:83
  72.8 2.3 %collective-permute-start.2 = (bf16[64,1536]{1,0:T(8,128)(2,1)S(1)}, bf16[64,1536]{1,0:T(8,128)(2,1)S(1)}, u32[]{:S(2)}, u32[]{:S(2)}) collective-permute-start(bf16[64,1536]{1,0:T(8,128)(2,1)S(1)} %get-tuple-element.25), channel_id=1, source_target_pairs={{0,2},{2,4},{4,6},{6,0},{1,3},{3,5},{5,7},{7,1},{8,10},{10,12},{12... | collective-permute-start | bytes 589832 | tf_op jit(solution)/shard_map/ppermute | solution.py:83
  75.1 0.0 copy-start.1
  75.1 0.0 copy-start.3
  75.1 0.5 collective-permute-done
  75.6 3.2 %collective-permute-done.3 = bf16[64,1536]{1,0:T(8,128)(2,1)S(1)} collective-permute-done((bf16[64,1536]{1,0:T(8,128)(2,1)S(1)}, bf16[64,1536]{1,0:T(8,128)(2,1)S(1)}, u32[]{:S(2)}, u32[]{:S(2)}) %collective-permute-start.3) | collective-permute-done | bytes 196640 | tf_op jit(solution)/shard_map/ppermute | solution.py:83
  78.8 2.9 %collective-permute-done.2 = bf16[64,1536]{1,0:T(8,128)(2,1)S(1)} collective-permute-done((bf16[64,1536]{1,0:T(8,128)(2,1)S(1)}, bf16[64,1536]{1,0:T(8,128)(2,1)S(1)}, u32[]{:S(2)}, u32[]{:S(2)}) %collective-permute-start.2) | collective-permute-done | bytes 196640 | tf_op jit(solution)/shard_map/ppermute | solution.py:83
  81.7 0.8 fusion.11
  82.5 0.0 copy-start
  82.5 0.0 copy-start.2
  82.5 0.3 all-to-all-done.2
  82.9 3.4 %all-to-all-start.3 = ((bf16[8,8,1536]{2,1,0:T(8,128)(2,1)}), bf16[8,8,1536]{2,1,0:T(8,128)(2,1)S(1)}, u32[]{:S(2)}, u32[]{:S(2)}) async-start(bf16[8,8,1536]{2,1,0:T(8,128)(2,1)} %fusion.11), calls=%async_computation.3 | async-start | bytes 393216 | tf_op jit(solution)/shard_map/all_to_all | solution.py:79
  86.3 0.0 copy-done.1
  86.3 0.1 multiply_reduce_fusion.1
  86.4 0.0 copy-done.3
  86.4 0.7 subtract_multiply_fusion.1
  87.1 9.9 %all-to-all-done.3 = bf16[8,8,1536]{2,1,0:T(8,128)(2,1)S(1)} async-done(((bf16[8,8,1536]{2,1,0:T(8,128)(2,1)}), bf16[8,8,1536]{2,1,0:T(8,128)(2,1)S(1)}, u32[]{:S(2)}, u32[]{:S(2)}) %all-to-all-start.3) | async-done | bytes 196640 | tf_op jit(solution)/shard_map/all_to_all | solution.py:79
  97.0 0.0 copy-done
  97.0 0.1 multiply_reduce_fusion
  97.2 0.0 copy-done.2
  97.2 0.7 subtract_multiply_fusion
  (6 shorter events, 0.1 us)
Async XLA Ops:
  2.2 17.6 %all-to-all-start.1 = ((bf16[8,8,1536]{2,1,0:T(8,128)(2,1)}), bf16[8,8,1536]{2,1,0:T(8,128)(2,1)S(1)}, u32[]{:S(2)}, u32[]{:S(2)}) async-start(bf16[8,8,1536]{2,1,0:T(8,128)(2,1)} %shard_map.87), calls=%async_computation.1 | async-start | bytes 393216 | tf_op jit(solution)/shard_map/all_to_all | solution.py:79
  19.8 29.5 %all-to-all-start = ((bf16[12,8,1536]{2,1,0:T(8,128)(2,1)}), bf16[12,8,1536]{2,1,0:T(8,128)(2,1)S(1)}, u32[]{:S(2)}, u32[]{:S(2)}) async-start(bf16[12,8,1536]{2,1,0:T(8,128)(2,1)} %get-tuple-element.21), calls=%async_computation | async-start | bytes 589824 | tf_op jit(solution)/shard_map/all_to_all | solution.py:79
  34.6 17.0 %copy-start.4 = (f32[1,256]{1,0:T(1,128)S(1)}, f32[1,256]{1,0:T(1,128)}, u32[]{:S(2)}) copy-start(f32[1,256]{1,0:T(1,128)} %get-tuple-element.20) | copy-start | bytes 3076
  34.6 16.9 %copy-start.5 = (f32[1,256]{1,0:T(1,128)S(1)}, f32[1,256]{1,0:T(1,128)}, u32[]{:S(2)}) copy-start(f32[1,256]{1,0:T(1,128)} %get-tuple-element.22) | copy-start | bytes 3076
  52.3 3.5 %collective-permute-start.1 = (bf16[96,1536]{1,0:T(8,128)(2,1)S(1)}, bf16[96,1536]{1,0:T(8,128)(2,1)S(1)}, u32[]{:S(2)}, u32[]{:S(2)}) collective-permute-start(bf16[96,1536]{1,0:T(8,128)(2,1)S(1)} %convolution_convert_fusion.1), channel_id=1, source_target_pairs={{0,1},{1,0},{2,3},{3,2},{4,5},{5,4},{6,7},{7,6},{8,9},{9,8},{10,11... | collective-permute-start | bytes 884744 | tf_op jit(solution)/shard_map/ppermute | solution.py:83
  56.5 26.3 %all-to-all-start.2 = ((bf16[12,8,1536]{2,1,0:T(8,128)(2,1)}), bf16[12,8,1536]{2,1,0:T(8,128)(2,1)S(1)}, u32[]{:S(2)}, u32[]{:S(2)}) async-start(bf16[12,8,1536]{2,1,0:T(8,128)(2,1)} %bitcast.12), calls=%async_computation.2 | async-start | bytes 589824 | tf_op jit(solution)/shard_map/all_to_all | solution.py:79
  65.9 9.8 %collective-permute-start = (bf16[64,1536]{1,0:T(8,128)(2,1)S(1)}, bf16[64,1536]{1,0:T(8,128)(2,1)S(1)}, u32[]{:S(2)}, u32[]{:S(2)}) collective-permute-start(bf16[64,1536]{1,0:T(8,128)(2,1)S(1)} %get-tuple-element.34), channel_id=1, source_target_pairs={{0,4},{2,6},{4,0},{6,2},{1,5},{3,7},{5,1},{7,3},{8,12},{10,14},{12... | collective-permute-start | bytes 589832 | tf_op jit(solution)/shard_map/ppermute | solution.py:83
  69.2 9.6 %collective-permute-start.3 = (bf16[64,1536]{1,0:T(8,128)(2,1)S(1)}, bf16[64,1536]{1,0:T(8,128)(2,1)S(1)}, u32[]{:S(2)}, u32[]{:S(2)}) collective-permute-start(bf16[64,1536]{1,0:T(8,128)(2,1)S(1)} %get-tuple-element.26), channel_id=1, source_target_pairs={{0,6},{2,0},{4,2},{6,4},{1,7},{3,1},{5,3},{7,5},{8,14},{10,8},{12,... | collective-permute-start | bytes 589832 | tf_op jit(solution)/shard_map/ppermute | solution.py:83
  72.8 8.9 %collective-permute-start.2 = (bf16[64,1536]{1,0:T(8,128)(2,1)S(1)}, bf16[64,1536]{1,0:T(8,128)(2,1)S(1)}, u32[]{:S(2)}, u32[]{:S(2)}) collective-permute-start(bf16[64,1536]{1,0:T(8,128)(2,1)S(1)} %get-tuple-element.25), channel_id=1, source_target_pairs={{0,2},{2,4},{4,6},{6,0},{1,3},{3,5},{5,7},{7,1},{8,10},{10,12},{12... | collective-permute-start | bytes 589832 | tf_op jit(solution)/shard_map/ppermute | solution.py:83
  75.1 11.2 %copy-start.1 = (f32[8,1536]{1,0:T(8,128)S(1)}, f32[8,1536]{1,0:T(8,128)}, u32[]{:S(2)}) copy-start(f32[8,1536]{1,0:T(8,128)} %get-tuple-element.29) | copy-start | bytes 147460
  75.1 11.3 %copy-start.3 = (f32[8,1536]{1,0:T(8,128)S(1)}, f32[8,1536]{1,0:T(8,128)}, u32[]{:S(2)}) copy-start(f32[8,1536]{1,0:T(8,128)} %get-tuple-element.30) | copy-start | bytes 147460
  82.5 14.5 %copy-start = (f32[8,1536]{1,0:T(8,128)S(1)}, f32[8,1536]{1,0:T(8,128)}, u32[]{:S(2)}) copy-start(f32[8,1536]{1,0:T(8,128)} %get-tuple-element.32) | copy-start | bytes 147460
  82.5 14.7 %copy-start.2 = (f32[8,1536]{1,0:T(8,128)S(1)}, f32[8,1536]{1,0:T(8,128)}, u32[]{:S(2)}) copy-start(f32[8,1536]{1,0:T(8,128)} %get-tuple-element.33) | copy-start | bytes 147460
  82.9 14.1 %all-to-all-start.3 = ((bf16[8,8,1536]{2,1,0:T(8,128)(2,1)}), bf16[8,8,1536]{2,1,0:T(8,128)(2,1)S(1)}, u32[]{:S(2)}, u32[]{:S(2)}) async-start(bf16[8,8,1536]{2,1,0:T(8,128)(2,1)} %fusion.11), calls=%async_computation.3 | async-start | bytes 393216 | tf_op jit(solution)/shard_map/all_to_all | solution.py:79

commit v5 on v4

--- a/solution.py
+++ b/solution.py
@@ -83,6 +83,11 @@
     return lax.ppermute(block, axis, [(i, (i + k) % n) for i in range(n)])
 
 
+def cross(block, k):
+    moves = [(x * NC + c, (x + (k if c == 0 else -k)) % NX * NC + c) for x in range(NX) for c in range(NC)]
+    return lax.ppermute(block, ("x", "core"), moves)
+
+
 def rows_at(array, start, size):
     starts = (start,) + (jnp.int32(0),) * (array.ndim - 1)
     return lax.dynamic_slice(array, starts, (size,) + array.shape[1:], allow_negative_indices=False)
@@ -131,25 +136,23 @@
     far = shift(far, "core", NC, 1)
 
     part = product(weights.T, images).astype(bf16).reshape(NX, half_rows, d)
-    blocks = [rows_at(part, (x + k) & (NX - 1), 1).reshape(half_rows, d) for k in range(NX)]
-    opposite = shift(blocks[2], "x", NX, 2)
-
+    ways = (0, 1 + 2 * c, 2, 3 - 2 * c)
+    blocks = [rows_at(part, (x + k) & (NX - 1), 1).reshape(half_rows, d) for k in ways]
     near = lax.optimization_barrier(product(near, texts))
     image_part = (near + far.astype(f32)).astype(bf16)
-    image_part, blocks[1], blocks[3] = lax.optimization_barrier((image_part, blocks[1], blocks[3]))
+    image_part, *blocks = lax.optimization_barrier((image_part, *blocks))
     image_parts = exchange(image_part.reshape(NZ, R, d), "z")
     unit_grad_image = image_parts.astype(f32).sum(axis=0)
 
+    opposite = shift(blocks[2], "x", NX, 2)
     total = blocks[0].astype(f32) + opposite.astype(f32)
-    total = total + shift(blocks[1], "x", NX, 1).astype(f32) + shift(blocks[3], "x", NX, 3).astype(f32)
+    total = total + cross(blocks[1], 1).astype(f32) + cross(blocks[3], 3).astype(f32)
     total = total.astype(bf16).reshape(NY, R, d)
-    total, unit_grad_image = lax.optimization_barrier((total, unit_grad_image))
+    image_grad = tangent(unit_grad_image, image_unit, image_gain)
+    total, image_grad = lax.optimization_barrier((total, image_grad))
     unit_grad_text = exchange(total, "y").astype(f32).sum(axis=0)
 
-    return (
-        tangent(unit_grad_image, image_unit, image_gain),
-        tangent(unit_grad_text, text_unit, text_gain),
-    )
+    return image_grad, tangent(unit_grad_text, text_unit, text_gain)
 
 
 def solution(mesh):

time: 98.7 us -> 98.5 us (level)
  blocking collectives: 16.9 us -> 30.1 us
  waiting for transfers between devices: 24.1 us -> 14.7 us
  starting transfers between devices: 45.8 us -> 42.6 us
    all_to_all x0 -> x1, blocking collectives: none -> 13.2 us  [exchange(): return lax.all_to_all(blocks, axis, split_axis=0, concat_axis=0, tiled=True)]
    all_to_all x4 -> x3, waiting for transfers between devices: 16.7 us -> 6.7 us  [exchange(): return lax.all_to_all(blocks, axis, split_axis=0, concat_axis=0, tiled=True)]
    ppermute x0 -> x2, waiting for transfers between devices: none -> 7.3 us  [cross(): return lax.ppermute(block, ('x', 'core'), moves)]
    ppermute x4 -> x2, waiting for transfers between devices: 7.33 us -> 0.71 us  [shift(): return lax.ppermute(block, axis, [(i, (i + k) % n) for i in range(n)])]
    ppermute x0 -> x2, starting transfers between devices: none -> 5.97 us  [cross(): return lax.ppermute(block, ('x', 'core'), moves)]
    ppermute x4 -> x2, starting transfers between devices: 11.2 us -> 5.41 us  [shift(): return lax.ppermute(block, axis, [(i, (i + k) % n) for i in range(n)])]
    all_to_all x4 -> x3, starting transfers between devices: 34.6 us -> 31.2 us  [exchange(): return lax.all_to_all(blocks, axis, split_axis=0, concat_axis=0, tiled=True)]
  transfers between devices with their start and end apart: 8 -> 7, of which waited for: 7 -> 4; matrix products, arithmetic and copies ran while one was open for 3% -> 2% of each run, Pallas kernels for 2% -> 2%
where the time goes in v5:
time: 98.5 us; the launch traced here: 97.7 us
  starting transfers between devices  42.6 us (43%)
  blocking collectives  30.1 us (31%)
  waiting for transfers between devices  14.7 us (15%)
  Pallas kernels  3.31 us (3%)
  other arithmetic  2.59 us (3%)
  between operations  2.11 us (2%)
  matrix products  1.34 us (1%)
  local copies, waits for them, and re-layouts  1 us (1%)
    all_to_all x3, starting transfers between devices, exchange(): return lax.all_to_all(blocks, axis, split_axis=0, concat_axis=0, tiled=True)  31.2 us
    all_gather x1, blocking collectives, shards(): lax.all_gather(exchange(text_send, 'y').reshape(half_rows, d), 'x', axis=...  14.7 us
    all_to_all x1, blocking collectives, exchange(): return lax.all_to_all(blocks, axis, split_axis=0, concat_axis=0, tiled=True)  13.2 us
    ppermute x2, waiting for transfers between devices, cross(): return lax.ppermute(block, ('x', 'core'), moves)  7.3 us
    all_to_all x3, waiting for transfers between devices, exchange(): return lax.all_to_all(blocks, axis, split_axis=0, concat_axis=0, tiled=True)  6.7 us
    ppermute x2, starting transfers between devices, cross(): return lax.ppermute(block, ('x', 'core'), moves)  5.97 us
    ppermute x2, starting transfers between devices, shift(): return lax.ppermute(block, axis, [(i, (i + k) % n) for i in range(n)])  5.41 us
    all_gather x1, blocking collectives, shards(): lax.all_gather(exchange(image_send, 'z').reshape(own, d), 'core', axis=0,...  2.22 us
  transfers between devices with their start and end apart: 7, of which 4 were waited for; matrix products, arithmetic and copies ran while one was open for 2% of the time, Pallas kernels for 2%

profile of v5, /device:TPU:64, one launch (start us, length us, event | category | flops | bytes accessed | tf_op | source)
XLA Modules:
  0.0 97.7 jit_solution(2159666609471931467)
XLA Ops:
  0.6 1.6 %shard_map.87 = bf16[8,8,1536]{2,1,0:T(8,128)(2,1)} custom-call(bf16[8,1536]{1,0:T(8,128)(2,1)} %mantissa_ref.1, s32[8]{0:T(128)} %exponent_ref.1), custom_call_target="tpu_custom_call" | custom-call | tf_op jit(solution)/shard_map/pallas_call | solution.py:56
  2.2 7.1 %all-to-all-start.1 = ((bf16[8,8,1536]{2,1,0:T(8,128)(2,1)}), bf16[8,8,1536]{2,1,0:T(8,128)(2,1)S(1)}, u32[]{:S(2)}, u32[]{:S(2)}) async-start(bf16[8,8,1536]{2,1,0:T(8,128)(2,1)} %shard_map.87), calls=%async_computation.1 | async-start | bytes 393216 | tf_op jit(solution)/shard_map/all_to_all | solution.py:79
  9.3 0.8 reshape.98
  10.2 0.1 reshape.99
  11.6 1.7 %shard_map.86 = (bf16[12,8,1536]{2,1,0:T(8,128)(2,1)}, f32[8,1536]{1,0:T(8,128)}, f32[8,1536]{1,0:T(8,128)}, f32[8,1536]{1,0:T(8,128)}, f32[8,1536]{1,0:T(8,128)}, /*index=5*/f32[1,256]{1,0:T(1,128)}, f32[1,256]{1,0:T(1,128)}) custom-call(bf16[8,1536]{1,0:T(8,128)(2,1)} %image_ref, s32[8]{0:T(128)} %image_exponent_ref.1, bf16[8,1536]{1,0:T(8,128)(2,1)} %mantissa_ref.1, ...), custom_call_target="tpu_custom_call" | custom-call | tf_op jit(solution)/shard_map/pallas_call | solution.py:68
  13.3 6.5 %all-to-all-done.1 = bf16[8,8,1536]{2,1,0:T(8,128)(2,1)S(1)} async-done(((bf16[8,8,1536]{2,1,0:T(8,128)(2,1)}), bf16[8,8,1536]{2,1,0:T(8,128)(2,1)S(1)}, u32[]{:S(2)}, u32[]{:S(2)}) %all-to-all-start.1) | async-done | bytes 196640 | tf_op jit(solution)/shard_map/all_to_all | solution.py:79
  19.8 14.8 %all-to-all-start = ((bf16[12,8,1536]{2,1,0:T(8,128)(2,1)}), bf16[12,8,1536]{2,1,0:T(8,128)(2,1)S(1)}, u32[]{:S(2)}, u32[]{:S(2)}) async-start(bf16[12,8,1536]{2,1,0:T(8,128)(2,1)} %get-tuple-element.23), calls=%async_computation | async-start | bytes 589824 | tf_op jit(solution)/shard_map/all_to_all | solution.py:79
  34.6 0.0 copy-start.4
  34.6 0.0 copy-start.5
  34.6 14.7 %all_gather.7 = bf16[256,1536]{1,0:T(8,128)(2,1)S(1)} all-gather(bf16[64,1536]{1,0:T(8,128)(2,1)S(1)} %bitcast.26), channel_id=1, replica_groups=mesh['y'=8,'z'=12,'x'=4,'core'=2] {'x'}, dimensions={0}, use_global_device_ids=true | all-gather | bytes 983040 | tf_op jit(solution)/shard_map/all_gather | solution.py:123
  49.3 0.0 all-to-all-done
  49.3 2.2 %all_gather.6 = bf16[192,1536]{1,0:T(8,128)(2,1)S(1)} all-gather(bf16[96,1536]{1,0:T(8,128)(2,1)S(1)} %bitcast.25), channel_id=1, replica_groups=mesh['y'=8,'z'=12,'x'=4,'core'=2] {'core'}, dimensions={0}, use_global_device_ids=true | all-gather | bytes 884736 | tf_op jit(solution)/shard_map/all_gather | solution.py:124
  51.6 0.0 copy-done.4
  51.6 0.0 copy-done.5
  51.6 0.5 fusion.7
  52.0 0.3 convolution_convert_fusion.1
  52.3 2.0 %collective-permute-start = (bf16[96,1536]{1,0:T(8,128)(2,1)S(1)}, bf16[96,1536]{1,0:T(8,128)(2,1)S(1)}, u32[]{:S(2)}, u32[]{:S(2)}) collective-permute-start(bf16[96,1536]{1,0:T(8,128)(2,1)S(1)} %convolution_convert_fusion.1), channel_id=1, source_target_pairs={{0,1},{1,0},{2,3},{3,2},{4,5},{5,4},{6,7},{7,6},{8,9},{9,8},{10,11... | collective-permute-start | bytes 884744 | tf_op jit(solution)/shard_map/ppermute | solution.py:83
  54.3 0.4 convolution_convert_fusion
  54.7 0.3 fusion.10
  55.0 0.1 dynamic-slice_bitcast_fusion
  55.0 0.7 collective-permute-done
  55.8 0.8 add_convert_fusion
  56.5 9.3 %all-to-all-start.2 = ((bf16[12,8,1536]{2,1,0:T(8,128)(2,1)}), bf16[12,8,1536]{2,1,0:T(8,128)(2,1)S(1)}, u32[]{:S(2)}, u32[]{:S(2)}) async-start(bf16[12,8,1536]{2,1,0:T(8,128)(2,1)} %bitcast.12), calls=%async_computation.2 | async-start | bytes 589824 | tf_op jit(solution)/shard_map/all_to_all | solution.py:79
  65.8 0.0 copy-start.1
  65.8 0.0 copy-start.3
  65.8 3.7 %collective-permute-start.3 = (bf16[64,1536]{1,0:T(8,128)(2,1)S(1)}, bf16[64,1536]{1,0:T(8,128)(2,1)S(1)}, u32[]{:S(2)}, u32[]{:S(2)}) collective-permute-start(bf16[64,1536]{1,0:T(8,128)(2,1)S(1)} %get-tuple-element.30), channel_id=1, source_target_pairs={{0,6},{1,3},{2,0},{3,5},{4,2},{5,7},{6,4},{7,1},{8,14},{9,11},{10,... | collective-permute-start | bytes 589832 | tf_op jit(solution)/shard_map/ppermute | solution.py:88
  69.5 2.3 %collective-permute-start.2 = (bf16[64,1536]{1,0:T(8,128)(2,1)S(1)}, bf16[64,1536]{1,0:T(8,128)(2,1)S(1)}, u32[]{:S(2)}, u32[]{:S(2)}) collective-permute-start(bf16[64,1536]{1,0:T(8,128)(2,1)S(1)} %get-tuple-element.29), channel_id=1, source_target_pairs={{0,2},{1,7},{2,4},{3,1},{4,6},{5,3},{6,0},{7,5},{8,10},{9,15},{10,... | collective-permute-start | bytes 589832 | tf_op jit(solution)/shard_map/ppermute | solution.py:88
  71.8 3.4 %collective-permute-start.1 = (bf16[64,1536]{1,0:T(8,128)(2,1)S(1)}, bf16[64,1536]{1,0:T(8,128)(2,1)S(1)}, u32[]{:S(2)}, u32[]{:S(2)}) collective-permute-start(bf16[64,1536]{1,0:T(8,128)(2,1)S(1)} %get-tuple-element.28), channel_id=1, source_target_pairs={{0,4},{2,6},{4,0},{6,2},{1,5},{3,7},{5,1},{7,3},{8,12},{10,14},{12... | collective-permute-start | bytes 589832 | tf_op jit(solution)/shard_map/ppermute | solution.py:83
  75.2 0.0 collective-permute-done.3
  75.2 7.3 %collective-permute-done.2 = bf16[64,1536]{1,0:T(8,128)(2,1)S(1)} collective-permute-done((bf16[64,1536]{1,0:T(8,128)(2,1)S(1)}, bf16[64,1536]{1,0:T(8,128)(2,1)S(1)}, u32[]{:S(2)}, u32[]{:S(2)}) %collective-permute-start.2) | collective-permute-done | bytes 196640 | tf_op jit(solution)/shard_map/ppermute | solution.py:88
  82.5 0.0 collective-permute-done.1
  82.5 0.1 fusion.8
  82.6 0.0 copy-start
  82.6 0.0 copy-start.2
  82.7 0.2 all-to-all-done.2
  82.9 0.0 copy-done.1
  82.9 0.1 multiply_reduce_fusion.1
  83.0 0.0 copy-done.3
  83.0 0.7 subtract_multiply_fusion.1
  83.7 13.2 %all_to_all.20 = bf16[8,8,1536]{2,1,0:T(8,128)(2,1)S(1)} all-to-all(bf16[8,8,1536]{2,1,0:T(8,128)(2,1)S(1)} %fusion.8), channel_id=1, replica_groups=mesh['y'=8,'z'=12,'x'=4,'core'=2] {'y'}, dimensions={0} | all-to-all | bytes 393216 | tf_op jit(solution)/shard_map/all_to_all | solution.py:79
  96.9 0.0 copy-done
  96.9 0.1 multiply_reduce_fusion
  97.0 0.0 copy-done.2
  97.0 0.7 subtract_multiply_fusion
  (6 shorter events, 0.1 us)
Async XLA Ops:
  2.2 17.6 %all-to-all-start.1 = ((bf16[8,8,1536]{2,1,0:T(8,128)(2,1)}), bf16[8,8,1536]{2,1,0:T(8,128)(2,1)S(1)}, u32[]{:S(2)}, u32[]{:S(2)}) async-start(bf16[8,8,1536]{2,1,0:T(8,128)(2,1)} %shard_map.87), calls=%async_computation.1 | async-start | bytes 393216 | tf_op jit(solution)/shard_map/all_to_all | solution.py:79
  19.8 29.5 %all-to-all-start = ((bf16[12,8,1536]{2,1,0:T(8,128)(2,1)}), bf16[12,8,1536]{2,1,0:T(8,128)(2,1)S(1)}, u32[]{:S(2)}, u32[]{:S(2)}) async-start(bf16[12,8,1536]{2,1,0:T(8,128)(2,1)} %get-tuple-element.23), calls=%async_computation | async-start | bytes 589824 | tf_op jit(solution)/shard_map/all_to_all | solution.py:79
  34.6 17.0 %copy-start.4 = (f32[1,256]{1,0:T(1,128)S(1)}, f32[1,256]{1,0:T(1,128)}, u32[]{:S(2)}) copy-start(f32[1,256]{1,0:T(1,128)} %get-tuple-element.22) | copy-start | bytes 3076
  34.6 16.9 %copy-start.5 = (f32[1,256]{1,0:T(1,128)S(1)}, f32[1,256]{1,0:T(1,128)}, u32[]{:S(2)}) copy-start(f32[1,256]{1,0:T(1,128)} %get-tuple-element.24) | copy-start | bytes 3076
  52.3 3.5 %collective-permute-start = (bf16[96,1536]{1,0:T(8,128)(2,1)S(1)}, bf16[96,1536]{1,0:T(8,128)(2,1)S(1)}, u32[]{:S(2)}, u32[]{:S(2)}) collective-permute-start(bf16[96,1536]{1,0:T(8,128)(2,1)S(1)} %convolution_convert_fusion.1), channel_id=1, source_target_pairs={{0,1},{1,0},{2,3},{3,2},{4,5},{5,4},{6,7},{7,6},{8,9},{9,8},{10,11... | collective-permute-start | bytes 884744 | tf_op jit(solution)/shard_map/ppermute | solution.py:83
  56.5 26.3 %all-to-all-start.2 = ((bf16[12,8,1536]{2,1,0:T(8,128)(2,1)}), bf16[12,8,1536]{2,1,0:T(8,128)(2,1)S(1)}, u32[]{:S(2)}, u32[]{:S(2)}) async-start(bf16[12,8,1536]{2,1,0:T(8,128)(2,1)} %bitcast.12), calls=%async_computation.2 | async-start | bytes 589824 | tf_op jit(solution)/shard_map/all_to_all | solution.py:79
  65.8 17.0 %copy-start.1 = (f32[8,1536]{1,0:T(8,128)S(1)}, f32[8,1536]{1,0:T(8,128)}, u32[]{:S(2)}) copy-start(f32[8,1536]{1,0:T(8,128)} %get-tuple-element.32) | copy-start | bytes 147460
  65.8 17.2 %copy-start.3 = (f32[8,1536]{1,0:T(8,128)S(1)}, f32[8,1536]{1,0:T(8,128)}, u32[]{:S(2)}) copy-start(f32[8,1536]{1,0:T(8,128)} %get-tuple-element.33) | copy-start | bytes 147460
  65.8 9.4 %collective-permute-start.3 = (bf16[64,1536]{1,0:T(8,128)(2,1)S(1)}, bf16[64,1536]{1,0:T(8,128)(2,1)S(1)}, u32[]{:S(2)}, u32[]{:S(2)}) collective-permute-start(bf16[64,1536]{1,0:T(8,128)(2,1)S(1)} %get-tuple-element.30), channel_id=1, source_target_pairs={{0,6},{1,3},{2,0},{3,5},{4,2},{5,7},{6,4},{7,1},{8,14},{9,11},{10,... | collective-permute-start | bytes 589832 | tf_op jit(solution)/shard_map/ppermute | solution.py:88
  69.5 13.0 %collective-permute-start.2 = (bf16[64,1536]{1,0:T(8,128)(2,1)S(1)}, bf16[64,1536]{1,0:T(8,128)(2,1)S(1)}, u32[]{:S(2)}, u32[]{:S(2)}) collective-permute-start(bf16[64,1536]{1,0:T(8,128)(2,1)S(1)} %get-tuple-element.29), channel_id=1, source_target_pairs={{0,2},{1,7},{2,4},{3,1},{4,6},{5,3},{6,0},{7,5},{8,10},{9,15},{10,... | collective-permute-start | bytes 589832 | tf_op jit(solution)/shard_map/ppermute | solution.py:88
  71.8 10.7 %collective-permute-start.1 = (bf16[64,1536]{1,0:T(8,128)(2,1)S(1)}, bf16[64,1536]{1,0:T(8,128)(2,1)S(1)}, u32[]{:S(2)}, u32[]{:S(2)}) collective-permute-start(bf16[64,1536]{1,0:T(8,128)(2,1)S(1)} %get-tuple-element.28), channel_id=1, source_target_pairs={{0,4},{2,6},{4,0},{6,2},{1,5},{3,7},{5,1},{7,3},{8,12},{10,14},{12... | collective-permute-start | bytes 589832 | tf_op jit(solution)/shard_map/ppermute | solution.py:83
  82.6 14.3 %copy-start = (f32[8,1536]{1,0:T(8,128)S(1)}, f32[8,1536]{1,0:T(8,128)}, u32[]{:S(2)}) copy-start(f32[8,1536]{1,0:T(8,128)} %get-tuple-element.36) | copy-start | bytes 147460
  82.6 14.4 %copy-start.2 = (f32[8,1536]{1,0:T(8,128)S(1)}, f32[8,1536]{1,0:T(8,128)}, u32[]{:S(2)}) copy-start(f32[8,1536]{1,0:T(8,128)} %get-tuple-element.37) | copy-start | bytes 147460

commit v6 on v5

--- a/solution.py
+++ b/solution.py
@@ -110,37 +110,41 @@
     near_rows = NX * half_rows
     own = NZ * R
 
-    place = positive.reshape(NZ, NX, NC, R).transpose(1, 2, 0, 3).reshape(NX, NC * own)
-    place = rows_at(place, x, 1).reshape(NC * own)
-    place = place - (z * (NC * near_rows) + c * half_rows)
-    place = jnp.where((place >= 0) & (place < NC * near_rows), place, -1)
+    place = positive.reshape(NZ, NX * NC, R).transpose(1, 0, 2).reshape(NX * NC, own)
+    place = place - z * (NX * NC * half_rows)
+    far_place = rows_at(place, x * NC + 1 - c, 1).reshape(own)
+    place = rows_at(place, x * NC + c, 1).reshape(own)
 
     text_send = text_prologue(text_mantissa, text_exponent)
-    image_mantissa, place = lax.optimization_barrier((image_mantissa, place))
+    image_mantissa, place, far_place = lax.optimization_barrier((image_mantissa, place, far_place))
     image_send, image_unit, image_gain, text_unit, text_gain, scale, bias = image_prologue(
         image_mantissa, image_exponent, text_mantissa, text_exponent, logit_scale, logit_bias
     )
     texts = lax.all_gather(exchange(text_send, "y").reshape(half_rows, d), "x", axis=0, tiled=True)
-    images = lax.all_gather(exchange(image_send, "z").reshape(own, d), "core", axis=0, tiled=True)
+    far_texts = shift(texts, "core", NC, 1)
+    images = exchange(image_send, "z").reshape(own, d)
+    far_images = shift(images, "core", NC, 1)
 
     column = jnp.arange(near_rows, dtype=jnp.int32)[None, :]
-    target = (column // half_rows) * (NC * half_rows) + column % half_rows
-    logits = scale * product(images, texts.T) + bias
-    label_sign = jnp.where(place[:, None] == target, 1.0, -1.0).astype(f32)
-    weights = (-label_sign * jax.nn.sigmoid(-label_sign * logits)).astype(bf16)
 
-    far = rows_at(weights, (1 - c) * own, own)
-    near = rows_at(weights, c * own, own)
-    far = product(far, texts).astype(bf16)
-    far, weights = lax.optimization_barrier((far, weights))
-    far = shift(far, "core", NC, 1)
+    def weigh(images, place, texts, core):
+        target = (column // half_rows * NC + core) * half_rows + column % half_rows
+        logits = scale * product(images, texts.T) + bias
+        label_sign = jnp.where(place[:, None] == target, 1.0, -1.0).astype(f32)
+        return (-label_sign * jax.nn.sigmoid(-label_sign * logits)).astype(bf16)
 
+    weights = weigh(images, place, texts, c)
+    near = lax.optimization_barrier(product(weights, texts))
+    cross_weights = weigh(images, place, far_texts, 1 - c)
+    image_part = (near + product(cross_weights, far_texts)).astype(bf16)
+
+    image_part, far_images = lax.optimization_barrier((image_part, far_images))
+    far_weights = weigh(far_images, far_place, texts, c)
+    weights = jnp.concatenate([weights, far_weights], axis=0)
+    images = jnp.concatenate([images, far_images], axis=0)
     part = product(weights.T, images).astype(bf16).reshape(NX, half_rows, d)
     ways = (0, 1 + 2 * c, 2, 3 - 2 * c)
     blocks = [rows_at(part, (x + k) & (NX - 1), 1).reshape(half_rows, d) for k in ways]
-    near = lax.optimization_barrier(product(near, texts))
-    image_part = (near + far.astype(f32)).astype(bf16)
-    image_part, *blocks = lax.optimization_barrier((image_part, *blocks))
     image_parts = exchange(image_part.reshape(NZ, R, d), "z")
     unit_grad_image = image_parts.astype(f32).sum(axis=0)
 

time: 98.5 us -> 98 us (level)
  starting transfers between devices: 42.6 us -> 46.2 us
  waiting for transfers between devices: 14.7 us -> 11.9 us
  blocking collectives: 30.1 us -> 27.9 us
  matrix products: 1.34 us -> 2.96 us
    ppermute x2, waiting for transfers between devices: 7.3 us -> 3.44 us  [cross(): return lax.ppermute(block, ('x', 'core'), moves)]
    ppermute x2 -> x3, starting transfers between devices: 5.41 us -> 7.82 us  [shift(): return lax.ppermute(block, axis, [(i, (i + k) % n) for i in range(n)])]
    all_gather x1 -> x0, blocking collectives: 2.22 us -> none  [shards(): lax.all_gather(exchange(image_send, 'z').reshape(own, d), 'core', axis=0,...]
    all_to_all x3, waiting for transfers between devices: 6.7 us -> 8.4 us  [exchange(): return lax.all_to_all(blocks, axis, split_axis=0, concat_axis=0, tiled=True)]
    dot_general x4 -> x5, matrix products: 1.34 us -> 2.96 us  [product(): return jnp.dot(a, b, preferred_element_type=f32)]
    ppermute x2, starting transfers between devices: 5.97 us -> 7.05 us  [cross(): return lax.ppermute(block, ('x', 'core'), moves)]
  transfers between devices with their start and end apart: 7 -> 8, of which waited for: 4 -> 4; matrix products, arithmetic and copies ran while one was open for 2% -> 4% of each run, Pallas kernels for 2% -> 2%
where the time goes in v6:
time: 98 us; the launch traced here: 97.2 us
  starting transfers between devices  46.2 us (47%)
  blocking collectives  27.9 us (28%)
  waiting for transfers between devices  11.9 us (12%)
  Pallas kernels  3.31 us (3%)
  matrix products  2.96 us (3%)
  other arithmetic  2.53 us (3%)
  between operations  2.14 us (2%)
    all_to_all x3, starting transfers between devices, exchange(): return lax.all_to_all(blocks, axis, split_axis=0, concat_axis=0, tiled=True)  31.3 us
    all_gather x1, blocking collectives, shards(): lax.all_gather(exchange(text_send, 'y').reshape(half_rows, d), 'x', axis=...  14.7 us
    all_to_all x1, blocking collectives, exchange(): return lax.all_to_all(blocks, axis, split_axis=0, concat_axis=0, tiled=True)  13.2 us
    all_to_all x3, waiting for transfers between devices, exchange(): return lax.all_to_all(blocks, axis, split_axis=0, concat_axis=0, tiled=True)  8.4 us
    ppermute x3, starting transfers between devices, shift(): return lax.ppermute(block, axis, [(i, (i + k) % n) for i in range(n)])  7.82 us
    ppermute x2, starting transfers between devices, cross(): return lax.ppermute(block, ('x', 'core'), moves)  7.05 us
    ppermute x2, waiting for transfers between devices, cross(): return lax.ppermute(block, ('x', 'core'), moves)  3.44 us
    dot_general x5, matrix products, product(): return jnp.dot(a, b, preferred_element_type=f32)  2.96 us
  transfers between devices with their start and end apart: 8, of which 4 were waited for; matrix products, arithmetic and copies ran while one was open for 4% of the time, Pallas kernels for 2%

profile of v6, /device:TPU:64, one launch (start us, length us, event | category | flops | bytes accessed | tf_op | source)
XLA Modules:
  0.0 97.2 jit_solution(3584192885767538930)
XLA Ops:
  0.6 1.6 %shard_map.87 = bf16[8,8,1536]{2,1,0:T(8,128)(2,1)} custom-call(bf16[8,1536]{1,0:T(8,128)(2,1)} %mantissa_ref.1, s32[8]{0:T(128)} %exponent_ref.1), custom_call_target="tpu_custom_call" | custom-call | tf_op jit(solution)/shard_map/pallas_call | solution.py:56
  2.2 7.1 %all-to-all-start.1 = ((bf16[8,8,1536]{2,1,0:T(8,128)(2,1)}), bf16[8,8,1536]{2,1,0:T(8,128)(2,1)S(1)}, u32[]{:S(2)}, u32[]{:S(2)}) async-start(bf16[8,8,1536]{2,1,0:T(8,128)(2,1)} %shard_map.87), calls=%async_computation.1 | async-start | bytes 393216 | tf_op jit(solution)/shard_map/all_to_all | solution.py:79
  9.3 0.7 broadcast_subtract_fusion
  10.0 0.1 sub.44
  10.1 0.1 sub.46
  11.5 1.7 %shard_map.86 = (bf16[12,8,1536]{2,1,0:T(8,128)(2,1)}, f32[8,1536]{1,0:T(8,128)}, f32[8,1536]{1,0:T(8,128)}, f32[8,1536]{1,0:T(8,128)}, f32[8,1536]{1,0:T(8,128)}, /*index=5*/f32[1,256]{1,0:T(1,128)}, f32[1,256]{1,0:T(1,128)}) custom-call(bf16[8,1536]{1,0:T(8,128)(2,1)} %image_ref, s32[8]{0:T(128)} %image_exponent_ref.1, bf16[8,1536]{1,0:T(8,128)(2,1)} %mantissa_ref.1, ...), custom_call_target="tpu_custom_call" | custom-call | tf_op jit(solution)/shard_map/pallas_call | solution.py:68
  13.2 6.6 %all-to-all-done.1 = bf16[8,8,1536]{2,1,0:T(8,128)(2,1)S(1)} async-done(((bf16[8,8,1536]{2,1,0:T(8,128)(2,1)}), bf16[8,8,1536]{2,1,0:T(8,128)(2,1)S(1)}, u32[]{:S(2)}, u32[]{:S(2)}) %all-to-all-start.1) | async-done | bytes 196640 | tf_op jit(solution)/shard_map/all_to_all | solution.py:79
  19.8 0.0 copy-start.4
  19.8 0.0 copy-start.5
  19.8 14.9 %all-to-all-start = ((bf16[12,8,1536]{2,1,0:T(8,128)(2,1)}), bf16[12,8,1536]{2,1,0:T(8,128)(2,1)S(1)}, u32[]{:S(2)}, u32[]{:S(2)}) async-start(bf16[12,8,1536]{2,1,0:T(8,128)(2,1)} %get-tuple-element.19), calls=%async_computation | async-start | bytes 589824 | tf_op jit(solution)/shard_map/all_to_all | solution.py:79
  34.7 14.7 %all_gather.3 = bf16[256,1536]{1,0:T(8,128)(2,1)S(1)} all-gather(bf16[64,1536]{1,0:T(8,128)(2,1)S(1)} %bitcast.38), channel_id=1, replica_groups=mesh['y'=8,'z'=12,'x'=4,'core'=2] {'x'}, dimensions={0}, use_global_device_ids=true | all-gather | bytes 983040 | tf_op jit(solution)/shard_map/all_gather | solution.py:123
  49.4 1.9 %collective-permute-start = (bf16[256,1536]{1,0:T(8,128)(2,1)S(1)}, bf16[256,1536]{1,0:T(8,128)(2,1)S(1)}, u32[]{:S(2)}, u32[]{:S(2)}) collective-permute-start(bf16[256,1536]{1,0:T(8,128)(2,1)S(1)} %all_gather.3), channel_id=1, source_target_pairs={{0,1},{1,0},{2,3},{3,2},{4,5},{5,4},{6,7},{7,6},{8,9},{9,8},{10,11... | collective-permute-start | bytes 2359304 | tf_op jit(solution)/shard_map/ppermute | solution.py:83
  51.4 0.0 all-to-all-done
  51.4 2.4 %collective-permute-start.1 = (bf16[96,1536]{1,0:T(8,128)(2,1)S(1)}, bf16[96,1536]{1,0:T(8,128)(2,1)S(1)}, u32[]{:S(2)}, u32[]{:S(2)}) collective-permute-start(bf16[96,1536]{1,0:T(8,128)(2,1)S(1)} %bitcast.34), channel_id=1, source_target_pairs={{0,1},{1,0},{2,3},{3,2},{4,5},{5,4},{6,7},{7,6},{8,9},{9,8},{10,11... | collective-permute-start | bytes 884744 | tf_op jit(solution)/shard_map/ppermute | solution.py:83
  53.8 0.0 copy-done.4
  53.8 0.0 copy-done.5
  53.8 0.4 fusion.24
  54.2 0.3 fusion.55
  54.5 0.0 collective-permute-done
  54.5 1.5 %fusion = bf16[96,1536]{1,0:T(8,128)(2,1)} fusion(f32[96,1536]{1,0:T(8,128)S(1)} %fusion.55, bf16[256,1536]{1,0:T(8,128)(2,1)S(1)} %collective-permute-done, s32[256]{0:T(256)S(1)} %multiply_add_fusion, f32[256]{0:T(256)S(1)} %bitcast.44, f32[256]{0:T(256)S(1)} %bitcast.41, s32[96]{0:T(128)S(1)} %get-tuple-element.16, bf16[12,8,1536]{2,1,0:T(8,128)(2,1)S(1)} %all-to-all-done), kind=kOutput, calls=%fused_computation.2 | convolution fusion | flops 151560192 | bytes 1969536 | tf_op jit(solution)/shard_map/dot_general | solution.py:97
  56.0 0.0 collective-permute-done.1
  56.0 9.3 %all-to-all-start.2 = ((bf16[12,8,1536]{2,1,0:T(8,128)(2,1)}), bf16[12,8,1536]{2,1,0:T(8,128)(2,1)S(1)}, u32[]{:S(2)}, u32[]{:S(2)}) async-start(bf16[12,8,1536]{2,1,0:T(8,128)(2,1)} %bitcast.13), calls=%async_computation.2 | async-start | bytes 589824 | tf_op jit(solution)/shard_map/all_to_all | solution.py:79
  65.4 0.4 fusion.22
  65.8 0.4 convolution_convert_fusion
  66.2 0.1 dynamic-slice_bitcast_fusion.2
  66.2 0.0 copy-start.1
  66.2 0.0 copy-start.3
  66.2 3.5 %collective-permute-start.2 = (bf16[64,1536]{1,0:T(8,128)(2,1)S(1)}, bf16[64,1536]{1,0:T(8,128)(2,1)S(1)}, u32[]{:S(2)}, u32[]{:S(2)}) collective-permute-start(bf16[64,1536]{1,0:T(8,128)(2,1)S(1)} %get-tuple-element.30), channel_id=1, source_target_pairs={{0,4},{2,6},{4,0},{6,2},{1,5},{3,7},{5,1},{7,3},{8,12},{10,14},{12... | collective-permute-start | bytes 589832 | tf_op jit(solution)/shard_map/ppermute | solution.py:83
  69.7 3.0 %collective-permute-start.3 = (bf16[64,1536]{1,0:T(8,128)(2,1)S(1)}, bf16[64,1536]{1,0:T(8,128)(2,1)S(1)}, u32[]{:S(2)}, u32[]{:S(2)}) collective-permute-start(bf16[64,1536]{1,0:T(8,128)(2,1)S(1)} %get-tuple-element.32), channel_id=1, source_target_pairs={{0,2},{1,7},{2,4},{3,1},{4,6},{5,3},{6,0},{7,5},{8,10},{9,15},{10,... | collective-permute-start | bytes 589832 | tf_op jit(solution)/shard_map/ppermute | solution.py:88
  72.7 4.1 %collective-permute-start.4 = (bf16[64,1536]{1,0:T(8,128)(2,1)S(1)}, bf16[64,1536]{1,0:T(8,128)(2,1)S(1)}, u32[]{:S(2)}, u32[]{:S(2)}) collective-permute-start(bf16[64,1536]{1,0:T(8,128)(2,1)S(1)} %get-tuple-element.31), channel_id=1, source_target_pairs={{0,6},{1,3},{2,0},{3,5},{4,2},{5,7},{6,4},{7,1},{8,14},{9,11},{10,... | collective-permute-start | bytes 589832 | tf_op jit(solution)/shard_map/ppermute | solution.py:88
  76.8 0.0 collective-permute-done.2
  76.8 2.3 %collective-permute-done.3 = bf16[64,1536]{1,0:T(8,128)(2,1)S(1)} collective-permute-done((bf16[64,1536]{1,0:T(8,128)(2,1)S(1)}, bf16[64,1536]{1,0:T(8,128)(2,1)S(1)}, u32[]{:S(2)}, u32[]{:S(2)}) %collective-permute-start.3) | collective-permute-done | bytes 196640 | tf_op jit(solution)/shard_map/ppermute | solution.py:88
  79.1 1.2 %collective-permute-done.4 = bf16[64,1536]{1,0:T(8,128)(2,1)S(1)} collective-permute-done((bf16[64,1536]{1,0:T(8,128)(2,1)S(1)}, bf16[64,1536]{1,0:T(8,128)(2,1)S(1)}, u32[]{:S(2)}, u32[]{:S(2)}) %collective-permute-start.4) | collective-permute-done | bytes 196640 | tf_op jit(solution)/shard_map/ppermute | solution.py:88
  80.3 0.1 fusion.31
  80.4 0.0 copy-start
  80.4 0.0 copy-start.2
  80.4 1.8 %all-to-all-done.2 = bf16[12,8,1536]{2,1,0:T(8,128)(2,1)S(1)} async-done(((bf16[12,8,1536]{2,1,0:T(8,128)(2,1)}), bf16[12,8,1536]{2,1,0:T(8,128)(2,1)S(1)}, u32[]{:S(2)}, u32[]{:S(2)}) %all-to-all-start.2) | async-done | bytes 294944 | tf_op jit(solution)/shard_map/all_to_all | solution.py:79
  82.3 0.0 copy-done.1
  82.3 0.1 multiply_reduce_fusion.1
  82.4 0.0 copy-done.3
  82.4 0.7 subtract_multiply_fusion.1
  83.1 13.2 %all_to_all.20 = bf16[8,8,1536]{2,1,0:T(8,128)(2,1)S(1)} all-to-all(bf16[8,8,1536]{2,1,0:T(8,128)(2,1)S(1)} %fusion.31), channel_id=1, replica_groups=mesh['y'=8,'z'=12,'x'=4,'core'=2] {'y'}, dimensions={0} | all-to-all | bytes 393216 | tf_op jit(solution)/shard_map/all_to_all | solution.py:79
  96.4 0.0 copy-done
  96.4 0.1 multiply_reduce_fusion
  96.5 0.0 copy-done.2
  96.5 0.7 subtract_multiply_fusion
  (6 shorter events, 0.1 us)
Async XLA Ops:
  2.2 17.6 %all-to-all-start.1 = ((bf16[8,8,1536]{2,1,0:T(8,128)(2,1)}), bf16[8,8,1536]{2,1,0:T(8,128)(2,1)S(1)}, u32[]{:S(2)}, u32[]{:S(2)}) async-start(bf16[8,8,1536]{2,1,0:T(8,128)(2,1)} %shard_map.87), calls=%async_computation.1 | async-start | bytes 393216 | tf_op jit(solution)/shard_map/all_to_all | solution.py:79
  19.8 34.0 %copy-start.4 = (f32[1,256]{1,0:T(1,128)S(1)}, f32[1,256]{1,0:T(1,128)}, u32[]{:S(2)}) copy-start(f32[1,256]{1,0:T(1,128)} %get-tuple-element.18) | copy-start | bytes 3076
  19.8 34.0 %copy-start.5 = (f32[1,256]{1,0:T(1,128)S(1)}, f32[1,256]{1,0:T(1,128)}, u32[]{:S(2)}) copy-start(f32[1,256]{1,0:T(1,128)} %get-tuple-element.20) | copy-start | bytes 3076
  19.8 31.6 %all-to-all-start = ((bf16[12,8,1536]{2,1,0:T(8,128)(2,1)}), bf16[12,8,1536]{2,1,0:T(8,128)(2,1)S(1)}, u32[]{:S(2)}, u32[]{:S(2)}) async-start(bf16[12,8,1536]{2,1,0:T(8,128)(2,1)} %get-tuple-element.19), calls=%async_computation | async-start | bytes 589824 | tf_op jit(solution)/shard_map/all_to_all | solution.py:79
  49.4 5.1 %collective-permute-start = (bf16[256,1536]{1,0:T(8,128)(2,1)S(1)}, bf16[256,1536]{1,0:T(8,128)(2,1)S(1)}, u32[]{:S(2)}, u32[]{:S(2)}) collective-permute-start(bf16[256,1536]{1,0:T(8,128)(2,1)S(1)} %all_gather.3), channel_id=1, source_target_pairs={{0,1},{1,0},{2,3},{3,2},{4,5},{5,4},{6,7},{7,6},{8,9},{9,8},{10,11... | collective-permute-start | bytes 2359304 | tf_op jit(solution)/shard_map/ppermute | solution.py:83
  51.4 4.6 %collective-permute-start.1 = (bf16[96,1536]{1,0:T(8,128)(2,1)S(1)}, bf16[96,1536]{1,0:T(8,128)(2,1)S(1)}, u32[]{:S(2)}, u32[]{:S(2)}) collective-permute-start(bf16[96,1536]{1,0:T(8,128)(2,1)S(1)} %bitcast.34), channel_id=1, source_target_pairs={{0,1},{1,0},{2,3},{3,2},{4,5},{5,4},{6,7},{7,6},{8,9},{9,8},{10,11... | collective-permute-start | bytes 884744 | tf_op jit(solution)/shard_map/ppermute | solution.py:83
  56.0 26.2 %all-to-all-start.2 = ((bf16[12,8,1536]{2,1,0:T(8,128)(2,1)}), bf16[12,8,1536]{2,1,0:T(8,128)(2,1)S(1)}, u32[]{:S(2)}, u32[]{:S(2)}) async-start(bf16[12,8,1536]{2,1,0:T(8,128)(2,1)} %bitcast.13), calls=%async_computation.2 | async-start | bytes 589824 | tf_op jit(solution)/shard_map/all_to_all | solution.py:79
  66.2 16.1 %copy-start.1 = (f32[8,1536]{1,0:T(8,128)S(1)}, f32[8,1536]{1,0:T(8,128)}, u32[]{:S(2)}) copy-start(f32[8,1536]{1,0:T(8,128)} %get-tuple-element.24) | copy-start | bytes 147460
  66.2 16.2 %copy-start.3 = (f32[8,1536]{1,0:T(8,128)S(1)}, f32[8,1536]{1,0:T(8,128)}, u32[]{:S(2)}) copy-start(f32[8,1536]{1,0:T(8,128)} %get-tuple-element.25) | copy-start | bytes 147460
  66.2 10.6 %collective-permute-start.2 = (bf16[64,1536]{1,0:T(8,128)(2,1)S(1)}, bf16[64,1536]{1,0:T(8,128)(2,1)S(1)}, u32[]{:S(2)}, u32[]{:S(2)}) collective-permute-start(bf16[64,1536]{1,0:T(8,128)(2,1)S(1)} %get-tuple-element.30), channel_id=1, source_target_pairs={{0,4},{2,6},{4,0},{6,2},{1,5},{3,7},{5,1},{7,3},{8,12},{10,14},{12... | collective-permute-start | bytes 589832 | tf_op jit(solution)/shard_map/ppermute | solution.py:83
  69.7 9.3 %collective-permute-start.3 = (bf16[64,1536]{1,0:T(8,128)(2,1)S(1)}, bf16[64,1536]{1,0:T(8,128)(2,1)S(1)}, u32[]{:S(2)}, u32[]{:S(2)}) collective-permute-start(bf16[64,1536]{1,0:T(8,128)(2,1)S(1)} %get-tuple-element.32), channel_id=1, source_target_pairs={{0,2},{1,7},{2,4},{3,1},{4,6},{5,3},{6,0},{7,5},{8,10},{9,15},{10,... | collective-permute-start | bytes 589832 | tf_op jit(solution)/shard_map/ppermute | solution.py:88
  72.7 7.6 %collective-permute-start.4 = (bf16[64,1536]{1,0:T(8,128)(2,1)S(1)}, bf16[64,1536]{1,0:T(8,128)(2,1)S(1)}, u32[]{:S(2)}, u32[]{:S(2)}) collective-permute-start(bf16[64,1536]{1,0:T(8,128)(2,1)S(1)} %get-tuple-element.31), channel_id=1, source_target_pairs={{0,6},{1,3},{2,0},{3,5},{4,2},{5,7},{6,4},{7,1},{8,14},{9,11},{10,... | collective-permute-start | bytes 589832 | tf_op jit(solution)/shard_map/ppermute | solution.py:88
  80.4 16.0 %copy-start = (f32[8,1536]{1,0:T(8,128)S(1)}, f32[8,1536]{1,0:T(8,128)}, u32[]{:S(2)}) copy-start(f32[8,1536]{1,0:T(8,128)} %get-tuple-element.28) | copy-start | bytes 147460
  80.4 16.1 %copy-start.2 = (f32[8,1536]{1,0:T(8,128)S(1)}, f32[8,1536]{1,0:T(8,128)}, u32[]{:S(2)}) copy-start(f32[8,1536]{1,0:T(8,128)} %get-tuple-element.29) | copy-start | bytes 147460

commit v7 on v6

--- a/solution.py
+++ b/solution.py
@@ -8,6 +8,7 @@
 epsilon = 1e-06
 AXES = ("y", "z", "x", "core")
 NY, NZ, NX, NC = 8, 12, 4, 2
+FIRST_Y, FIRST_Z = 4, 11
 R = 8
 f32 = jnp.float32
 bf16 = jnp.bfloat16
@@ -75,8 +76,10 @@
     )(image, image_exponent, text, text_exponent, scale, bias)
 
 
-def exchange(blocks, axis):
-    return lax.all_to_all(blocks, axis, split_axis=0, concat_axis=0, tiled=True)
+def exchange(blocks, axis, first=0):
+    n = blocks.shape[0]
+    order = [[(first + k) % n for k in range(n)]]
+    return lax.all_to_all(blocks, axis, split_axis=0, concat_axis=0, axis_index_groups=order, tiled=True)
 
 
 def shift(block, axis, n, k):
@@ -112,30 +115,30 @@
 
     place = positive.reshape(NZ, NX * NC, R).transpose(1, 0, 2).reshape(NX * NC, own)
     place = place - z * (NX * NC * half_rows)
-    far_place = rows_at(place, x * NC + 1 - c, 1).reshape(own)
-    place = rows_at(place, x * NC + c, 1).reshape(own)
+    far_place = jnp.roll(rows_at(place, x * NC + 1 - c, 1).reshape(own), -FIRST_Z * R)
+    place = jnp.roll(rows_at(place, x * NC + c, 1).reshape(own), -FIRST_Z * R)
 
     text_send = text_prologue(text_mantissa, text_exponent)
     image_mantissa, place, far_place = lax.optimization_barrier((image_mantissa, place, far_place))
     image_send, image_unit, image_gain, text_unit, text_gain, scale, bias = image_prologue(
         image_mantissa, image_exponent, text_mantissa, text_exponent, logit_scale, logit_bias
     )
-    texts = lax.all_gather(exchange(text_send, "y").reshape(half_rows, d), "x", axis=0, tiled=True)
+    texts = lax.all_gather(exchange(text_send, "y", FIRST_Y).reshape(half_rows, d), "x", axis=0, tiled=True)
     far_texts = shift(texts, "core", NC, 1)
-    images = exchange(image_send, "z").reshape(own, d)
+    images = exchange(image_send, "z", FIRST_Z).reshape(own, d)
     far_images = shift(images, "core", NC, 1)
 
     column = jnp.arange(near_rows, dtype=jnp.int32)[None, :]
 
     def weigh(images, place, texts, core):
-        target = (column // half_rows * NC + core) * half_rows + column % half_rows
+        target = (column // half_rows * NC + core) * half_rows + (column + FIRST_Y * R) % half_rows
         logits = scale * product(images, texts.T) + bias
         label_sign = jnp.where(place[:, None] == target, 1.0, -1.0).astype(f32)
         return (-label_sign * jax.nn.sigmoid(-label_sign * logits)).astype(bf16)
 
     weights = weigh(images, place, texts, c)
-    near = lax.optimization_barrier(product(weights, texts))
-    cross_weights = weigh(images, place, far_texts, 1 - c)
+    near = lax.optimization_barrier(product(jnp.roll(weights, (FIRST_Z - 3) * R, axis=0), texts))
+    cross_weights = jnp.roll(weigh(images, place, far_texts, 1 - c), (FIRST_Z - 3) * R, axis=0)
     image_part = (near + product(cross_weights, far_texts)).astype(bf16)
 
     image_part, far_images = lax.optimization_barrier((image_part, far_images))
@@ -145,7 +148,7 @@
     part = product(weights.T, images).astype(bf16).reshape(NX, half_rows, d)
     ways = (0, 1 + 2 * c, 2, 3 - 2 * c)
     blocks = [rows_at(part, (x + k) & (NX - 1), 1).reshape(half_rows, d) for k in ways]
-    image_parts = exchange(image_part.reshape(NZ, R, d), "z")
+    image_parts = exchange(image_part.reshape(NZ, R, d), "z", 3)
     unit_grad_image = image_parts.astype(f32).sum(axis=0)
 
     opposite = shift(blocks[2], "x", NX, 2)
@@ -154,7 +157,7 @@
     total = total.astype(bf16).reshape(NY, R, d)
     image_grad = tangent(unit_grad_image, image_unit, image_gain)
     total, image_grad = lax.optimization_barrier((total, image_grad))
-    unit_grad_text = exchange(total, "y").astype(f32).sum(axis=0)
+    unit_grad_text = exchange(total, "y", FIRST_Y).astype(f32).sum(axis=0)
 
     return image_grad, tangent(unit_grad_text, text_unit, text_gain)
 

time: 98 us -> 93.2 us (0.951)
  the two profiles are of different devices: /device:TPU:64 before, /device:TPU:1 now
where the time goes in v7:
time: 93.2 us; the launch traced here: 92.4 us
  starting transfers between devices  50.1 us (54%)
  blocking collectives  25.1 us (27%)
  waiting for transfers between devices  5.83 us (6%)
  Pallas kernels  3.33 us (4%)
  matrix products  2.81 us (3%)
  other arithmetic  2.68 us (3%)
  between operations  2.22 us (2%)
    all_to_all x3, starting transfers between devices, exchange(): lax.all_to_all(blocks, axis, split_axis=0, concat_axis=0, axis_index_grou...  34.1 us
    all_gather x1, blocking collectives, shards(): lax.all_gather(exchange(text_send, 'y', FIRST_Y).reshape(half_rows, d), '...  12.6 us
    all_to_all x1, blocking collectives, exchange(): lax.all_to_all(blocks, axis, split_axis=0, concat_axis=0, axis_index_grou...  12.4 us
    ppermute x3, starting transfers between devices, shift(): return lax.ppermute(block, axis, [(i, (i + k) % n) for i in range(n)])  10.2 us
    ppermute x2, starting transfers between devices, cross(): return lax.ppermute(block, ('x', 'core'), moves)  5.82 us
    ppermute x2, waiting for transfers between devices, cross(): return lax.ppermute(block, ('x', 'core'), moves)  5.69 us
    dot_general x6, matrix products, product(): return jnp.dot(a, b, preferred_element_type=f32)  2.81 us
  transfers between devices with their start and end apart: 8, of which 3 were waited for; matrix products, arithmetic and copies ran while one was open for 4% of the time, Pallas kernels for 2%

profile of v7, /device:TPU:1, one launch (start us, length us, event | category | flops | bytes accessed | tf_op | source)
XLA Modules:
  0.0 92.4 jit_solution(4211601772393322490)
XLA Ops:
  0.6 1.6 %shard_map.87 = bf16[8,8,1536]{2,1,0:T(8,128)(2,1)} custom-call(bf16[8,1536]{1,0:T(8,128)(2,1)} %mantissa_ref.1, s32[8]{0:T(128)} %exponent_ref.1), custom_call_target="tpu_custom_call" | custom-call | tf_op jit(solution)/shard_map/pallas_call | solution.py:57
  2.3 9.7 %all-to-all-start.1 = ((bf16[8,8,1536]{2,1,0:T(8,128)(2,1)}), bf16[8,8,1536]{2,1,0:T(8,128)(2,1)S(1)}, u32[]{:S(2)}, u32[]{:S(2)}) async-start(bf16[8,8,1536]{2,1,0:T(8,128)(2,1)} %shard_map.87), calls=%async_computation.1 | async-start | bytes 393216 | tf_op jit(solution)/shard_map/all_to_all | solution.py:82
  11.9 0.7 broadcast_subtract_fusion
  12.6 0.1 sub.44
  12.7 0.1 sub.46
  12.9 0.1 slice_bitcast_fusion.1
  12.9 0.1 pad_add_fusion
  13.0 0.1 pad_add_fusion.1
  14.4 1.7 %shard_map.86 = (bf16[12,8,1536]{2,1,0:T(8,128)(2,1)}, f32[8,1536]{1,0:T(8,128)}, f32[8,1536]{1,0:T(8,128)}, f32[8,1536]{1,0:T(8,128)}, f32[8,1536]{1,0:T(8,128)}, /*index=5*/f32[1,256]{1,0:T(1,128)}, f32[1,256]{1,0:T(1,128)}) custom-call(bf16[8,1536]{1,0:T(8,128)(2,1)} %image_ref, s32[8]{0:T(128)} %image_exponent_ref.1, bf16[8,1536]{1,0:T(8,128)(2,1)} %mantissa_ref.1, ...), custom_call_target="tpu_custom_call" | custom-call | tf_op jit(solution)/shard_map/pallas_call | solution.py:69
  16.1 0.0 all-to-all-done.1
  16.1 0.0 copy-start.5
  16.1 17.1 %all-to-all-start = ((bf16[12,8,1536]{2,1,0:T(8,128)(2,1)}), bf16[12,8,1536]{2,1,0:T(8,128)(2,1)S(1)}, u32[]{:S(2)}, u32[]{:S(2)}) async-start(bf16[12,8,1536]{2,1,0:T(8,128)(2,1)} %get-tuple-element.19), calls=%async_computation | async-start | bytes 589824 | tf_op jit(solution)/shard_map/all_to_all | solution.py:82
  33.2 12.6 %all_gather.3 = bf16[256,1536]{1,0:T(8,128)(2,1)S(1)} all-gather(bf16[64,1536]{1,0:T(8,128)(2,1)S(1)} %bitcast.38), channel_id=1, replica_groups=mesh['y'=8,'z'=12,'x'=4,'core'=2] {'x'}, dimensions={0}, use_global_device_ids=true | all-gather | bytes 983040 | tf_op jit(solution)/shard_map/all_gather | solution.py:126
  45.8 4.2 %collective-permute-start = (bf16[256,1536]{1,0:T(8,128)(2,1)S(1)}, bf16[256,1536]{1,0:T(8,128)(2,1)S(1)}, u32[]{:S(2)}, u32[]{:S(2)}) collective-permute-start(bf16[256,1536]{1,0:T(8,128)(2,1)S(1)} %all_gather.3), channel_id=1, source_target_pairs={{0,1},{1,0},{2,3},{3,2},{4,5},{5,4},{6,7},{7,6},{8,9},{9,8},{10,11... | collective-permute-start | bytes 2359304 | tf_op jit(solution)/shard_map/ppermute | solution.py:86
  50.1 0.0 all-to-all-done
  50.1 0.0 copy-done.4
  50.1 0.0 copy-done.5
  50.1 0.4 fusion.24
  50.5 0.3 fusion.35
  50.8 1.9 %collective-permute-start.1 = (bf16[96,1536]{1,0:T(8,128)(2,1)S(1)}, bf16[96,1536]{1,0:T(8,128)(2,1)S(1)}, u32[]{:S(2)}, u32[]{:S(2)}) collective-permute-start(bf16[96,1536]{1,0:T(8,128)(2,1)S(1)} %bitcast.39), channel_id=1, source_target_pairs={{0,1},{1,0},{2,3},{3,2},{4,5},{5,4},{6,7},{7,6},{8,9},{9,8},{10,11... | collective-permute-start | bytes 884744 | tf_op jit(solution)/shard_map/ppermute | solution.py:86
  52.7 0.0 collective-permute-done
  52.7 0.4 fusion.23
  53.2 1.0 %fusion = bf16[96,1536]{1,0:T(8,128)(2,1)} fusion(f32[96,1536]{1,0:T(8,128)S(1)} %fusion.35, bf16[256,1536]{1,0:T(8,128)(2,1)S(1)} %collective-permute-done, bf16[32,256]{1,0:T(8,128)(2,1)S(1)} %slice.55, bf16[64,256]{1,0:T(8,128)(2,1)S(1)} %slice.54), kind=kOutput, calls=%fused_computation.2 | convolution fusion | flops 75890688 | bytes 1720320 | tf_op jit(solution)/shard_map/dot_general | solution.py:100
  54.1 0.1 collective-permute-done.1
  54.3 7.3 %all-to-all-start.2 = ((bf16[12,8,1536]{2,1,0:T(8,128)(2,1)}), bf16[12,8,1536]{2,1,0:T(8,128)(2,1)S(1)}, u32[]{:S(2)}, u32[]{:S(2)}) async-start(bf16[12,8,1536]{2,1,0:T(8,128)(2,1)} %bitcast.15), calls=%async_computation.2 | async-start | bytes 589824 | tf_op jit(solution)/shard_map/all_to_all | solution.py:82
  61.5 0.4 fusion.22
  61.9 0.4 convolution_convert_fusion
  62.3 0.1 dynamic-slice_bitcast_fusion.2
  62.4 0.0 copy-start.1
  62.4 0.0 copy-start.3
  62.4 4.1 %collective-permute-start.2 = (bf16[64,1536]{1,0:T(8,128)(2,1)S(1)}, bf16[64,1536]{1,0:T(8,128)(2,1)S(1)}, u32[]{:S(2)}, u32[]{:S(2)}) collective-permute-start(bf16[64,1536]{1,0:T(8,128)(2,1)S(1)} %get-tuple-element.30), channel_id=1, source_target_pairs={{0,4},{2,6},{4,0},{6,2},{1,5},{3,7},{5,1},{7,3},{8,12},{10,14},{12... | collective-permute-start | bytes 589832 | tf_op jit(solution)/shard_map/ppermute | solution.py:86
  66.5 3.9 %collective-permute-start.3 = (bf16[64,1536]{1,0:T(8,128)(2,1)S(1)}, bf16[64,1536]{1,0:T(8,128)(2,1)S(1)}, u32[]{:S(2)}, u32[]{:S(2)}) collective-permute-start(bf16[64,1536]{1,0:T(8,128)(2,1)S(1)} %get-tuple-element.32), channel_id=1, source_target_pairs={{0,2},{1,7},{2,4},{3,1},{4,6},{5,3},{6,0},{7,5},{8,10},{9,15},{10,... | collective-permute-start | bytes 589832 | tf_op jit(solution)/shard_map/ppermute | solution.py:91
  70.4 1.9 %collective-permute-start.4 = (bf16[64,1536]{1,0:T(8,128)(2,1)S(1)}, bf16[64,1536]{1,0:T(8,128)(2,1)S(1)}, u32[]{:S(2)}, u32[]{:S(2)}) collective-permute-start(bf16[64,1536]{1,0:T(8,128)(2,1)S(1)} %get-tuple-element.31), channel_id=1, source_target_pairs={{0,6},{1,3},{2,0},{3,5},{4,2},{5,7},{6,4},{7,1},{8,14},{9,11},{10,... | collective-permute-start | bytes 589832 | tf_op jit(solution)/shard_map/ppermute | solution.py:91
  72.4 0.0 collective-permute-done.2
  72.4 3.1 %collective-permute-done.3 = bf16[64,1536]{1,0:T(8,128)(2,1)S(1)} collective-permute-done((bf16[64,1536]{1,0:T(8,128)(2,1)S(1)}, bf16[64,1536]{1,0:T(8,128)(2,1)S(1)}, u32[]{:S(2)}, u32[]{:S(2)}) %collective-permute-start.3) | collective-permute-done | bytes 196640 | tf_op jit(solution)/shard_map/ppermute | solution.py:91
  75.4 2.6 %collective-permute-done.4 = bf16[64,1536]{1,0:T(8,128)(2,1)S(1)} collective-permute-done((bf16[64,1536]{1,0:T(8,128)(2,1)S(1)}, bf16[64,1536]{1,0:T(8,128)(2,1)S(1)}, u32[]{:S(2)}, u32[]{:S(2)}) %collective-permute-start.4) | collective-permute-done | bytes 196640 | tf_op jit(solution)/shard_map/ppermute | solution.py:91
  78.1 0.1 fusion.31
  78.2 0.0 copy-start
  78.2 0.0 copy-start.2
  78.2 0.0 all-to-all-done.2
  78.2 0.0 copy-done.1
  78.2 0.1 multiply_reduce_fusion.1
  78.4 0.0 copy-done.3
  78.4 0.7 subtract_multiply_fusion.1
  79.1 12.4 %all_to_all.20 = bf16[8,8,1536]{2,1,0:T(8,128)(2,1)S(1)} all-to-all(bf16[8,8,1536]{2,1,0:T(8,128)(2,1)S(1)} %fusion.31), channel_id=1, replica_groups={{384,480,576,672,0,96,192,288},{385,481,577,673,1,97,193,289},{386,482,..., dimensions={0} | all-to-all | bytes 393216 | tf_op jit(solution)/shard_map/all_to_all | solution.py:82
  91.6 0.1 multiply_reduce_fusion
  91.7 0.0 copy-done.2
  91.7 0.7 subtract_multiply_fusion
  (13 shorter events, 0.1 us)
Async XLA Ops:
  2.3 13.8 %all-to-all-start.1 = ((bf16[8,8,1536]{2,1,0:T(8,128)(2,1)}), bf16[8,8,1536]{2,1,0:T(8,128)(2,1)S(1)}, u32[]{:S(2)}, u32[]{:S(2)}) async-start(bf16[8,8,1536]{2,1,0:T(8,128)(2,1)} %shard_map.87), calls=%async_computation.1 | async-start | bytes 393216 | tf_op jit(solution)/shard_map/all_to_all | solution.py:82
  16.1 34.0 %copy-start.4 = (f32[1,256]{1,0:T(1,128)S(1)}, f32[1,256]{1,0:T(1,128)}, u32[]{:S(2)}) copy-start(f32[1,256]{1,0:T(1,128)} %get-tuple-element.18) | copy-start | bytes 3076
  16.1 34.0 %copy-start.5 = (f32[1,256]{1,0:T(1,128)S(1)}, f32[1,256]{1,0:T(1,128)}, u32[]{:S(2)}) copy-start(f32[1,256]{1,0:T(1,128)} %get-tuple-element.20) | copy-start | bytes 3076
  16.1 34.0 %all-to-all-start = ((bf16[12,8,1536]{2,1,0:T(8,128)(2,1)}), bf16[12,8,1536]{2,1,0:T(8,128)(2,1)S(1)}, u32[]{:S(2)}, u32[]{:S(2)}) async-start(bf16[12,8,1536]{2,1,0:T(8,128)(2,1)} %get-tuple-element.19), calls=%async_computation | async-start | bytes 589824 | tf_op jit(solution)/shard_map/all_to_all | solution.py:82
  45.8 6.9 %collective-permute-start = (bf16[256,1536]{1,0:T(8,128)(2,1)S(1)}, bf16[256,1536]{1,0:T(8,128)(2,1)S(1)}, u32[]{:S(2)}, u32[]{:S(2)}) collective-permute-start(bf16[256,1536]{1,0:T(8,128)(2,1)S(1)} %all_gather.3), channel_id=1, source_target_pairs={{0,1},{1,0},{2,3},{3,2},{4,5},{5,4},{6,7},{7,6},{8,9},{9,8},{10,11... | collective-permute-start | bytes 2359304 | tf_op jit(solution)/shard_map/ppermute | solution.py:86
  50.8 3.5 %collective-permute-start.1 = (bf16[96,1536]{1,0:T(8,128)(2,1)S(1)}, bf16[96,1536]{1,0:T(8,128)(2,1)S(1)}, u32[]{:S(2)}, u32[]{:S(2)}) collective-permute-start(bf16[96,1536]{1,0:T(8,128)(2,1)S(1)} %bitcast.39), channel_id=1, source_target_pairs={{0,1},{1,0},{2,3},{3,2},{4,5},{5,4},{6,7},{7,6},{8,9},{9,8},{10,11... | collective-permute-start | bytes 884744 | tf_op jit(solution)/shard_map/ppermute | solution.py:86
  54.3 23.9 %all-to-all-start.2 = ((bf16[12,8,1536]{2,1,0:T(8,128)(2,1)}), bf16[12,8,1536]{2,1,0:T(8,128)(2,1)S(1)}, u32[]{:S(2)}, u32[]{:S(2)}) async-start(bf16[12,8,1536]{2,1,0:T(8,128)(2,1)} %bitcast.15), calls=%async_computation.2 | async-start | bytes 589824 | tf_op jit(solution)/shard_map/all_to_all | solution.py:82
  62.4 15.9 %copy-start.1 = (f32[8,1536]{1,0:T(8,128)S(1)}, f32[8,1536]{1,0:T(8,128)}, u32[]{:S(2)}) copy-start(f32[8,1536]{1,0:T(8,128)} %get-tuple-element.24) | copy-start | bytes 147460
  62.4 16.0 %copy-start.3 = (f32[8,1536]{1,0:T(8,128)S(1)}, f32[8,1536]{1,0:T(8,128)}, u32[]{:S(2)}) copy-start(f32[8,1536]{1,0:T(8,128)} %get-tuple-element.25) | copy-start | bytes 147460
  62.4 10.0 %collective-permute-start.2 = (bf16[64,1536]{1,0:T(8,128)(2,1)S(1)}, bf16[64,1536]{1,0:T(8,128)(2,1)S(1)}, u32[]{:S(2)}, u32[]{:S(2)}) collective-permute-start(bf16[64,1536]{1,0:T(8,128)(2,1)S(1)} %get-tuple-element.30), channel_id=1, source_target_pairs={{0,4},{2,6},{4,0},{6,2},{1,5},{3,7},{5,1},{7,3},{8,12},{10,14},{12... | collective-permute-start | bytes 589832 | tf_op jit(solution)/shard_map/ppermute | solution.py:86
  66.5 8.9 %collective-permute-start.3 = (bf16[64,1536]{1,0:T(8,128)(2,1)S(1)}, bf16[64,1536]{1,0:T(8,128)(2,1)S(1)}, u32[]{:S(2)}, u32[]{:S(2)}) collective-permute-start(bf16[64,1536]{1,0:T(8,128)(2,1)S(1)} %get-tuple-element.32), channel_id=1, source_target_pairs={{0,2},{1,7},{2,4},{3,1},{4,6},{5,3},{6,0},{7,5},{8,10},{9,15},{10,... | collective-permute-start | bytes 589832 | tf_op jit(solution)/shard_map/ppermute | solution.py:91
  70.4 7.6 %collective-permute-start.4 = (bf16[64,1536]{1,0:T(8,128)(2,1)S(1)}, bf16[64,1536]{1,0:T(8,128)(2,1)S(1)}, u32[]{:S(2)}, u32[]{:S(2)}) collective-permute-start(bf16[64,1536]{1,0:T(8,128)(2,1)S(1)} %get-tuple-element.31), channel_id=1, source_target_pairs={{0,6},{1,3},{2,0},{3,5},{4,2},{5,7},{6,4},{7,1},{8,14},{9,11},{10,... | collective-permute-start | bytes 589832 | tf_op jit(solution)/shard_map/ppermute | solution.py:91
  78.2 13.4 %copy-start = (f32[8,1536]{1,0:T(8,128)S(1)}, f32[8,1536]{1,0:T(8,128)}, u32[]{:S(2)}) copy-start(f32[8,1536]{1,0:T(8,128)} %get-tuple-element.28) | copy-start | bytes 147460
  78.2 13.5 %copy-start.2 = (f32[8,1536]{1,0:T(8,128)S(1)}, f32[8,1536]{1,0:T(8,128)}, u32[]{:S(2)}) copy-start(f32[8,1536]{1,0:T(8,128)} %get-tuple-element.29) | copy-start | bytes 147460

commit v8 on v7

--- a/solution.py
+++ b/solution.py
@@ -151,12 +151,11 @@
     image_parts = exchange(image_part.reshape(NZ, R, d), "z", 3)
     unit_grad_image = image_parts.astype(f32).sum(axis=0)
 
-    opposite = shift(blocks[2], "x", NX, 2)
-    total = blocks[0].astype(f32) + opposite.astype(f32)
-    total = total + cross(blocks[1], 1).astype(f32) + cross(blocks[3], 3).astype(f32)
+    received = [shift(blocks[2], "x", NX, 2), cross(blocks[1], 1), cross(blocks[3], 3)]
+    image_grad = tangent(unit_grad_image, image_unit, image_gain)
+    total, image_grad = lax.optimization_barrier((blocks[0], image_grad))
+    total = total.astype(f32) + sum(block.astype(f32) for block in received)
     total = total.astype(bf16).reshape(NY, R, d)
-    image_grad = tangent(unit_grad_image, image_unit, image_gain)
-    total, image_grad = lax.optimization_barrier((total, image_grad))
     unit_grad_text = exchange(total, "y", FIRST_Y).astype(f32).sum(axis=0)
 
     return image_grad, tangent(unit_grad_text, text_unit, text_gain)

time: 93.2 us -> 91.2 us (0.979)
  the two profiles are of different devices: /device:TPU:1 before, /device:TPU:6 now
where the time goes in v8:
time: 91.2 us; the launch traced here: 90.2 us
  starting transfers between devices  46.4 us (51%)
  blocking collectives  26.4 us (29%)
  waiting for transfers between devices  5.95 us (7%)
  Pallas kernels  3.33 us (4%)
  matrix products  2.8 us (3%)
  other arithmetic  2.68 us (3%)
  between operations  2.16 us (2%)
    all_to_all x3, starting transfers between devices, exchange(): lax.all_to_all(blocks, axis, split_axis=0, concat_axis=0, axis_index_grou...  32.9 us
    all_gather x1, blocking collectives, shards(): lax.all_gather(exchange(text_send, 'y', FIRST_Y).reshape(half_rows, d), '...  14.3 us
    all_to_all x1, blocking collectives, exchange(): lax.all_to_all(blocks, axis, split_axis=0, concat_axis=0, axis_index_grou...  12.1 us
    ppermute x3, starting transfers between devices, shift(): return lax.ppermute(block, axis, [(i, (i + k) % n) for i in range(n)])  7.69 us
    all_to_all x3, waiting for transfers between devices, exchange(): lax.all_to_all(blocks, axis, split_axis=0, concat_axis=0, axis_index_grou...  5.85 us
    ppermute x2, starting transfers between devices, cross(): return lax.ppermute(block, ('x', 'core'), moves)  5.84 us
    dot_general x6, matrix products, product(): return jnp.dot(a, b, preferred_element_type=f32)  2.8 us
  transfers between devices with their start and end apart: 8, of which 3 were waited for; matrix products, arithmetic and copies ran while one was open for 5% of the time, Pallas kernels for 2%

profile of v8, /device:TPU:6, one launch (start us, length us, event | category | flops | bytes accessed | tf_op | source)
XLA Modules:
  0.0 90.2 jit_solution(5771169312290869195)
XLA Ops:
  0.6 1.6 %shard_map.87 = bf16[8,8,1536]{2,1,0:T(8,128)(2,1)} custom-call(bf16[8,1536]{1,0:T(8,128)(2,1)} %mantissa_ref.1, s32[8]{0:T(128)} %exponent_ref.1), custom_call_target="tpu_custom_call" | custom-call | tf_op jit(solution)/shard_map/pallas_call | solution.py:57
  2.3 9.1 %all-to-all-start.1 = ((bf16[8,8,1536]{2,1,0:T(8,128)(2,1)}), bf16[8,8,1536]{2,1,0:T(8,128)(2,1)S(1)}, u32[]{:S(2)}, u32[]{:S(2)}) async-start(bf16[8,8,1536]{2,1,0:T(8,128)(2,1)} %shard_map.87), calls=%async_computation.1 | async-start | bytes 393216 | tf_op jit(solution)/shard_map/all_to_all | solution.py:82
  11.4 0.7 broadcast_subtract_fusion
  12.1 0.1 sub.44
  12.2 0.1 sub.46
  12.3 0.1 slice_bitcast_fusion.1
  12.4 0.1 pad_add_fusion
  12.5 0.1 pad_add_fusion.1
  13.8 1.7 %shard_map.86 = (bf16[12,8,1536]{2,1,0:T(8,128)(2,1)}, f32[8,1536]{1,0:T(8,128)}, f32[8,1536]{1,0:T(8,128)}, f32[8,1536]{1,0:T(8,128)}, f32[8,1536]{1,0:T(8,128)}, /*index=5*/f32[1,256]{1,0:T(1,128)}, f32[1,256]{1,0:T(1,128)}) custom-call(bf16[8,1536]{1,0:T(8,128)(2,1)} %image_ref, s32[8]{0:T(128)} %image_exponent_ref.1, bf16[8,1536]{1,0:T(8,128)(2,1)} %mantissa_ref.1, ...), custom_call_target="tpu_custom_call" | custom-call | tf_op jit(solution)/shard_map/pallas_call | solution.py:69
  15.5 1.2 %all-to-all-done.1 = bf16[8,8,1536]{2,1,0:T(8,128)(2,1)S(1)} async-done(((bf16[8,8,1536]{2,1,0:T(8,128)(2,1)}), bf16[8,8,1536]{2,1,0:T(8,128)(2,1)S(1)}, u32[]{:S(2)}, u32[]{:S(2)}) %all-to-all-start.1) | async-done | bytes 196640 | tf_op jit(solution)/shard_map/all_to_all | solution.py:82
  16.8 0.0 copy-start.4
  16.8 0.0 copy-start.5
  16.8 16.2 %all-to-all-start = ((bf16[12,8,1536]{2,1,0:T(8,128)(2,1)}), bf16[12,8,1536]{2,1,0:T(8,128)(2,1)S(1)}, u32[]{:S(2)}, u32[]{:S(2)}) async-start(bf16[12,8,1536]{2,1,0:T(8,128)(2,1)} %get-tuple-element.19), calls=%async_computation | async-start | bytes 589824 | tf_op jit(solution)/shard_map/all_to_all | solution.py:82
  33.0 14.3 %all_gather.3 = bf16[256,1536]{1,0:T(8,128)(2,1)S(1)} all-gather(bf16[64,1536]{1,0:T(8,128)(2,1)S(1)} %bitcast.36), channel_id=1, replica_groups=mesh['y'=8,'z'=12,'x'=4,'core'=2] {'x'}, dimensions={0}, use_global_device_ids=true | all-gather | bytes 983040 | tf_op jit(solution)/shard_map/all_gather | solution.py:126
  47.3 1.9 %collective-permute-start = (bf16[256,1536]{1,0:T(8,128)(2,1)S(1)}, bf16[256,1536]{1,0:T(8,128)(2,1)S(1)}, u32[]{:S(2)}, u32[]{:S(2)}) collective-permute-start(bf16[256,1536]{1,0:T(8,128)(2,1)S(1)} %all_gather.3), channel_id=1, source_target_pairs={{0,1},{1,0},{2,3},{3,2},{4,5},{5,4},{6,7},{7,6},{8,9},{9,8},{10,11... | collective-permute-start | bytes 2359304 | tf_op jit(solution)/shard_map/ppermute | solution.py:86
  49.2 0.0 all-to-all-done
  49.2 0.0 copy-done.4
  49.2 0.0 copy-done.5
  49.3 0.4 fusion.24
  49.7 0.3 fusion.32
  49.9 2.4 %collective-permute-start.1 = (bf16[96,1536]{1,0:T(8,128)(2,1)S(1)}, bf16[96,1536]{1,0:T(8,128)(2,1)S(1)}, u32[]{:S(2)}, u32[]{:S(2)}) collective-permute-start(bf16[96,1536]{1,0:T(8,128)(2,1)S(1)} %bitcast.37), channel_id=1, source_target_pairs={{0,1},{1,0},{2,3},{3,2},{4,5},{5,4},{6,7},{7,6},{8,9},{9,8},{10,11... | collective-permute-start | bytes 884744 | tf_op jit(solution)/shard_map/ppermute | solution.py:86
  52.4 0.0 collective-permute-done
  52.4 0.4 fusion.23
  52.8 1.0 %fusion = bf16[96,1536]{1,0:T(8,128)(2,1)} fusion(f32[96,1536]{1,0:T(8,128)S(1)} %fusion.32, bf16[256,1536]{1,0:T(8,128)(2,1)S(1)} %collective-permute-done, bf16[32,256]{1,0:T(8,128)(2,1)S(1)} %slice.55, bf16[64,256]{1,0:T(8,128)(2,1)S(1)} %slice.54), kind=kOutput, calls=%fused_computation.2 | convolution fusion | flops 75890688 | bytes 1720320 | tf_op jit(solution)/shard_map/dot_general | solution.py:100
  53.8 0.0 collective-permute-done.1
  53.8 7.6 %all-to-all-start.2 = ((bf16[12,8,1536]{2,1,0:T(8,128)(2,1)}), bf16[12,8,1536]{2,1,0:T(8,128)(2,1)S(1)}, u32[]{:S(2)}, u32[]{:S(2)}) async-start(bf16[12,8,1536]{2,1,0:T(8,128)(2,1)} %bitcast.11), calls=%async_computation.2 | async-start | bytes 589824 | tf_op jit(solution)/shard_map/all_to_all | solution.py:82
  61.3 0.4 fusion.22
  61.7 0.4 convolution_convert_fusion
  62.1 0.0 copy-start.1
  62.1 0.0 copy-start.3
  62.2 0.1 dynamic-slice_bitcast_fusion.2
  62.2 3.4 %collective-permute-start.2 = (bf16[64,1536]{1,0:T(8,128)(2,1)S(1)}, bf16[64,1536]{1,0:T(8,128)(2,1)S(1)}, u32[]{:S(2)}, u32[]{:S(2)}) collective-permute-start(bf16[64,1536]{1,0:T(8,128)(2,1)S(1)} %get-tuple-element.30), channel_id=1, source_target_pairs={{0,4},{2,6},{4,0},{6,2},{1,5},{3,7},{5,1},{7,3},{8,12},{10,14},{12... | collective-permute-start | bytes 589832 | tf_op jit(solution)/shard_map/ppermute | solution.py:86
  65.6 2.7 %collective-permute-start.3 = (bf16[64,1536]{1,0:T(8,128)(2,1)S(1)}, bf16[64,1536]{1,0:T(8,128)(2,1)S(1)}, u32[]{:S(2)}, u32[]{:S(2)}) collective-permute-start(bf16[64,1536]{1,0:T(8,128)(2,1)S(1)} %get-tuple-element.32), channel_id=1, source_target_pairs={{0,2},{1,7},{2,4},{3,1},{4,6},{5,3},{6,0},{7,5},{8,10},{9,15},{10,... | collective-permute-start | bytes 589832 | tf_op jit(solution)/shard_map/ppermute | solution.py:91
  68.3 3.2 %collective-permute-start.4 = (bf16[64,1536]{1,0:T(8,128)(2,1)S(1)}, bf16[64,1536]{1,0:T(8,128)(2,1)S(1)}, u32[]{:S(2)}, u32[]{:S(2)}) collective-permute-start(bf16[64,1536]{1,0:T(8,128)(2,1)S(1)} %get-tuple-element.31), channel_id=1, source_target_pairs={{0,6},{1,3},{2,0},{3,5},{4,2},{5,7},{6,4},{7,1},{8,14},{9,11},{10,... | collective-permute-start | bytes 589832 | tf_op jit(solution)/shard_map/ppermute | solution.py:91
  71.5 4.6 %all-to-all-done.2 = bf16[12,8,1536]{2,1,0:T(8,128)(2,1)S(1)} async-done(((bf16[12,8,1536]{2,1,0:T(8,128)(2,1)}), bf16[12,8,1536]{2,1,0:T(8,128)(2,1)S(1)}, u32[]{:S(2)}, u32[]{:S(2)}) %all-to-all-start.2) | async-done | bytes 294944 | tf_op jit(solution)/shard_map/all_to_all | solution.py:82
  76.1 0.0 copy-done.1
  76.1 0.1 multiply_reduce_fusion.1
  76.3 0.0 copy-done.3
  76.3 0.7 subtract_multiply_fusion.1
  77.0 0.0 collective-permute-done.2
  77.0 0.0 collective-permute-done.3
  77.0 0.1 collective-permute-done.4
  77.1 0.1 fusion.28
  77.2 12.1 %all_to_all.20 = bf16[8,8,1536]{2,1,0:T(8,128)(2,1)S(1)} all-to-all(bf16[8,8,1536]{2,1,0:T(8,128)(2,1)S(1)} %fusion.28), channel_id=1, replica_groups={{384,480,576,672,0,96,192,288},{385,481,577,673,1,97,193,289},{386,482,..., dimensions={0} | all-to-all | bytes 393216 | tf_op jit(solution)/shard_map/all_to_all | solution.py:82
  89.3 0.0 copy-done
  89.3 0.1 multiply_reduce_fusion
  89.5 0.0 copy-done.2
  89.5 0.7 subtract_multiply_fusion
  (13 shorter events, 0.1 us)
Async XLA Ops:
  2.3 14.5 %all-to-all-start.1 = ((bf16[8,8,1536]{2,1,0:T(8,128)(2,1)}), bf16[8,8,1536]{2,1,0:T(8,128)(2,1)S(1)}, u32[]{:S(2)}, u32[]{:S(2)}) async-start(bf16[8,8,1536]{2,1,0:T(8,128)(2,1)} %shard_map.87), calls=%async_computation.1 | async-start | bytes 393216 | tf_op jit(solution)/shard_map/all_to_all | solution.py:82
  16.8 32.5 %copy-start.4 = (f32[1,256]{1,0:T(1,128)S(1)}, f32[1,256]{1,0:T(1,128)}, u32[]{:S(2)}) copy-start(f32[1,256]{1,0:T(1,128)} %get-tuple-element.18) | copy-start | bytes 3076
  16.8 32.5 %copy-start.5 = (f32[1,256]{1,0:T(1,128)S(1)}, f32[1,256]{1,0:T(1,128)}, u32[]{:S(2)}) copy-start(f32[1,256]{1,0:T(1,128)} %get-tuple-element.20) | copy-start | bytes 3076
  16.8 32.5 %all-to-all-start = ((bf16[12,8,1536]{2,1,0:T(8,128)(2,1)}), bf16[12,8,1536]{2,1,0:T(8,128)(2,1)S(1)}, u32[]{:S(2)}, u32[]{:S(2)}) async-start(bf16[12,8,1536]{2,1,0:T(8,128)(2,1)} %get-tuple-element.19), calls=%async_computation | async-start | bytes 589824 | tf_op jit(solution)/shard_map/all_to_all | solution.py:82
  47.3 5.1 %collective-permute-start = (bf16[256,1536]{1,0:T(8,128)(2,1)S(1)}, bf16[256,1536]{1,0:T(8,128)(2,1)S(1)}, u32[]{:S(2)}, u32[]{:S(2)}) collective-permute-start(bf16[256,1536]{1,0:T(8,128)(2,1)S(1)} %all_gather.3), channel_id=1, source_target_pairs={{0,1},{1,0},{2,3},{3,2},{4,5},{5,4},{6,7},{7,6},{8,9},{9,8},{10,11... | collective-permute-start | bytes 2359304 | tf_op jit(solution)/shard_map/ppermute | solution.py:86
  49.9 3.8 %collective-permute-start.1 = (bf16[96,1536]{1,0:T(8,128)(2,1)S(1)}, bf16[96,1536]{1,0:T(8,128)(2,1)S(1)}, u32[]{:S(2)}, u32[]{:S(2)}) collective-permute-start(bf16[96,1536]{1,0:T(8,128)(2,1)S(1)} %bitcast.37), channel_id=1, source_target_pairs={{0,1},{1,0},{2,3},{3,2},{4,5},{5,4},{6,7},{7,6},{8,9},{9,8},{10,11... | collective-permute-start | bytes 884744 | tf_op jit(solution)/shard_map/ppermute | solution.py:86
  53.8 22.3 %all-to-all-start.2 = ((bf16[12,8,1536]{2,1,0:T(8,128)(2,1)}), bf16[12,8,1536]{2,1,0:T(8,128)(2,1)S(1)}, u32[]{:S(2)}, u32[]{:S(2)}) async-start(bf16[12,8,1536]{2,1,0:T(8,128)(2,1)} %bitcast.11), calls=%async_computation.2 | async-start | bytes 589824 | tf_op jit(solution)/shard_map/all_to_all | solution.py:82
  62.1 14.0 %copy-start.1 = (f32[8,1536]{1,0:T(8,128)S(1)}, f32[8,1536]{1,0:T(8,128)}, u32[]{:S(2)}) copy-start(f32[8,1536]{1,0:T(8,128)} %get-tuple-element.24) | copy-start | bytes 147460
  62.1 14.1 %copy-start.3 = (f32[8,1536]{1,0:T(8,128)S(1)}, f32[8,1536]{1,0:T(8,128)}, u32[]{:S(2)}) copy-start(f32[8,1536]{1,0:T(8,128)} %get-tuple-element.25) | copy-start | bytes 147460
  62.2 14.7 %collective-permute-start.2 = (bf16[64,1536]{1,0:T(8,128)(2,1)S(1)}, bf16[64,1536]{1,0:T(8,128)(2,1)S(1)}, u32[]{:S(2)}, u32[]{:S(2)}) collective-permute-start(bf16[64,1536]{1,0:T(8,128)(2,1)S(1)} %get-tuple-element.30), channel_id=1, source_target_pairs={{0,4},{2,6},{4,0},{6,2},{1,5},{3,7},{5,1},{7,3},{8,12},{10,14},{12... | collective-permute-start | bytes 589832 | tf_op jit(solution)/shard_map/ppermute | solution.py:86
  65.6 11.4 %collective-permute-start.3 = (bf16[64,1536]{1,0:T(8,128)(2,1)S(1)}, bf16[64,1536]{1,0:T(8,128)(2,1)S(1)}, u32[]{:S(2)}, u32[]{:S(2)}) collective-permute-start(bf16[64,1536]{1,0:T(8,128)(2,1)S(1)} %get-tuple-element.32), channel_id=1, source_target_pairs={{0,2},{1,7},{2,4},{3,1},{4,6},{5,3},{6,0},{7,5},{8,10},{9,15},{10,... | collective-permute-start | bytes 589832 | tf_op jit(solution)/shard_map/ppermute | solution.py:91
  68.3 8.8 %collective-permute-start.4 = (bf16[64,1536]{1,0:T(8,128)(2,1)S(1)}, bf16[64,1536]{1,0:T(8,128)(2,1)S(1)}, u32[]{:S(2)}, u32[]{:S(2)}) collective-permute-start(bf16[64,1536]{1,0:T(8,128)(2,1)S(1)} %get-tuple-element.31), channel_id=1, source_target_pairs={{0,6},{1,3},{2,0},{3,5},{4,2},{5,7},{6,4},{7,1},{8,14},{9,11},{10,... | collective-permute-start | bytes 589832 | tf_op jit(solution)/shard_map/ppermute | solution.py:91
  77.0 12.4 %copy-start = (f32[8,1536]{1,0:T(8,128)S(1)}, f32[8,1536]{1,0:T(8,128)}, u32[]{:S(2)}) copy-start(f32[8,1536]{1,0:T(8,128)} %get-tuple-element.28) | copy-start | bytes 147460
  77.0 12.5 %copy-start.2 = (f32[8,1536]{1,0:T(8,128)S(1)}, f32[8,1536]{1,0:T(8,128)}, u32[]{:S(2)}) copy-start(f32[8,1536]{1,0:T(8,128)} %get-tuple-element.29) | copy-start | bytes 147460

commit v9 on v8

--- a/solution.py
+++ b/solution.py
@@ -8,7 +8,7 @@
 epsilon = 1e-06
 AXES = ("y", "z", "x", "core")
 NY, NZ, NX, NC = 8, 12, 4, 2
-FIRST_Y, FIRST_Z = 4, 11
+FIRST_Y, FIRST_Z = 4, 10
 R = 8
 f32 = jnp.float32
 bf16 = jnp.bfloat16
@@ -146,12 +146,13 @@
     weights = jnp.concatenate([weights, far_weights], axis=0)
     images = jnp.concatenate([images, far_images], axis=0)
     part = product(weights.T, images).astype(bf16).reshape(NX, half_rows, d)
-    ways = (0, 1 + 2 * c, 2, 3 - 2 * c)
+    ways = range(NX)
     blocks = [rows_at(part, (x + k) & (NX - 1), 1).reshape(half_rows, d) for k in ways]
     image_parts = exchange(image_part.reshape(NZ, R, d), "z", 3)
     unit_grad_image = image_parts.astype(f32).sum(axis=0)
 
-    received = [shift(blocks[2], "x", NX, 2), cross(blocks[1], 1), cross(blocks[3], 3)]
+    opposite = shift(blocks[2], "x", NX, 2)
+    received = [opposite, shift(blocks[1], "x", NX, 1), shift(blocks[3], "x", NX, 3)]
     image_grad = tangent(unit_grad_image, image_unit, image_gain)
     total, image_grad = lax.optimization_barrier((blocks[0], image_grad))
     total = total.astype(f32) + sum(block.astype(f32) for block in received)

time: 91.2 us -> 90.6 us (level)
    ppermute x3 -> x5, starting transfers between devices: 7.69 us -> 13.5 us  [shift(): return lax.ppermute(block, axis, [(i, (i + k) % n) for i in range(n)])]
    ppermute x2 -> x0, starting transfers between devices: 5.84 us -> none  [cross(): return lax.ppermute(block, ('x', 'core'), moves)]
where the time goes in v9:
time: 90.6 us; the launch traced here: 89.8 us
  starting transfers between devices  46.1 us (51%)
  blocking collectives  25.9 us (29%)
  waiting for transfers between devices  6.41 us (7%)
  Pallas kernels  3.33 us (4%)
  matrix products  2.81 us (3%)
  other arithmetic  2.68 us (3%)
  between operations  2.16 us (2%)
    all_to_all x3, starting transfers between devices, exchange(): lax.all_to_all(blocks, axis, split_axis=0, concat_axis=0, axis_index_grou...  32.6 us
    all_gather x1, blocking collectives, shards(): lax.all_gather(exchange(text_send, 'y', FIRST_Y).reshape(half_rows, d), '...  14.3 us
    ppermute x5, starting transfers between devices, shift(): return lax.ppermute(block, axis, [(i, (i + k) % n) for i in range(n)])  13.5 us
    all_to_all x1, blocking collectives, exchange(): lax.all_to_all(blocks, axis, split_axis=0, concat_axis=0, axis_index_grou...  11.6 us
    all_to_all x3, waiting for transfers between devices, exchange(): lax.all_to_all(blocks, axis, split_axis=0, concat_axis=0, axis_index_grou...  5.84 us
    dot_general x6, matrix products, product(): return jnp.dot(a, b, preferred_element_type=f32)  2.81 us
  transfers between devices with their start and end apart: 8, of which 3 were waited for; matrix products, arithmetic and copies ran while one was open for 5% of the time, Pallas kernels for 2%

profile of v9, /device:TPU:6, one launch (start us, length us, event | category | flops | bytes accessed | tf_op | source)
XLA Modules:
  0.0 89.8 jit_solution(17366416286005461573)
XLA Ops:
  0.6 1.6 %shard_map.87 = bf16[8,8,1536]{2,1,0:T(8,128)(2,1)} custom-call(bf16[8,1536]{1,0:T(8,128)(2,1)} %mantissa_ref.1, s32[8]{0:T(128)} %exponent_ref.1), custom_call_target="tpu_custom_call" | custom-call | tf_op jit(solution)/shard_map/pallas_call | solution.py:57
  2.3 9.1 %all-to-all-start.1 = ((bf16[8,8,1536]{2,1,0:T(8,128)(2,1)}), bf16[8,8,1536]{2,1,0:T(8,128)(2,1)S(1)}, u32[]{:S(2)}, u32[]{:S(2)}) async-start(bf16[8,8,1536]{2,1,0:T(8,128)(2,1)} %shard_map.87), calls=%async_computation.1 | async-start | bytes 393216 | tf_op jit(solution)/shard_map/all_to_all | solution.py:82
  11.4 0.7 broadcast_subtract_fusion
  12.1 0.1 sub.41
  12.2 0.1 sub.43
  12.3 0.1 slice_bitcast_fusion.1
  12.4 0.1 pad_add_fusion
  12.5 0.1 pad_add_fusion.1
  13.8 1.7 %shard_map.86 = (bf16[12,8,1536]{2,1,0:T(8,128)(2,1)}, f32[8,1536]{1,0:T(8,128)}, f32[8,1536]{1,0:T(8,128)}, f32[8,1536]{1,0:T(8,128)}, f32[8,1536]{1,0:T(8,128)}, /*index=5*/f32[1,256]{1,0:T(1,128)}, f32[1,256]{1,0:T(1,128)}) custom-call(bf16[8,1536]{1,0:T(8,128)(2,1)} %image_ref, s32[8]{0:T(128)} %image_exponent_ref.1, bf16[8,1536]{1,0:T(8,128)(2,1)} %mantissa_ref.1, ...), custom_call_target="tpu_custom_call" | custom-call | tf_op jit(solution)/shard_map/pallas_call | solution.py:69
  15.5 1.2 %all-to-all-done.1 = bf16[8,8,1536]{2,1,0:T(8,128)(2,1)S(1)} async-done(((bf16[8,8,1536]{2,1,0:T(8,128)(2,1)}), bf16[8,8,1536]{2,1,0:T(8,128)(2,1)S(1)}, u32[]{:S(2)}, u32[]{:S(2)}) %all-to-all-start.1) | async-done | bytes 196640 | tf_op jit(solution)/shard_map/all_to_all | solution.py:82
  16.8 0.0 copy-start.4
  16.8 0.0 copy-start.5
  16.8 16.2 %all-to-all-start = ((bf16[12,8,1536]{2,1,0:T(8,128)(2,1)}), bf16[12,8,1536]{2,1,0:T(8,128)(2,1)S(1)}, u32[]{:S(2)}, u32[]{:S(2)}) async-start(bf16[12,8,1536]{2,1,0:T(8,128)(2,1)} %get-tuple-element.19), calls=%async_computation | async-start | bytes 589824 | tf_op jit(solution)/shard_map/all_to_all | solution.py:82
  33.0 14.3 %all_gather.3 = bf16[256,1536]{1,0:T(8,128)(2,1)S(1)} all-gather(bf16[64,1536]{1,0:T(8,128)(2,1)S(1)} %bitcast.36), channel_id=1, replica_groups=mesh['y'=8,'z'=12,'x'=4,'core'=2] {'x'}, dimensions={0}, use_global_device_ids=true | all-gather | bytes 983040 | tf_op jit(solution)/shard_map/all_gather | solution.py:126
  47.3 1.9 %collective-permute-start = (bf16[256,1536]{1,0:T(8,128)(2,1)S(1)}, bf16[256,1536]{1,0:T(8,128)(2,1)S(1)}, u32[]{:S(2)}, u32[]{:S(2)}) collective-permute-start(bf16[256,1536]{1,0:T(8,128)(2,1)S(1)} %all_gather.3), channel_id=1, source_target_pairs={{0,1},{1,0},{2,3},{3,2},{4,5},{5,4},{6,7},{7,6},{8,9},{9,8},{10,11... | collective-permute-start | bytes 2359304 | tf_op jit(solution)/shard_map/ppermute | solution.py:86
  49.2 0.0 all-to-all-done
  49.3 0.0 copy-done.4
  49.3 0.0 copy-done.5
  49.3 0.4 fusion.24
  49.7 0.3 fusion.32
  50.0 2.4 %collective-permute-start.1 = (bf16[96,1536]{1,0:T(8,128)(2,1)S(1)}, bf16[96,1536]{1,0:T(8,128)(2,1)S(1)}, u32[]{:S(2)}, u32[]{:S(2)}) collective-permute-start(bf16[96,1536]{1,0:T(8,128)(2,1)S(1)} %bitcast.37), channel_id=1, source_target_pairs={{0,1},{1,0},{2,3},{3,2},{4,5},{5,4},{6,7},{7,6},{8,9},{9,8},{10,11... | collective-permute-start | bytes 884744 | tf_op jit(solution)/shard_map/ppermute | solution.py:86
  52.4 0.0 collective-permute-done
  52.4 0.4 fusion.23
  52.8 1.0 %fusion = bf16[96,1536]{1,0:T(8,128)(2,1)} fusion(f32[96,1536]{1,0:T(8,128)S(1)} %fusion.32, bf16[256,1536]{1,0:T(8,128)(2,1)S(1)} %collective-permute-done, bf16[40,256]{1,0:T(8,128)(2,1)S(1)} %slice.55, bf16[56,256]{1,0:T(8,128)(2,1)S(1)} %slice.54), kind=kOutput, calls=%fused_computation.2 | convolution fusion | flops 75890688 | bytes 1720320 | tf_op jit(solution)/shard_map/dot_general | solution.py:100
  53.8 0.0 collective-permute-done.1
  53.8 7.2 %all-to-all-start.2 = ((bf16[12,8,1536]{2,1,0:T(8,128)(2,1)}), bf16[12,8,1536]{2,1,0:T(8,128)(2,1)S(1)}, u32[]{:S(2)}, u32[]{:S(2)}) async-start(bf16[12,8,1536]{2,1,0:T(8,128)(2,1)} %bitcast.11), calls=%async_computation.2 | async-start | bytes 589824 | tf_op jit(solution)/shard_map/all_to_all | solution.py:82
  61.0 0.4 fusion.22
  61.4 0.4 convolution_convert_fusion
  61.8 0.0 copy-start.1
  61.8 0.0 copy-start.3
  61.9 0.1 dynamic-slice_bitcast_fusion.2
  61.9 3.4 %collective-permute-start.2 = (bf16[64,1536]{1,0:T(8,128)(2,1)S(1)}, bf16[64,1536]{1,0:T(8,128)(2,1)S(1)}, u32[]{:S(2)}, u32[]{:S(2)}) collective-permute-start(bf16[64,1536]{1,0:T(8,128)(2,1)S(1)} %get-tuple-element.30), channel_id=1, source_target_pairs={{0,4},{2,6},{4,0},{6,2},{1,5},{3,7},{5,1},{7,3},{8,12},{10,14},{12... | collective-permute-start | bytes 589832 | tf_op jit(solution)/shard_map/ppermute | solution.py:86
  65.3 2.8 %collective-permute-start.3 = (bf16[64,1536]{1,0:T(8,128)(2,1)S(1)}, bf16[64,1536]{1,0:T(8,128)(2,1)S(1)}, u32[]{:S(2)}, u32[]{:S(2)}) collective-permute-start(bf16[64,1536]{1,0:T(8,128)(2,1)S(1)} %get-tuple-element.32), channel_id=1, source_target_pairs={{0,2},{2,4},{4,6},{6,0},{1,3},{3,5},{5,7},{7,1},{8,10},{10,12},{12... | collective-permute-start | bytes 589832 | tf_op jit(solution)/shard_map/ppermute | solution.py:86
  68.1 3.1 %collective-permute-start.4 = (bf16[64,1536]{1,0:T(8,128)(2,1)S(1)}, bf16[64,1536]{1,0:T(8,128)(2,1)S(1)}, u32[]{:S(2)}, u32[]{:S(2)}) collective-permute-start(bf16[64,1536]{1,0:T(8,128)(2,1)S(1)} %get-tuple-element.31), channel_id=1, source_target_pairs={{0,6},{2,0},{4,2},{6,4},{1,7},{3,1},{5,3},{7,5},{8,14},{10,8},{12,... | collective-permute-start | bytes 589832 | tf_op jit(solution)/shard_map/ppermute | solution.py:86
  71.2 4.6 %all-to-all-done.2 = bf16[12,8,1536]{2,1,0:T(8,128)(2,1)S(1)} async-done(((bf16[12,8,1536]{2,1,0:T(8,128)(2,1)}), bf16[12,8,1536]{2,1,0:T(8,128)(2,1)S(1)}, u32[]{:S(2)}, u32[]{:S(2)}) %all-to-all-start.2) | async-done | bytes 294944 | tf_op jit(solution)/shard_map/all_to_all | solution.py:82
  75.8 0.0 copy-done.1
  75.8 0.1 multiply_reduce_fusion.1
  76.0 0.0 copy-done.3
  76.0 0.7 subtract_multiply_fusion.1
  76.7 0.0 collective-permute-done.2
  76.7 0.0 collective-permute-done.3
  76.7 0.6 collective-permute-done.4
  77.2 0.1 fusion.28
  77.3 11.6 %all_to_all.20 = bf16[8,8,1536]{2,1,0:T(8,128)(2,1)S(1)} all-to-all(bf16[8,8,1536]{2,1,0:T(8,128)(2,1)S(1)} %fusion.28), channel_id=1, replica_groups={{384,480,576,672,0,96,192,288},{385,481,577,673,1,97,193,289},{386,482,..., dimensions={0} | all-to-all | bytes 393216 | tf_op jit(solution)/shard_map/all_to_all | solution.py:82
  88.9 0.0 copy-done
  88.9 0.1 multiply_reduce_fusion
  89.1 0.0 copy-done.2
  89.1 0.7 subtract_multiply_fusion
  (13 shorter events, 0.1 us)
Async XLA Ops:
  2.3 14.5 %all-to-all-start.1 = ((bf16[8,8,1536]{2,1,0:T(8,128)(2,1)}), bf16[8,8,1536]{2,1,0:T(8,128)(2,1)S(1)}, u32[]{:S(2)}, u32[]{:S(2)}) async-start(bf16[8,8,1536]{2,1,0:T(8,128)(2,1)} %shard_map.87), calls=%async_computation.1 | async-start | bytes 393216 | tf_op jit(solution)/shard_map/all_to_all | solution.py:82
  16.8 32.5 %copy-start.4 = (f32[1,256]{1,0:T(1,128)S(1)}, f32[1,256]{1,0:T(1,128)}, u32[]{:S(2)}) copy-start(f32[1,256]{1,0:T(1,128)} %get-tuple-element.18) | copy-start | bytes 3076
  16.8 32.5 %copy-start.5 = (f32[1,256]{1,0:T(1,128)S(1)}, f32[1,256]{1,0:T(1,128)}, u32[]{:S(2)}) copy-start(f32[1,256]{1,0:T(1,128)} %get-tuple-element.20) | copy-start | bytes 3076
  16.8 32.5 %all-to-all-start = ((bf16[12,8,1536]{2,1,0:T(8,128)(2,1)}), bf16[12,8,1536]{2,1,0:T(8,128)(2,1)S(1)}, u32[]{:S(2)}, u32[]{:S(2)}) async-start(bf16[12,8,1536]{2,1,0:T(8,128)(2,1)} %get-tuple-element.19), calls=%async_computation | async-start | bytes 589824 | tf_op jit(solution)/shard_map/all_to_all | solution.py:82
  47.3 5.1 %collective-permute-start = (bf16[256,1536]{1,0:T(8,128)(2,1)S(1)}, bf16[256,1536]{1,0:T(8,128)(2,1)S(1)}, u32[]{:S(2)}, u32[]{:S(2)}) collective-permute-start(bf16[256,1536]{1,0:T(8,128)(2,1)S(1)} %all_gather.3), channel_id=1, source_target_pairs={{0,1},{1,0},{2,3},{3,2},{4,5},{5,4},{6,7},{7,6},{8,9},{9,8},{10,11... | collective-permute-start | bytes 2359304 | tf_op jit(solution)/shard_map/ppermute | solution.py:86
  50.0 3.8 %collective-permute-start.1 = (bf16[96,1536]{1,0:T(8,128)(2,1)S(1)}, bf16[96,1536]{1,0:T(8,128)(2,1)S(1)}, u32[]{:S(2)}, u32[]{:S(2)}) collective-permute-start(bf16[96,1536]{1,0:T(8,128)(2,1)S(1)} %bitcast.37), channel_id=1, source_target_pairs={{0,1},{1,0},{2,3},{3,2},{4,5},{5,4},{6,7},{7,6},{8,9},{9,8},{10,11... | collective-permute-start | bytes 884744 | tf_op jit(solution)/shard_map/ppermute | solution.py:86
  53.8 22.0 %all-to-all-start.2 = ((bf16[12,8,1536]{2,1,0:T(8,128)(2,1)}), bf16[12,8,1536]{2,1,0:T(8,128)(2,1)S(1)}, u32[]{:S(2)}, u32[]{:S(2)}) async-start(bf16[12,8,1536]{2,1,0:T(8,128)(2,1)} %bitcast.11), calls=%async_computation.2 | async-start | bytes 589824 | tf_op jit(solution)/shard_map/all_to_all | solution.py:82
  61.8 14.0 %copy-start.1 = (f32[8,1536]{1,0:T(8,128)S(1)}, f32[8,1536]{1,0:T(8,128)}, u32[]{:S(2)}) copy-start(f32[8,1536]{1,0:T(8,128)} %get-tuple-element.24) | copy-start | bytes 147460
  61.8 14.1 %copy-start.3 = (f32[8,1536]{1,0:T(8,128)S(1)}, f32[8,1536]{1,0:T(8,128)}, u32[]{:S(2)}) copy-start(f32[8,1536]{1,0:T(8,128)} %get-tuple-element.25) | copy-start | bytes 147460
  61.9 14.7 %collective-permute-start.2 = (bf16[64,1536]{1,0:T(8,128)(2,1)S(1)}, bf16[64,1536]{1,0:T(8,128)(2,1)S(1)}, u32[]{:S(2)}, u32[]{:S(2)}) collective-permute-start(bf16[64,1536]{1,0:T(8,128)(2,1)S(1)} %get-tuple-element.30), channel_id=1, source_target_pairs={{0,4},{2,6},{4,0},{6,2},{1,5},{3,7},{5,1},{7,3},{8,12},{10,14},{12... | collective-permute-start | bytes 589832 | tf_op jit(solution)/shard_map/ppermute | solution.py:86
  65.3 11.4 %collective-permute-start.3 = (bf16[64,1536]{1,0:T(8,128)(2,1)S(1)}, bf16[64,1536]{1,0:T(8,128)(2,1)S(1)}, u32[]{:S(2)}, u32[]{:S(2)}) collective-permute-start(bf16[64,1536]{1,0:T(8,128)(2,1)S(1)} %get-tuple-element.32), channel_id=1, source_target_pairs={{0,2},{2,4},{4,6},{6,0},{1,3},{3,5},{5,7},{7,1},{8,10},{10,12},{12... | collective-permute-start | bytes 589832 | tf_op jit(solution)/shard_map/ppermute | solution.py:86
  68.1 9.1 %collective-permute-start.4 = (bf16[64,1536]{1,0:T(8,128)(2,1)S(1)}, bf16[64,1536]{1,0:T(8,128)(2,1)S(1)}, u32[]{:S(2)}, u32[]{:S(2)}) collective-permute-start(bf16[64,1536]{1,0:T(8,128)(2,1)S(1)} %get-tuple-element.31), channel_id=1, source_target_pairs={{0,6},{2,0},{4,2},{6,4},{1,7},{3,1},{5,3},{7,5},{8,14},{10,8},{12,... | collective-permute-start | bytes 589832 | tf_op jit(solution)/shard_map/ppermute | solution.py:86
  76.7 12.3 %copy-start = (f32[8,1536]{1,0:T(8,128)S(1)}, f32[8,1536]{1,0:T(8,128)}, u32[]{:S(2)}) copy-start(f32[8,1536]{1,0:T(8,128)} %get-tuple-element.28) | copy-start | bytes 147460
  76.7 12.4 %copy-start.2 = (f32[8,1536]{1,0:T(8,128)S(1)}, f32[8,1536]{1,0:T(8,128)}, u32[]{:S(2)}) copy-start(f32[8,1536]{1,0:T(8,128)} %get-tuple-element.29) | copy-start | bytes 147460

commit v10 on v9

--- a/solution.py
+++ b/solution.py
@@ -8,7 +8,8 @@
 epsilon = 1e-06
 AXES = ("y", "z", "x", "core")
 NY, NZ, NX, NC = 8, 12, 4, 2
-FIRST_Y, FIRST_Z = 4, 10
+FIRST_Z = 10
+Y_ORDER = [4, 0, 1, 7, 2, 6, 3, 5]
 R = 8
 f32 = jnp.float32
 bf16 = jnp.bfloat16
@@ -76,19 +77,16 @@
     )(image, image_exponent, text, text_exponent, scale, bias)
 
 
-def exchange(blocks, axis, first=0):
-    n = blocks.shape[0]
-    order = [[(first + k) % n for k in range(n)]]
-    return lax.all_to_all(blocks, axis, split_axis=0, concat_axis=0, axis_index_groups=order, tiled=True)
+def ring(n, first):
+    return [(first + k) % n for k in range(n)]
+
+
+def exchange(blocks, axis, order):
+    return lax.all_to_all(blocks, axis, split_axis=0, concat_axis=0, axis_index_groups=[order], tiled=True)
 
 
 def shift(block, axis, n, k):
     return lax.ppermute(block, axis, [(i, (i + k) % n) for i in range(n)])
-
-
-def cross(block, k):
-    moves = [(x * NC + c, (x + (k if c == 0 else -k)) % NX * NC + c) for x in range(NX) for c in range(NC)]
-    return lax.ppermute(block, ("x", "core"), moves)
 
 
 def rows_at(array, start, size):
@@ -123,15 +121,16 @@
     image_send, image_unit, image_gain, text_unit, text_gain, scale, bias = image_prologue(
         image_mantissa, image_exponent, text_mantissa, text_exponent, logit_scale, logit_bias
     )
-    texts = lax.all_gather(exchange(text_send, "y", FIRST_Y).reshape(half_rows, d), "x", axis=0, tiled=True)
+    texts = lax.all_gather(exchange(text_send, "y", Y_ORDER).reshape(half_rows, d), "x", axis=0, tiled=True)
     far_texts = shift(texts, "core", NC, 1)
-    images = exchange(image_send, "z", FIRST_Z).reshape(own, d)
+    images = exchange(image_send, "z", ring(NZ, FIRST_Z)).reshape(own, d)
     far_images = shift(images, "core", NC, 1)
 
     column = jnp.arange(near_rows, dtype=jnp.int32)[None, :]
+    held = jnp.asarray([k * R + r for _ in range(NX) for k in Y_ORDER for r in range(R)], jnp.int32)[None, :]
 
     def weigh(images, place, texts, core):
-        target = (column // half_rows * NC + core) * half_rows + (column + FIRST_Y * R) % half_rows
+        target = (column // half_rows * NC + core) * half_rows + held
         logits = scale * product(images, texts.T) + bias
         label_sign = jnp.where(place[:, None] == target, 1.0, -1.0).astype(f32)
         return (-label_sign * jax.nn.sigmoid(-label_sign * logits)).astype(bf16)
@@ -148,7 +147,7 @@
     part = product(weights.T, images).astype(bf16).reshape(NX, half_rows, d)
     ways = range(NX)
     blocks = [rows_at(part, (x + k) & (NX - 1), 1).reshape(half_rows, d) for k in ways]
-    image_parts = exchange(image_part.reshape(NZ, R, d), "z", 3)
+    image_parts = exchange(image_part.reshape(NZ, R, d), "z", ring(NZ, 3))
     unit_grad_image = image_parts.astype(f32).sum(axis=0)
 
     opposite = shift(blocks[2], "x", NX, 2)
@@ -157,7 +156,7 @@
     total, image_grad = lax.optimization_barrier((blocks[0], image_grad))
     total = total.astype(f32) + sum(block.astype(f32) for block in received)
     total = total.astype(bf16).reshape(NY, R, d)
-    unit_grad_text = exchange(total, "y", FIRST_Y).astype(f32).sum(axis=0)
+    unit_grad_text = exchange(total, "y", Y_ORDER).astype(f32).sum(axis=0)
 
     return image_grad, tangent(unit_grad_text, text_unit, text_gain)
 

time: 90.6 us -> 90.2 us (level)
  no operation moved by 1% of the time
where the time goes in v10:
time: 90.2 us; the launch traced here: 89.3 us
  starting transfers between devices  46.1 us (51%)
  blocking collectives  25.7 us (28%)
  waiting for transfers between devices  6.11 us (7%)
  Pallas kernels  3.31 us (4%)
  matrix products  2.82 us (3%)
  other arithmetic  2.67 us (3%)
  between operations  2.17 us (2%)
    all_to_all x3, starting transfers between devices, exchange(): lax.all_to_all(blocks, axis, split_axis=0, concat_axis=0, axis_index_grou...  32.6 us
    all_gather x1, blocking collectives, shards(): lax.all_gather(exchange(text_send, 'y', Y_ORDER).reshape(half_rows, d), '...  14.3 us
    ppermute x5, starting transfers between devices, shift(): return lax.ppermute(block, axis, [(i, (i + k) % n) for i in range(n)])  13.5 us
    all_to_all x1, blocking collectives, exchange(): lax.all_to_all(blocks, axis, split_axis=0, concat_axis=0, axis_index_grou...  11.4 us
    all_to_all x3, waiting for transfers between devices, exchange(): lax.all_to_all(blocks, axis, split_axis=0, concat_axis=0, axis_index_grou...  5.88 us
    dot_general x6, matrix products, product(): return jnp.dot(a, b, preferred_element_type=f32)  2.82 us
  transfers between devices with their start and end apart: 8, of which 3 were waited for; matrix products, arithmetic and copies ran while one was open for 5% of the time, Pallas kernels for 2%

profile of v10, /device:TPU:6, one launch (start us, length us, event | category | flops | bytes accessed | tf_op | source)
XLA Modules:
  0.0 89.3 jit_solution(17258286654073811740)
XLA Ops:
  0.6 1.6 %shard_map.96 = bf16[8,8,1536]{2,1,0:T(8,128)(2,1)} custom-call(bf16[8,1536]{1,0:T(8,128)(2,1)} %mantissa_ref.1, s32[8]{0:T(128)} %exponent_ref.1), custom_call_target="tpu_custom_call" | custom-call | tf_op jit(solution)/shard_map/pallas_call | solution.py:58
  2.2 9.1 %all-to-all-start.1 = ((bf16[8,8,1536]{2,1,0:T(8,128)(2,1)}), bf16[8,8,1536]{2,1,0:T(8,128)(2,1)S(1)}, u32[]{:S(2)}, u32[]{:S(2)}) async-start(bf16[8,8,1536]{2,1,0:T(8,128)(2,1)} %shard_map.96), calls=%async_computation.1 | async-start | bytes 393216 | tf_op jit(solution)/shard_map/all_to_all | solution.py:85
  11.4 0.7 broadcast_subtract_fusion
  12.0 0.1 sub.41
  12.2 0.1 sub.43
  12.3 0.1 slice_bitcast_fusion.1
  12.3 0.1 pad_add_fusion
  12.4 0.1 pad_add_fusion.1
  13.8 1.7 %shard_map.95 = (bf16[12,8,1536]{2,1,0:T(8,128)(2,1)}, f32[8,1536]{1,0:T(8,128)}, f32[8,1536]{1,0:T(8,128)}, f32[8,1536]{1,0:T(8,128)}, f32[8,1536]{1,0:T(8,128)}, /*index=5*/f32[1,256]{1,0:T(1,128)}, f32[1,256]{1,0:T(1,128)}) custom-call(bf16[8,1536]{1,0:T(8,128)(2,1)} %image_ref, s32[8]{0:T(128)} %image_exponent_ref.1, bf16[8,1536]{1,0:T(8,128)(2,1)} %mantissa_ref.1, ...), custom_call_target="tpu_custom_call" | custom-call | tf_op jit(solution)/shard_map/pallas_call | solution.py:70
  15.5 1.3 %all-to-all-done.1 = bf16[8,8,1536]{2,1,0:T(8,128)(2,1)S(1)} async-done(((bf16[8,8,1536]{2,1,0:T(8,128)(2,1)}), bf16[8,8,1536]{2,1,0:T(8,128)(2,1)S(1)}, u32[]{:S(2)}, u32[]{:S(2)}) %all-to-all-start.1) | async-done | bytes 196640 | tf_op jit(solution)/shard_map/all_to_all | solution.py:85
  16.8 0.0 copy-start.4
  16.8 16.2 %all-to-all-start = ((bf16[12,8,1536]{2,1,0:T(8,128)(2,1)}), bf16[12,8,1536]{2,1,0:T(8,128)(2,1)S(1)}, u32[]{:S(2)}, u32[]{:S(2)}) async-start(bf16[12,8,1536]{2,1,0:T(8,128)(2,1)} %get-tuple-element.19), calls=%async_computation | async-start | bytes 589824 | tf_op jit(solution)/shard_map/all_to_all | solution.py:85
  33.0 14.3 %all_gather.3 = bf16[256,1536]{1,0:T(8,128)(2,1)S(1)} all-gather(bf16[64,1536]{1,0:T(8,128)(2,1)S(1)} %bitcast.36), channel_id=1, replica_groups=mesh['y'=8,'z'=12,'x'=4,'core'=2] {'x'}, dimensions={0}, use_global_device_ids=true | all-gather | bytes 983040 | tf_op jit(solution)/shard_map/all_gather | solution.py:124
  47.3 1.9 %collective-permute-start = (bf16[256,1536]{1,0:T(8,128)(2,1)S(1)}, bf16[256,1536]{1,0:T(8,128)(2,1)S(1)}, u32[]{:S(2)}, u32[]{:S(2)}) collective-permute-start(bf16[256,1536]{1,0:T(8,128)(2,1)S(1)} %all_gather.3), channel_id=1, source_target_pairs={{0,1},{1,0},{2,3},{3,2},{4,5},{5,4},{6,7},{7,6},{8,9},{9,8},{10,11... | collective-permute-start | bytes 2359304 | tf_op jit(solution)/shard_map/ppermute | solution.py:89
  49.2 0.0 copy-done.4
  49.3 0.0 all-to-all-done
  49.3 0.0 copy-done.5
  49.3 0.0 copy-done.6
  49.3 0.4 fusion.24
  49.7 0.3 fusion.32
  50.0 2.4 %collective-permute-start.1 = (bf16[96,1536]{1,0:T(8,128)(2,1)S(1)}, bf16[96,1536]{1,0:T(8,128)(2,1)S(1)}, u32[]{:S(2)}, u32[]{:S(2)}) collective-permute-start(bf16[96,1536]{1,0:T(8,128)(2,1)S(1)} %bitcast.37), channel_id=1, source_target_pairs={{0,1},{1,0},{2,3},{3,2},{4,5},{5,4},{6,7},{7,6},{8,9},{9,8},{10,11... | collective-permute-start | bytes 884744 | tf_op jit(solution)/shard_map/ppermute | solution.py:89
  52.4 0.0 collective-permute-done
  52.4 0.4 fusion.23
  52.8 1.0 %fusion = bf16[96,1536]{1,0:T(8,128)(2,1)} fusion(f32[96,1536]{1,0:T(8,128)S(1)} %fusion.32, bf16[256,1536]{1,0:T(8,128)(2,1)S(1)} %collective-permute-done, bf16[40,256]{1,0:T(8,128)(2,1)S(1)} %slice.55, bf16[56,256]{1,0:T(8,128)(2,1)S(1)} %slice.54), kind=kOutput, calls=%fused_computation.2 | convolution fusion | flops 75890688 | bytes 1720320 | tf_op jit(solution)/shard_map/dot_general | solution.py:98
  53.8 0.0 collective-permute-done.1
  53.8 7.2 %all-to-all-start.2 = ((bf16[12,8,1536]{2,1,0:T(8,128)(2,1)}), bf16[12,8,1536]{2,1,0:T(8,128)(2,1)S(1)}, u32[]{:S(2)}, u32[]{:S(2)}) async-start(bf16[12,8,1536]{2,1,0:T(8,128)(2,1)} %bitcast.11), calls=%async_computation.2 | async-start | bytes 589824 | tf_op jit(solution)/shard_map/all_to_all | solution.py:85
  61.1 0.4 fusion.22
  61.5 0.4 convolution_convert_fusion
  61.9 0.0 copy-start.1
  61.9 0.0 copy-start.3
  61.9 0.1 dynamic-slice_bitcast_fusion.2
  62.0 3.4 %collective-permute-start.2 = (bf16[64,1536]{1,0:T(8,128)(2,1)S(1)}, bf16[64,1536]{1,0:T(8,128)(2,1)S(1)}, u32[]{:S(2)}, u32[]{:S(2)}) collective-permute-start(bf16[64,1536]{1,0:T(8,128)(2,1)S(1)} %get-tuple-element.30), channel_id=1, source_target_pairs={{0,4},{2,6},{4,0},{6,2},{1,5},{3,7},{5,1},{7,3},{8,12},{10,14},{12... | collective-permute-start | bytes 589832 | tf_op jit(solution)/shard_map/ppermute | solution.py:89
  65.3 2.4 %collective-permute-start.3 = (bf16[64,1536]{1,0:T(8,128)(2,1)S(1)}, bf16[64,1536]{1,0:T(8,128)(2,1)S(1)}, u32[]{:S(2)}, u32[]{:S(2)}) collective-permute-start(bf16[64,1536]{1,0:T(8,128)(2,1)S(1)} %get-tuple-element.32), channel_id=1, source_target_pairs={{0,2},{2,4},{4,6},{6,0},{1,3},{3,5},{5,7},{7,1},{8,10},{10,12},{12... | collective-permute-start | bytes 589832 | tf_op jit(solution)/shard_map/ppermute | solution.py:89
  67.8 3.4 %collective-permute-start.4 = (bf16[64,1536]{1,0:T(8,128)(2,1)S(1)}, bf16[64,1536]{1,0:T(8,128)(2,1)S(1)}, u32[]{:S(2)}, u32[]{:S(2)}) collective-permute-start(bf16[64,1536]{1,0:T(8,128)(2,1)S(1)} %get-tuple-element.31), channel_id=1, source_target_pairs={{0,6},{2,0},{4,2},{6,4},{1,7},{3,1},{5,3},{7,5},{8,14},{10,8},{12,... | collective-permute-start | bytes 589832 | tf_op jit(solution)/shard_map/ppermute | solution.py:89
  71.2 4.6 %all-to-all-done.2 = bf16[12,8,1536]{2,1,0:T(8,128)(2,1)S(1)} async-done(((bf16[12,8,1536]{2,1,0:T(8,128)(2,1)}), bf16[12,8,1536]{2,1,0:T(8,128)(2,1)S(1)}, u32[]{:S(2)}, u32[]{:S(2)}) %all-to-all-start.2) | async-done | bytes 294944 | tf_op jit(solution)/shard_map/all_to_all | solution.py:85
  75.8 0.0 copy-done.1
  75.9 0.1 multiply_reduce_fusion.1
  76.0 0.0 copy-done.3
  76.0 0.7 subtract_multiply_fusion.1
  76.7 0.0 collective-permute-done.2
  76.7 0.0 collective-permute-done.3
  76.7 0.2 collective-permute-done.4
  76.9 0.1 fusion.28
  77.0 11.4 %all_to_all.20 = bf16[8,8,1536]{2,1,0:T(8,128)(2,1)S(1)} all-to-all(bf16[8,8,1536]{2,1,0:T(8,128)(2,1)S(1)} %fusion.28), channel_id=1, replica_groups={{384,0,96,672,192,576,288,480},{385,1,97,673,193,577,289,481},{386,2,98..., dimensions={0} | all-to-all | bytes 393216 | tf_op jit(solution)/shard_map/all_to_all | solution.py:85
  88.5 0.0 copy-done
  88.5 0.1 multiply_reduce_fusion
  88.6 0.0 copy-done.2
  88.6 0.7 subtract_multiply_fusion
  (14 shorter events, 0.1 us)
Async XLA Ops:
  2.2 14.5 %all-to-all-start.1 = ((bf16[8,8,1536]{2,1,0:T(8,128)(2,1)}), bf16[8,8,1536]{2,1,0:T(8,128)(2,1)S(1)}, u32[]{:S(2)}, u32[]{:S(2)}) async-start(bf16[8,8,1536]{2,1,0:T(8,128)(2,1)} %shard_map.96), calls=%async_computation.1 | async-start | bytes 393216 | tf_op jit(solution)/shard_map/all_to_all | solution.py:85
  16.8 32.5 %copy-start.4 = (s32[256]{0:T(256)S(1)}, s32[256]{0:T(256)}, u32[]{:S(2)}) copy-start(s32[256]{0:T(256)} %constant.54.clone) | copy-start | bytes 3076
  16.8 32.5 %copy-start.5 = (f32[1,256]{1,0:T(1,128)S(1)}, f32[1,256]{1,0:T(1,128)}, u32[]{:S(2)}) copy-start(f32[1,256]{1,0:T(1,128)} %get-tuple-element.18) | copy-start | bytes 3076
  16.8 32.5 %copy-start.6 = (f32[1,256]{1,0:T(1,128)S(1)}, f32[1,256]{1,0:T(1,128)}, u32[]{:S(2)}) copy-start(f32[1,256]{1,0:T(1,128)} %get-tuple-element.20) | copy-start | bytes 3076
  16.8 32.5 %all-to-all-start = ((bf16[12,8,1536]{2,1,0:T(8,128)(2,1)}), bf16[12,8,1536]{2,1,0:T(8,128)(2,1)S(1)}, u32[]{:S(2)}, u32[]{:S(2)}) async-start(bf16[12,8,1536]{2,1,0:T(8,128)(2,1)} %get-tuple-element.19), calls=%async_computation | async-start | bytes 589824 | tf_op jit(solution)/shard_map/all_to_all | solution.py:85
  47.3 5.1 %collective-permute-start = (bf16[256,1536]{1,0:T(8,128)(2,1)S(1)}, bf16[256,1536]{1,0:T(8,128)(2,1)S(1)}, u32[]{:S(2)}, u32[]{:S(2)}) collective-permute-start(bf16[256,1536]{1,0:T(8,128)(2,1)S(1)} %all_gather.3), channel_id=1, source_target_pairs={{0,1},{1,0},{2,3},{3,2},{4,5},{5,4},{6,7},{7,6},{8,9},{9,8},{10,11... | collective-permute-start | bytes 2359304 | tf_op jit(solution)/shard_map/ppermute | solution.py:89
  50.0 3.8 %collective-permute-start.1 = (bf16[96,1536]{1,0:T(8,128)(2,1)S(1)}, bf16[96,1536]{1,0:T(8,128)(2,1)S(1)}, u32[]{:S(2)}, u32[]{:S(2)}) collective-permute-start(bf16[96,1536]{1,0:T(8,128)(2,1)S(1)} %bitcast.37), channel_id=1, source_target_pairs={{0,1},{1,0},{2,3},{3,2},{4,5},{5,4},{6,7},{7,6},{8,9},{9,8},{10,11... | collective-permute-start | bytes 884744 | tf_op jit(solution)/shard_map/ppermute | solution.py:89
  53.8 22.0 %all-to-all-start.2 = ((bf16[12,8,1536]{2,1,0:T(8,128)(2,1)}), bf16[12,8,1536]{2,1,0:T(8,128)(2,1)S(1)}, u32[]{:S(2)}, u32[]{:S(2)}) async-start(bf16[12,8,1536]{2,1,0:T(8,128)(2,1)} %bitcast.11), calls=%async_computation.2 | async-start | bytes 589824 | tf_op jit(solution)/shard_map/all_to_all | solution.py:85
  61.9 14.0 %copy-start.1 = (f32[8,1536]{1,0:T(8,128)S(1)}, f32[8,1536]{1,0:T(8,128)}, u32[]{:S(2)}) copy-start(f32[8,1536]{1,0:T(8,128)} %get-tuple-element.24) | copy-start | bytes 147460
  61.9 14.1 %copy-start.3 = (f32[8,1536]{1,0:T(8,128)S(1)}, f32[8,1536]{1,0:T(8,128)}, u32[]{:S(2)}) copy-start(f32[8,1536]{1,0:T(8,128)} %get-tuple-element.25) | copy-start | bytes 147460
  62.0 14.7 %collective-permute-start.2 = (bf16[64,1536]{1,0:T(8,128)(2,1)S(1)}, bf16[64,1536]{1,0:T(8,128)(2,1)S(1)}, u32[]{:S(2)}, u32[]{:S(2)}) collective-permute-start(bf16[64,1536]{1,0:T(8,128)(2,1)S(1)} %get-tuple-element.30), channel_id=1, source_target_pairs={{0,4},{2,6},{4,0},{6,2},{1,5},{3,7},{5,1},{7,3},{8,12},{10,14},{12... | collective-permute-start | bytes 589832 | tf_op jit(solution)/shard_map/ppermute | solution.py:89
  65.3 11.4 %collective-permute-start.3 = (bf16[64,1536]{1,0:T(8,128)(2,1)S(1)}, bf16[64,1536]{1,0:T(8,128)(2,1)S(1)}, u32[]{:S(2)}, u32[]{:S(2)}) collective-permute-start(bf16[64,1536]{1,0:T(8,128)(2,1)S(1)} %get-tuple-element.32), channel_id=1, source_target_pairs={{0,2},{2,4},{4,6},{6,0},{1,3},{3,5},{5,7},{7,1},{8,10},{10,12},{12... | collective-permute-start | bytes 589832 | tf_op jit(solution)/shard_map/ppermute | solution.py:89
  67.8 9.2 %collective-permute-start.4 = (bf16[64,1536]{1,0:T(8,128)(2,1)S(1)}, bf16[64,1536]{1,0:T(8,128)(2,1)S(1)}, u32[]{:S(2)}, u32[]{:S(2)}) collective-permute-start(bf16[64,1536]{1,0:T(8,128)(2,1)S(1)} %get-tuple-element.31), channel_id=1, source_target_pairs={{0,6},{2,0},{4,2},{6,4},{1,7},{3,1},{5,3},{7,5},{8,14},{10,8},{12,... | collective-permute-start | bytes 589832 | tf_op jit(solution)/shard_map/ppermute | solution.py:89
  76.7 11.8 %copy-start = (f32[8,1536]{1,0:T(8,128)S(1)}, f32[8,1536]{1,0:T(8,128)}, u32[]{:S(2)}) copy-start(f32[8,1536]{1,0:T(8,128)} %get-tuple-element.28) | copy-start | bytes 147460
  76.7 11.9 %copy-start.2 = (f32[8,1536]{1,0:T(8,128)S(1)}, f32[8,1536]{1,0:T(8,128)}, u32[]{:S(2)}) copy-start(f32[8,1536]{1,0:T(8,128)} %get-tuple-element.29) | copy-start | bytes 147460

commit v11 on v10

--- a/solution.py
+++ b/solution.py
@@ -8,7 +8,9 @@
 epsilon = 1e-06
 AXES = ("y", "z", "x", "core")
 NY, NZ, NX, NC = 8, 12, 4, 2
-FIRST_Z = 10
+Z_RETURN = [3, 9, 8, 10, 7, 11, 0, 6, 1, 5, 2, 4]
+TURN = Z_RETURN.index(10)
+Z_ORDER = Z_RETURN[TURN:] + Z_RETURN[:TURN]
 Y_ORDER = [4, 0, 1, 7, 2, 6, 3, 5]
 R = 8
 f32 = jnp.float32
@@ -77,8 +79,8 @@
     )(image, image_exponent, text, text_exponent, scale, bias)
 
 
-def ring(n, first):
-    return [(first + k) % n for k in range(n)]
+def by_order(place):
+    return jnp.concatenate([place[k * R : (k + 1) * R] for k in Z_ORDER])
 
 
 def exchange(blocks, axis, order):
@@ -113,8 +115,8 @@
 
     place = positive.reshape(NZ, NX * NC, R).transpose(1, 0, 2).reshape(NX * NC, own)
     place = place - z * (NX * NC * half_rows)
-    far_place = jnp.roll(rows_at(place, x * NC + 1 - c, 1).reshape(own), -FIRST_Z * R)
-    place = jnp.roll(rows_at(place, x * NC + c, 1).reshape(own), -FIRST_Z * R)
+    far_place = by_order(rows_at(place, x * NC + 1 - c, 1).reshape(own))
+    place = by_order(rows_at(place, x * NC + c, 1).reshape(own))
 
     text_send = text_prologue(text_mantissa, text_exponent)
     image_mantissa, place, far_place = lax.optimization_barrier((image_mantissa, place, far_place))
@@ -123,7 +125,7 @@
     )
     texts = lax.all_gather(exchange(text_send, "y", Y_ORDER).reshape(half_rows, d), "x", axis=0, tiled=True)
     far_texts = shift(texts, "core", NC, 1)
-    images = exchange(image_send, "z", ring(NZ, FIRST_Z)).reshape(own, d)
+    images = exchange(image_send, "z", Z_ORDER).reshape(own, d)
     far_images = shift(images, "core", NC, 1)
 
     column = jnp.arange(near_rows, dtype=jnp.int32)[None, :]
@@ -136,8 +138,8 @@
         return (-label_sign * jax.nn.sigmoid(-label_sign * logits)).astype(bf16)
 
     weights = weigh(images, place, texts, c)
-    near = lax.optimization_barrier(product(jnp.roll(weights, (FIRST_Z - 3) * R, axis=0), texts))
-    cross_weights = jnp.roll(weigh(images, place, far_texts, 1 - c), (FIRST_Z - 3) * R, axis=0)
+    near = lax.optimization_barrier(product(jnp.roll(weights, TURN * R, axis=0), texts))
+    cross_weights = jnp.roll(weigh(images, place, far_texts, 1 - c), TURN * R, axis=0)
     image_part = (near + product(cross_weights, far_texts)).astype(bf16)
 
     image_part, far_images = lax.optimization_barrier((image_part, far_images))
@@ -147,7 +149,7 @@
     part = product(weights.T, images).astype(bf16).reshape(NX, half_rows, d)
     ways = range(NX)
     blocks = [rows_at(part, (x + k) & (NX - 1), 1).reshape(half_rows, d) for k in ways]
-    image_parts = exchange(image_part.reshape(NZ, R, d), "z", ring(NZ, 3))
+    image_parts = exchange(image_part.reshape(NZ, R, d), "z", Z_RETURN)
     unit_grad_image = image_parts.astype(f32).sum(axis=0)
 
     opposite = shift(blocks[2], "x", NX, 2)

time: 90.2 us -> 90.7 us (level)
  transfers between devices with their start and end apart: 8 -> 8, of which waited for: 3 -> 2; matrix products, arithmetic and copies ran while one was open for 5% -> 6% of each run, Pallas kernels for 2% -> 2%
where the time goes in v11:
time: 90.7 us; the launch traced here: 89.5 us
  starting transfers between devices  46.4 us (51%)
  blocking collectives  25.7 us (28%)
  waiting for transfers between devices  5.95 us (7%)
  Pallas kernels  3.31 us (4%)
  matrix products  2.83 us (3%)
  other arithmetic  2.52 us (3%)
  between operations  2.19 us (2%)
    all_to_all x3, starting transfers between devices, exchange(): lax.all_to_all(blocks, axis, split_axis=0, concat_axis=0, axis_index_grou...  32.8 us
    all_gather x1, blocking collectives, shards(): lax.all_gather(exchange(text_send, 'y', Y_ORDER).reshape(half_rows, d), '...  14.1 us
    ppermute x5, starting transfers between devices, shift(): return lax.ppermute(block, axis, [(i, (i + k) % n) for i in range(n)])  13.5 us
    all_to_all x1, blocking collectives, exchange(): lax.all_to_all(blocks, axis, split_axis=0, concat_axis=0, axis_index_grou...  11.6 us
    all_to_all x3, waiting for transfers between devices, exchange(): lax.all_to_all(blocks, axis, split_axis=0, concat_axis=0, axis_index_grou...  5.93 us
    dot_general x6, matrix products, product(): return jnp.dot(a, b, preferred_element_type=f32)  2.83 us
  transfers between devices with their start and end apart: 8, of which 2 were waited for; matrix products, arithmetic and copies ran while one was open for 6% of the time, Pallas kernels for 2%

profile of v11, /device:TPU:6, one launch (start us, length us, event | category | flops | bytes accessed | tf_op | source)
XLA Modules:
  0.0 89.5 jit_solution(7426508239094830788)
XLA Ops:
  0.6 1.6 %shard_map.96 = bf16[8,8,1536]{2,1,0:T(8,128)(2,1)} custom-call(bf16[8,1536]{1,0:T(8,128)(2,1)} %mantissa_ref.1, s32[8]{0:T(128)} %exponent_ref.1), custom_call_target="tpu_custom_call" | custom-call | tf_op jit(solution)/shard_map/pallas_call | solution.py:60
  2.2 9.1 %all-to-all-start.1 = ((bf16[8,8,1536]{2,1,0:T(8,128)(2,1)}), bf16[8,8,1536]{2,1,0:T(8,128)(2,1)S(1)}, u32[]{:S(2)}, u32[]{:S(2)}) async-start(bf16[8,8,1536]{2,1,0:T(8,128)(2,1)} %shard_map.96), calls=%async_computation.1 | async-start | bytes 393216 | tf_op jit(solution)/shard_map/all_to_all | solution.py:87
  11.4 0.7 broadcast_subtract_fusion
  12.0 0.1 sub.41
  12.2 0.1 sub.43
  12.3 0.1 slice_bitcast_fusion
  12.3 0.1 concatenate.20
  12.4 0.1 slice_bitcast_fusion.12
  12.5 0.1 concatenate.19
  13.9 1.7 %shard_map.95 = (bf16[12,8,1536]{2,1,0:T(8,128)(2,1)}, f32[8,1536]{1,0:T(8,128)}, f32[8,1536]{1,0:T(8,128)}, f32[8,1536]{1,0:T(8,128)}, f32[8,1536]{1,0:T(8,128)}, /*index=5*/f32[1,256]{1,0:T(1,128)}, f32[1,256]{1,0:T(1,128)}) custom-call(bf16[8,1536]{1,0:T(8,128)(2,1)} %image_ref, s32[8]{0:T(128)} %image_exponent_ref.1, bf16[8,1536]{1,0:T(8,128)(2,1)} %mantissa_ref.1, ...), custom_call_target="tpu_custom_call" | custom-call | tf_op jit(solution)/shard_map/pallas_call | solution.py:72
  15.6 1.2 %all-to-all-done.1 = bf16[8,8,1536]{2,1,0:T(8,128)(2,1)S(1)} async-done(((bf16[8,8,1536]{2,1,0:T(8,128)(2,1)}), bf16[8,8,1536]{2,1,0:T(8,128)(2,1)S(1)}, u32[]{:S(2)}, u32[]{:S(2)}) %all-to-all-start.1) | async-done | bytes 196640 | tf_op jit(solution)/shard_map/all_to_all | solution.py:87
  16.8 16.2 %all-to-all-start = ((bf16[12,8,1536]{2,1,0:T(8,128)(2,1)}), bf16[12,8,1536]{2,1,0:T(8,128)(2,1)S(1)}, u32[]{:S(2)}, u32[]{:S(2)}) async-start(bf16[12,8,1536]{2,1,0:T(8,128)(2,1)} %get-tuple-element.19), calls=%async_computation | async-start | bytes 589824 | tf_op jit(solution)/shard_map/all_to_all | solution.py:87
  33.0 14.1 %all_gather.3 = bf16[256,1536]{1,0:T(8,128)(2,1)S(1)} all-gather(bf16[64,1536]{1,0:T(8,128)(2,1)S(1)} %bitcast.76), channel_id=1, replica_groups=mesh['y'=8,'z'=12,'x'=4,'core'=2] {'x'}, dimensions={0}, use_global_device_ids=true | all-gather | bytes 983040 | tf_op jit(solution)/shard_map/all_gather | solution.py:126
  47.1 1.9 %collective-permute-start = (bf16[256,1536]{1,0:T(8,128)(2,1)S(1)}, bf16[256,1536]{1,0:T(8,128)(2,1)S(1)}, u32[]{:S(2)}, u32[]{:S(2)}) collective-permute-start(bf16[256,1536]{1,0:T(8,128)(2,1)S(1)} %all_gather.3), channel_id=1, source_target_pairs={{0,1},{1,0},{2,3},{3,2},{4,5},{5,4},{6,7},{7,6},{8,9},{9,8},{10,11... | collective-permute-start | bytes 2359304 | tf_op jit(solution)/shard_map/ppermute | solution.py:91
  49.0 0.0 copy-done.4
  49.0 0.0 all-to-all-done
  49.0 0.0 copy-done.5
  49.0 0.0 copy-done.6
  49.0 0.4 fusion.24
  49.5 0.3 fusion.32
  49.7 2.4 %collective-permute-start.1 = (bf16[96,1536]{1,0:T(8,128)(2,1)S(1)}, bf16[96,1536]{1,0:T(8,128)(2,1)S(1)}, u32[]{:S(2)}, u32[]{:S(2)}) collective-permute-start(bf16[96,1536]{1,0:T(8,128)(2,1)S(1)} %bitcast.77), channel_id=1, source_target_pairs={{0,1},{1,0},{2,3},{3,2},{4,5},{5,4},{6,7},{7,6},{8,9},{9,8},{10,11... | collective-permute-start | bytes 884744 | tf_op jit(solution)/shard_map/ppermute | solution.py:91
  52.1 0.0 collective-permute-done
  52.1 0.4 fusion.23
  52.6 1.0 %fusion = bf16[96,1536]{1,0:T(8,128)(2,1)} fusion(f32[96,1536]{1,0:T(8,128)S(1)} %fusion.32, bf16[256,1536]{1,0:T(8,128)(2,1)S(1)} %collective-permute-done, bf16[72,256]{1,0:T(8,128)(2,1)S(1)} %slice.213, bf16[24,256]{1,0:T(8,128)(2,1)S(1)} %slice.212), kind=kOutput, calls=%fused_computation.2 | convolution fusion | flops 75890688 | bytes 1720320 | tf_op jit(solution)/shard_map/dot_general | solution.py:100
  53.6 0.0 collective-permute-done.1
  53.6 7.5 %all-to-all-start.2 = ((bf16[12,8,1536]{2,1,0:T(8,128)(2,1)}), bf16[12,8,1536]{2,1,0:T(8,128)(2,1)S(1)}, u32[]{:S(2)}, u32[]{:S(2)}) async-start(bf16[12,8,1536]{2,1,0:T(8,128)(2,1)} %bitcast.31), calls=%async_computation.2 | async-start | bytes 589824 | tf_op jit(solution)/shard_map/all_to_all | solution.py:87
  61.1 0.4 fusion.22
  61.5 0.4 convolution_convert_fusion
  61.9 0.0 copy-start.1
  61.9 0.0 copy-start.3
  61.9 0.1 dynamic-slice_bitcast_fusion.2
  62.0 3.4 %collective-permute-start.2 = (bf16[64,1536]{1,0:T(8,128)(2,1)S(1)}, bf16[64,1536]{1,0:T(8,128)(2,1)S(1)}, u32[]{:S(2)}, u32[]{:S(2)}) collective-permute-start(bf16[64,1536]{1,0:T(8,128)(2,1)S(1)} %get-tuple-element.30), channel_id=1, source_target_pairs={{0,4},{2,6},{4,0},{6,2},{1,5},{3,7},{5,1},{7,3},{8,12},{10,14},{12... | collective-permute-start | bytes 589832 | tf_op jit(solution)/shard_map/ppermute | solution.py:91
  65.4 1.9 %collective-permute-start.3 = (bf16[64,1536]{1,0:T(8,128)(2,1)S(1)}, bf16[64,1536]{1,0:T(8,128)(2,1)S(1)}, u32[]{:S(2)}, u32[]{:S(2)}) collective-permute-start(bf16[64,1536]{1,0:T(8,128)(2,1)S(1)} %get-tuple-element.32), channel_id=1, source_target_pairs={{0,2},{2,4},{4,6},{6,0},{1,3},{3,5},{5,7},{7,1},{8,10},{10,12},{12... | collective-permute-start | bytes 589832 | tf_op jit(solution)/shard_map/ppermute | solution.py:91
  67.3 3.9 %collective-permute-start.4 = (bf16[64,1536]{1,0:T(8,128)(2,1)S(1)}, bf16[64,1536]{1,0:T(8,128)(2,1)S(1)}, u32[]{:S(2)}, u32[]{:S(2)}) collective-permute-start(bf16[64,1536]{1,0:T(8,128)(2,1)S(1)} %get-tuple-element.31), channel_id=1, source_target_pairs={{0,6},{2,0},{4,2},{6,4},{1,7},{3,1},{5,3},{7,5},{8,14},{10,8},{12,... | collective-permute-start | bytes 589832 | tf_op jit(solution)/shard_map/ppermute | solution.py:91
  71.2 4.8 %all-to-all-done.2 = bf16[12,8,1536]{2,1,0:T(8,128)(2,1)S(1)} async-done(((bf16[12,8,1536]{2,1,0:T(8,128)(2,1)}), bf16[12,8,1536]{2,1,0:T(8,128)(2,1)S(1)}, u32[]{:S(2)}, u32[]{:S(2)}) %all-to-all-start.2) | async-done | bytes 294944 | tf_op jit(solution)/shard_map/all_to_all | solution.py:87
  76.0 0.0 copy-done.1
  76.0 0.1 multiply_reduce_fusion.1
  76.2 0.0 copy-done.3
  76.2 0.7 subtract_multiply_fusion.1
  76.9 0.0 collective-permute-done.2
  76.9 0.0 collective-permute-done.3
  76.9 0.0 collective-permute-done.4
  76.9 0.1 fusion.28
  77.0 11.6 %all_to_all.20 = bf16[8,8,1536]{2,1,0:T(8,128)(2,1)S(1)} all-to-all(bf16[8,8,1536]{2,1,0:T(8,128)(2,1)S(1)} %fusion.28), channel_id=1, replica_groups={{384,0,96,672,192,576,288,480},{385,1,97,673,193,577,289,481},{386,2,98..., dimensions={0} | all-to-all | bytes 393216 | tf_op jit(solution)/shard_map/all_to_all | solution.py:87
  88.6 0.0 copy-done
  88.6 0.1 multiply_reduce_fusion
  88.8 0.0 copy-done.2
  88.8 0.7 subtract_multiply_fusion
  (14 shorter events, 0.1 us)
Async XLA Ops:
  2.2 14.5 %all-to-all-start.1 = ((bf16[8,8,1536]{2,1,0:T(8,128)(2,1)}), bf16[8,8,1536]{2,1,0:T(8,128)(2,1)S(1)}, u32[]{:S(2)}, u32[]{:S(2)}) async-start(bf16[8,8,1536]{2,1,0:T(8,128)(2,1)} %shard_map.96), calls=%async_computation.1 | async-start | bytes 393216 | tf_op jit(solution)/shard_map/all_to_all | solution.py:87
  16.8 32.2 %copy-start.4 = (s32[256]{0:T(256)S(1)}, s32[256]{0:T(256)}, u32[]{:S(2)}) copy-start(s32[256]{0:T(256)} %constant.54.clone) | copy-start | bytes 3076
  16.8 32.2 %copy-start.5 = (f32[1,256]{1,0:T(1,128)S(1)}, f32[1,256]{1,0:T(1,128)}, u32[]{:S(2)}) copy-start(f32[1,256]{1,0:T(1,128)} %get-tuple-element.18) | copy-start | bytes 3076
  16.8 32.2 %copy-start.6 = (f32[1,256]{1,0:T(1,128)S(1)}, f32[1,256]{1,0:T(1,128)}, u32[]{:S(2)}) copy-start(f32[1,256]{1,0:T(1,128)} %get-tuple-element.20) | copy-start | bytes 3076
  16.8 32.2 %all-to-all-start = ((bf16[12,8,1536]{2,1,0:T(8,128)(2,1)}), bf16[12,8,1536]{2,1,0:T(8,128)(2,1)S(1)}, u32[]{:S(2)}, u32[]{:S(2)}) async-start(bf16[12,8,1536]{2,1,0:T(8,128)(2,1)} %get-tuple-element.19), calls=%async_computation | async-start | bytes 589824 | tf_op jit(solution)/shard_map/all_to_all | solution.py:87
  47.1 5.1 %collective-permute-start = (bf16[256,1536]{1,0:T(8,128)(2,1)S(1)}, bf16[256,1536]{1,0:T(8,128)(2,1)S(1)}, u32[]{:S(2)}, u32[]{:S(2)}) collective-permute-start(bf16[256,1536]{1,0:T(8,128)(2,1)S(1)} %all_gather.3), channel_id=1, source_target_pairs={{0,1},{1,0},{2,3},{3,2},{4,5},{5,4},{6,7},{7,6},{8,9},{9,8},{10,11... | collective-permute-start | bytes 2359304 | tf_op jit(solution)/shard_map/ppermute | solution.py:91
  49.7 3.8 %collective-permute-start.1 = (bf16[96,1536]{1,0:T(8,128)(2,1)S(1)}, bf16[96,1536]{1,0:T(8,128)(2,1)S(1)}, u32[]{:S(2)}, u32[]{:S(2)}) collective-permute-start(bf16[96,1536]{1,0:T(8,128)(2,1)S(1)} %bitcast.77), channel_id=1, source_target_pairs={{0,1},{1,0},{2,3},{3,2},{4,5},{5,4},{6,7},{7,6},{8,9},{9,8},{10,11... | collective-permute-start | bytes 884744 | tf_op jit(solution)/shard_map/ppermute | solution.py:91
  53.6 22.4 %all-to-all-start.2 = ((bf16[12,8,1536]{2,1,0:T(8,128)(2,1)}), bf16[12,8,1536]{2,1,0:T(8,128)(2,1)S(1)}, u32[]{:S(2)}, u32[]{:S(2)}) async-start(bf16[12,8,1536]{2,1,0:T(8,128)(2,1)} %bitcast.31), calls=%async_computation.2 | async-start | bytes 589824 | tf_op jit(solution)/shard_map/all_to_all | solution.py:87
  61.9 14.2 %copy-start.1 = (f32[8,1536]{1,0:T(8,128)S(1)}, f32[8,1536]{1,0:T(8,128)}, u32[]{:S(2)}) copy-start(f32[8,1536]{1,0:T(8,128)} %get-tuple-element.24) | copy-start | bytes 147460
  61.9 14.3 %copy-start.3 = (f32[8,1536]{1,0:T(8,128)S(1)}, f32[8,1536]{1,0:T(8,128)}, u32[]{:S(2)}) copy-start(f32[8,1536]{1,0:T(8,128)} %get-tuple-element.25) | copy-start | bytes 147460
  62.0 14.9 %collective-permute-start.2 = (bf16[64,1536]{1,0:T(8,128)(2,1)S(1)}, bf16[64,1536]{1,0:T(8,128)(2,1)S(1)}, u32[]{:S(2)}, u32[]{:S(2)}) collective-permute-start(bf16[64,1536]{1,0:T(8,128)(2,1)S(1)} %get-tuple-element.30), channel_id=1, source_target_pairs={{0,4},{2,6},{4,0},{6,2},{1,5},{3,7},{5,1},{7,3},{8,12},{10,14},{12... | collective-permute-start | bytes 589832 | tf_op jit(solution)/shard_map/ppermute | solution.py:91
  65.4 11.5 %collective-permute-start.3 = (bf16[64,1536]{1,0:T(8,128)(2,1)S(1)}, bf16[64,1536]{1,0:T(8,128)(2,1)S(1)}, u32[]{:S(2)}, u32[]{:S(2)}) collective-permute-start(bf16[64,1536]{1,0:T(8,128)(2,1)S(1)} %get-tuple-element.32), channel_id=1, source_target_pairs={{0,2},{2,4},{4,6},{6,0},{1,3},{3,5},{5,7},{7,1},{8,10},{10,12},{12... | collective-permute-start | bytes 589832 | tf_op jit(solution)/shard_map/ppermute | solution.py:91
  67.3 9.6 %collective-permute-start.4 = (bf16[64,1536]{1,0:T(8,128)(2,1)S(1)}, bf16[64,1536]{1,0:T(8,128)(2,1)S(1)}, u32[]{:S(2)}, u32[]{:S(2)}) collective-permute-start(bf16[64,1536]{1,0:T(8,128)(2,1)S(1)} %get-tuple-element.31), channel_id=1, source_target_pairs={{0,6},{2,0},{4,2},{6,4},{1,7},{3,1},{5,3},{7,5},{8,14},{10,8},{12,... | collective-permute-start | bytes 589832 | tf_op jit(solution)/shard_map/ppermute | solution.py:91
  76.9 11.8 %copy-start = (f32[8,1536]{1,0:T(8,128)S(1)}, f32[8,1536]{1,0:T(8,128)}, u32[]{:S(2)}) copy-start(f32[8,1536]{1,0:T(8,128)} %get-tuple-element.28) | copy-start | bytes 147460
  76.9 11.9 %copy-start.2 = (f32[8,1536]{1,0:T(8,128)S(1)}, f32[8,1536]{1,0:T(8,128)}, u32[]{:S(2)}) copy-start(f32[8,1536]{1,0:T(8,128)} %get-tuple-element.29) | copy-start | bytes 147460

commit v12 on v10

--- a/solution.py
+++ b/solution.py
@@ -8,7 +8,7 @@
 epsilon = 1e-06
 AXES = ("y", "z", "x", "core")
 NY, NZ, NX, NC = 8, 12, 4, 2
-FIRST_Z = 10
+FIRST_Z, FIRST_X = 10, 2
 Y_ORDER = [4, 0, 1, 7, 2, 6, 3, 5]
 R = 8
 f32 = jnp.float32
@@ -33,21 +33,21 @@
 
 
 def image_kernel(
-    image_ref, image_exponent_ref, text_ref, text_exponent_ref, scale_ref, bias_ref,
+    image_ref, image_exponent_ref, text_ref, text_exponent_ref, affine_ref,
     send_ref, image_unit_ref, image_gain_ref, text_unit_ref, text_gain_ref, scale_row_ref, bias_row_ref,
 ):
     norm, unit = unit_rows(image_ref, image_exponent_ref)
     half = unit.astype(bf16)
     for k in range(NZ):
         send_ref[k] = half
-    factor = scale_ref[0]
+    factor = affine_ref[0]
     image_unit_ref[...] = unit
     image_gain_ref[...] = jnp.broadcast_to(factor / norm, unit.shape)
     norm, unit = unit_rows(text_ref, text_exponent_ref)
     text_unit_ref[...] = unit
     text_gain_ref[...] = jnp.broadcast_to(factor / norm, unit.shape)
     scale_row_ref[...] = jnp.full(scale_row_ref.shape, factor, f32)
-    bias_row_ref[...] = jnp.full(bias_row_ref.shape, bias_ref[0], f32)
+    bias_row_ref[...] = jnp.full(bias_row_ref.shape, affine_ref[1], f32)
 
 
 vmem = pl.BlockSpec(memory_space=pltpu.VMEM)
@@ -63,7 +63,7 @@
     )(mantissa, exponent)
 
 
-def image_prologue(image, image_exponent, text, text_exponent, scale, bias):
+def image_prologue(image, image_exponent, text, text_exponent, affine):
     d = image.shape[1]
     rows = jax.ShapeDtypeStruct((R, d), f32)
     row = jax.ShapeDtypeStruct((1, NX * NY * R), f32)
@@ -72,9 +72,9 @@
         out_shape=(
             jax.ShapeDtypeStruct((NZ, R, d), bf16), rows, rows, rows, rows, row, row,
         ),
-        in_specs=[vmem, smem, vmem, smem, smem, smem],
+        in_specs=[vmem, smem, vmem, smem, smem],
         out_specs=(vmem,) * 7,
-    )(image, image_exponent, text, text_exponent, scale, bias)
+    )(image, image_exponent, text, text_exponent, affine)
 
 
 def ring(n, first):
@@ -119,9 +119,9 @@
     text_send = text_prologue(text_mantissa, text_exponent)
     image_mantissa, place, far_place = lax.optimization_barrier((image_mantissa, place, far_place))
     image_send, image_unit, image_gain, text_unit, text_gain, scale, bias = image_prologue(
-        image_mantissa, image_exponent, text_mantissa, text_exponent, logit_scale, logit_bias
+        image_mantissa, image_exponent, text_mantissa, text_exponent, jnp.concatenate([logit_scale, logit_bias])
     )
-    texts = lax.all_gather(exchange(text_send, "y", Y_ORDER).reshape(half_rows, d), "x", axis=0, tiled=True)
+    texts = lax.all_gather(exchange(text_send, "y", Y_ORDER).reshape(half_rows, d), "x", axis=0, tiled=True, axis_index_groups=[ring(NX, FIRST_X)])
     far_texts = shift(texts, "core", NC, 1)
     images = exchange(image_send, "z", ring(NZ, FIRST_Z)).reshape(own, d)
     far_images = shift(images, "core", NC, 1)
@@ -130,7 +130,7 @@
     held = jnp.asarray([k * R + r for _ in range(NX) for k in Y_ORDER for r in range(R)], jnp.int32)[None, :]
 
     def weigh(images, place, texts, core):
-        target = (column // half_rows * NC + core) * half_rows + held
+        target = ((column // half_rows + FIRST_X) % NX * NC + core) * half_rows + held
         logits = scale * product(images, texts.T) + bias
         label_sign = jnp.where(place[:, None] == target, 1.0, -1.0).astype(f32)
         return (-label_sign * jax.nn.sigmoid(-label_sign * logits)).astype(bf16)
@@ -146,7 +146,7 @@
     images = jnp.concatenate([images, far_images], axis=0)
     part = product(weights.T, images).astype(bf16).reshape(NX, half_rows, d)
     ways = range(NX)
-    blocks = [rows_at(part, (x + k) & (NX - 1), 1).reshape(half_rows, d) for k in ways]
+    blocks = [rows_at(part, (x + k - FIRST_X) & (NX - 1), 1).reshape(half_rows, d) for k in ways]
     image_parts = exchange(image_part.reshape(NZ, R, d), "z", ring(NZ, 3))
     unit_grad_image = image_parts.astype(f32).sum(axis=0)
 

time: 90.2 us -> 90.2 us (level)
  transfers between devices with their start and end apart: 8 -> 8, of which waited for: 3 -> 3; matrix products, arithmetic and copies ran while one was open for 5% -> 6% of each run, Pallas kernels for 2% -> 2%
where the time goes in v12:
time: 90.2 us; the launch traced here: 89.3 us
  starting transfers between devices  46.1 us (51%)
  blocking collectives  25.7 us (28%)
  waiting for transfers between devices  5.46 us (6%)
  other arithmetic  3.32 us (4%)
  Pallas kernels  3.31 us (4%)
  matrix products  2.82 us (3%)
  between operations  2.17 us (2%)
    all_to_all x3, starting transfers between devices, exchange(): lax.all_to_all(blocks, axis, split_axis=0, concat_axis=0, axis_index_grou...  32.6 us
    all_gather x1, blocking collectives, shards(): lax.all_gather(exchange(text_send, 'y', Y_ORDER).reshape(half_rows, d), '...  14.3 us
    ppermute x5, starting transfers between devices, shift(): return lax.ppermute(block, axis, [(i, (i + k) % n) for i in range(n)])  13.5 us
    all_to_all x1, blocking collectives, exchange(): lax.all_to_all(blocks, axis, split_axis=0, concat_axis=0, axis_index_grou...  11.4 us
    all_to_all x3, waiting for transfers between devices, exchange(): lax.all_to_all(blocks, axis, split_axis=0, concat_axis=0, axis_index_grou...  5.23 us
    dot_general x6, matrix products, product(): return jnp.dot(a, b, preferred_element_type=f32)  2.82 us
  transfers between devices with their start and end apart: 8, of which 3 were waited for; matrix products, arithmetic and copies ran while one was open for 6% of the time, Pallas kernels for 2%

profile of v12, /device:TPU:6, one launch (start us, length us, event | category | flops | bytes accessed | tf_op | source)
XLA Modules:
  0.0 89.3 jit_solution(14865851511557351774)
XLA Ops:
  0.6 1.6 %shard_map.96 = bf16[8,8,1536]{2,1,0:T(8,128)(2,1)} custom-call(bf16[8,1536]{1,0:T(8,128)(2,1)} %mantissa_ref.1, s32[8]{0:T(128)} %exponent_ref.1), custom_call_target="tpu_custom_call" | custom-call | tf_op jit(solution)/shard_map/pallas_call | solution.py:58
  2.2 9.1 %all-to-all-start.1 = ((bf16[8,8,1536]{2,1,0:T(8,128)(2,1)}), bf16[8,8,1536]{2,1,0:T(8,128)(2,1)S(1)}, u32[]{:S(2)}, u32[]{:S(2)}) async-start(bf16[8,8,1536]{2,1,0:T(8,128)(2,1)} %shard_map.96), calls=%async_computation.1 | async-start | bytes 393216 | tf_op jit(solution)/shard_map/all_to_all | solution.py:85
  11.4 0.7 broadcast_subtract_fusion
  12.0 0.1 sub.51
  12.2 0.1 sub.53
  12.3 0.1 slice_bitcast_fusion.1
  12.3 0.1 pad_add_fusion
  12.4 0.1 pad_add_fusion.1
  13.8 0.6 pad_maximum_fusion.affine_ref
  14.5 1.7 %shard_map.95 = (bf16[12,8,1536]{2,1,0:T(8,128)(2,1)}, f32[8,1536]{1,0:T(8,128)}, f32[8,1536]{1,0:T(8,128)}, f32[8,1536]{1,0:T(8,128)}, f32[8,1536]{1,0:T(8,128)}, /*index=5*/f32[1,256]{1,0:T(1,128)}, f32[1,256]{1,0:T(1,128)}) custom-call(bf16[8,1536]{1,0:T(8,128)(2,1)} %image_ref, s32[8]{0:T(128)} %image_exponent_ref.1, bf16[8,1536]{1,0:T(8,128)(2,1)} %mantissa_ref.1, ...), custom_call_target="tpu_custom_call" | custom-call | tf_op jit(solution)/shard_map/pallas_call | solution.py:70
  16.2 0.6 all-to-all-done.1
  16.8 16.2 %all-to-all-start = ((bf16[12,8,1536]{2,1,0:T(8,128)(2,1)}), bf16[12,8,1536]{2,1,0:T(8,128)(2,1)S(1)}, u32[]{:S(2)}, u32[]{:S(2)}) async-start(bf16[12,8,1536]{2,1,0:T(8,128)(2,1)} %get-tuple-element.19), calls=%async_computation | async-start | bytes 589824 | tf_op jit(solution)/shard_map/all_to_all | solution.py:85
  33.0 14.3 %all_gather.3 = bf16[256,1536]{1,0:T(8,128)(2,1)S(1)} all-gather(bf16[64,1536]{1,0:T(8,128)(2,1)S(1)} %bitcast.36), channel_id=1, replica_groups={{4,6,0,2},{5,7,1,3},{12,14,8,10},{13,15,9,11},{20,22,16,18},{21,23,17,1..., dimensions={0}, use_global_device_ids=true | all-gather | bytes 983040 | tf_op jit(solution)/shard_map/all_gather | solution.py:124
  47.3 1.9 %collective-permute-start = (bf16[256,1536]{1,0:T(8,128)(2,1)S(1)}, bf16[256,1536]{1,0:T(8,128)(2,1)S(1)}, u32[]{:S(2)}, u32[]{:S(2)}) collective-permute-start(bf16[256,1536]{1,0:T(8,128)(2,1)S(1)} %all_gather.3), channel_id=1, source_target_pairs={{0,1},{1,0},{2,3},{3,2},{4,5},{5,4},{6,7},{7,6},{8,9},{9,8},{10,11... | collective-permute-start | bytes 2359304 | tf_op jit(solution)/shard_map/ppermute | solution.py:89
  49.2 0.0 copy-done.4
  49.3 0.0 all-to-all-done
  49.3 0.0 copy-done.5
  49.3 0.0 copy-done.6
  49.3 0.4 fusion.24
  49.7 0.3 fusion.32
  50.0 2.4 %collective-permute-start.1 = (bf16[96,1536]{1,0:T(8,128)(2,1)S(1)}, bf16[96,1536]{1,0:T(8,128)(2,1)S(1)}, u32[]{:S(2)}, u32[]{:S(2)}) collective-permute-start(bf16[96,1536]{1,0:T(8,128)(2,1)S(1)} %bitcast.37), channel_id=1, source_target_pairs={{0,1},{1,0},{2,3},{3,2},{4,5},{5,4},{6,7},{7,6},{8,9},{9,8},{10,11... | collective-permute-start | bytes 884744 | tf_op jit(solution)/shard_map/ppermute | solution.py:89
  52.4 0.0 collective-permute-done
  52.4 0.4 fusion.23
  52.8 1.0 %fusion = bf16[96,1536]{1,0:T(8,128)(2,1)} fusion(f32[96,1536]{1,0:T(8,128)S(1)} %fusion.32, bf16[256,1536]{1,0:T(8,128)(2,1)S(1)} %collective-permute-done, bf16[40,256]{1,0:T(8,128)(2,1)S(1)} %slice.55, bf16[56,256]{1,0:T(8,128)(2,1)S(1)} %slice.54), kind=kOutput, calls=%fused_computation.2 | convolution fusion | flops 75890688 | bytes 1720320 | tf_op jit(solution)/shard_map/dot_general | solution.py:98
  53.8 0.0 collective-permute-done.1
  53.8 7.2 %all-to-all-start.2 = ((bf16[12,8,1536]{2,1,0:T(8,128)(2,1)}), bf16[12,8,1536]{2,1,0:T(8,128)(2,1)S(1)}, u32[]{:S(2)}, u32[]{:S(2)}) async-start(bf16[12,8,1536]{2,1,0:T(8,128)(2,1)} %bitcast.11), calls=%async_computation.2 | async-start | bytes 589824 | tf_op jit(solution)/shard_map/all_to_all | solution.py:85
  61.1 0.4 fusion.22
  61.5 0.4 convolution_convert_fusion
  61.9 0.0 copy-start.1
  61.9 0.0 copy-start.3
  61.9 0.1 dynamic-slice_bitcast_fusion.2
  62.0 3.4 %collective-permute-start.2 = (bf16[64,1536]{1,0:T(8,128)(2,1)S(1)}, bf16[64,1536]{1,0:T(8,128)(2,1)S(1)}, u32[]{:S(2)}, u32[]{:S(2)}) collective-permute-start(bf16[64,1536]{1,0:T(8,128)(2,1)S(1)} %get-tuple-element.30), channel_id=1, source_target_pairs={{0,4},{2,6},{4,0},{6,2},{1,5},{3,7},{5,1},{7,3},{8,12},{10,14},{12... | collective-permute-start | bytes 589832 | tf_op jit(solution)/shard_map/ppermute | solution.py:89
  65.3 2.4 %collective-permute-start.3 = (bf16[64,1536]{1,0:T(8,128)(2,1)S(1)}, bf16[64,1536]{1,0:T(8,128)(2,1)S(1)}, u32[]{:S(2)}, u32[]{:S(2)}) collective-permute-start(bf16[64,1536]{1,0:T(8,128)(2,1)S(1)} %get-tuple-element.32), channel_id=1, source_target_pairs={{0,2},{2,4},{4,6},{6,0},{1,3},{3,5},{5,7},{7,1},{8,10},{10,12},{12... | collective-permute-start | bytes 589832 | tf_op jit(solution)/shard_map/ppermute | solution.py:89
  67.8 3.4 %collective-permute-start.4 = (bf16[64,1536]{1,0:T(8,128)(2,1)S(1)}, bf16[64,1536]{1,0:T(8,128)(2,1)S(1)}, u32[]{:S(2)}, u32[]{:S(2)}) collective-permute-start(bf16[64,1536]{1,0:T(8,128)(2,1)S(1)} %get-tuple-element.31), channel_id=1, source_target_pairs={{0,6},{2,0},{4,2},{6,4},{1,7},{3,1},{5,3},{7,5},{8,14},{10,8},{12,... | collective-permute-start | bytes 589832 | tf_op jit(solution)/shard_map/ppermute | solution.py:89
  71.2 4.6 %all-to-all-done.2 = bf16[12,8,1536]{2,1,0:T(8,128)(2,1)S(1)} async-done(((bf16[12,8,1536]{2,1,0:T(8,128)(2,1)}), bf16[12,8,1536]{2,1,0:T(8,128)(2,1)S(1)}, u32[]{:S(2)}, u32[]{:S(2)}) %all-to-all-start.2) | async-done | bytes 294944 | tf_op jit(solution)/shard_map/all_to_all | solution.py:85
  75.8 0.0 copy-done.1
  75.9 0.1 multiply_reduce_fusion.1
  76.0 0.0 copy-done.3
  76.0 0.7 subtract_multiply_fusion.1
  76.7 0.0 collective-permute-done.2
  76.7 0.0 collective-permute-done.3
  76.7 0.2 collective-permute-done.4
  76.9 0.1 fusion.28
  77.0 11.4 %all_to_all.20 = bf16[8,8,1536]{2,1,0:T(8,128)(2,1)S(1)} all-to-all(bf16[8,8,1536]{2,1,0:T(8,128)(2,1)S(1)} %fusion.28), channel_id=1, replica_groups={{384,0,96,672,192,576,288,480},{385,1,97,673,193,577,289,481},{386,2,98..., dimensions={0} | all-to-all | bytes 393216 | tf_op jit(solution)/shard_map/all_to_all | solution.py:85
  88.5 0.0 copy-done
  88.5 0.1 multiply_reduce_fusion
  88.6 0.0 copy-done.2
  88.6 0.7 subtract_multiply_fusion
  (15 shorter events, 0.1 us)
Async XLA Ops:
  2.2 14.5 %all-to-all-start.1 = ((bf16[8,8,1536]{2,1,0:T(8,128)(2,1)}), bf16[8,8,1536]{2,1,0:T(8,128)(2,1)S(1)}, u32[]{:S(2)}, u32[]{:S(2)}) async-start(bf16[8,8,1536]{2,1,0:T(8,128)(2,1)} %shard_map.96), calls=%async_computation.1 | async-start | bytes 393216 | tf_op jit(solution)/shard_map/all_to_all | solution.py:85
  16.8 32.5 %copy-start.4 = (s32[256]{0:T(256)S(1)}, s32[256]{0:T(256)}, u32[]{:S(2)}) copy-start(s32[256]{0:T(256)} %constant.81.clone) | copy-start | bytes 3076
  16.8 32.5 %copy-start.5 = (f32[1,256]{1,0:T(1,128)S(1)}, f32[1,256]{1,0:T(1,128)}, u32[]{:S(2)}) copy-start(f32[1,256]{1,0:T(1,128)} %get-tuple-element.18) | copy-start | bytes 3076
  16.8 32.5 %copy-start.6 = (f32[1,256]{1,0:T(1,128)S(1)}, f32[1,256]{1,0:T(1,128)}, u32[]{:S(2)}) copy-start(f32[1,256]{1,0:T(1,128)} %get-tuple-element.20) | copy-start | bytes 3076
  16.8 32.5 %all-to-all-start = ((bf16[12,8,1536]{2,1,0:T(8,128)(2,1)}), bf16[12,8,1536]{2,1,0:T(8,128)(2,1)S(1)}, u32[]{:S(2)}, u32[]{:S(2)}) async-start(bf16[12,8,1536]{2,1,0:T(8,128)(2,1)} %get-tuple-element.19), calls=%async_computation | async-start | bytes 589824 | tf_op jit(solution)/shard_map/all_to_all | solution.py:85
  47.3 5.1 %collective-permute-start = (bf16[256,1536]{1,0:T(8,128)(2,1)S(1)}, bf16[256,1536]{1,0:T(8,128)(2,1)S(1)}, u32[]{:S(2)}, u32[]{:S(2)}) collective-permute-start(bf16[256,1536]{1,0:T(8,128)(2,1)S(1)} %all_gather.3), channel_id=1, source_target_pairs={{0,1},{1,0},{2,3},{3,2},{4,5},{5,4},{6,7},{7,6},{8,9},{9,8},{10,11... | collective-permute-start | bytes 2359304 | tf_op jit(solution)/shard_map/ppermute | solution.py:89
  50.0 3.8 %collective-permute-start.1 = (bf16[96,1536]{1,0:T(8,128)(2,1)S(1)}, bf16[96,1536]{1,0:T(8,128)(2,1)S(1)}, u32[]{:S(2)}, u32[]{:S(2)}) collective-permute-start(bf16[96,1536]{1,0:T(8,128)(2,1)S(1)} %bitcast.37), channel_id=1, source_target_pairs={{0,1},{1,0},{2,3},{3,2},{4,5},{5,4},{6,7},{7,6},{8,9},{9,8},{10,11... | collective-permute-start | bytes 884744 | tf_op jit(solution)/shard_map/ppermute | solution.py:89
  53.8 22.0 %all-to-all-start.2 = ((bf16[12,8,1536]{2,1,0:T(8,128)(2,1)}), bf16[12,8,1536]{2,1,0:T(8,128)(2,1)S(1)}, u32[]{:S(2)}, u32[]{:S(2)}) async-start(bf16[12,8,1536]{2,1,0:T(8,128)(2,1)} %bitcast.11), calls=%async_computation.2 | async-start | bytes 589824 | tf_op jit(solution)/shard_map/all_to_all | solution.py:85
  61.9 14.0 %copy-start.1 = (f32[8,1536]{1,0:T(8,128)S(1)}, f32[8,1536]{1,0:T(8,128)}, u32[]{:S(2)}) copy-start(f32[8,1536]{1,0:T(8,128)} %get-tuple-element.24) | copy-start | bytes 147460
  61.9 14.1 %copy-start.3 = (f32[8,1536]{1,0:T(8,128)S(1)}, f32[8,1536]{1,0:T(8,128)}, u32[]{:S(2)}) copy-start(f32[8,1536]{1,0:T(8,128)} %get-tuple-element.25) | copy-start | bytes 147460
  62.0 14.7 %collective-permute-start.2 = (bf16[64,1536]{1,0:T(8,128)(2,1)S(1)}, bf16[64,1536]{1,0:T(8,128)(2,1)S(1)}, u32[]{:S(2)}, u32[]{:S(2)}) collective-permute-start(bf16[64,1536]{1,0:T(8,128)(2,1)S(1)} %get-tuple-element.30), channel_id=1, source_target_pairs={{0,4},{2,6},{4,0},{6,2},{1,5},{3,7},{5,1},{7,3},{8,12},{10,14},{12... | collective-permute-start | bytes 589832 | tf_op jit(solution)/shard_map/ppermute | solution.py:89
  65.3 11.4 %collective-permute-start.3 = (bf16[64,1536]{1,0:T(8,128)(2,1)S(1)}, bf16[64,1536]{1,0:T(8,128)(2,1)S(1)}, u32[]{:S(2)}, u32[]{:S(2)}) collective-permute-start(bf16[64,1536]{1,0:T(8,128)(2,1)S(1)} %get-tuple-element.32), channel_id=1, source_target_pairs={{0,2},{2,4},{4,6},{6,0},{1,3},{3,5},{5,7},{7,1},{8,10},{10,12},{12... | collective-permute-start | bytes 589832 | tf_op jit(solution)/shard_map/ppermute | solution.py:89
  67.8 9.2 %collective-permute-start.4 = (bf16[64,1536]{1,0:T(8,128)(2,1)S(1)}, bf16[64,1536]{1,0:T(8,128)(2,1)S(1)}, u32[]{:S(2)}, u32[]{:S(2)}) collective-permute-start(bf16[64,1536]{1,0:T(8,128)(2,1)S(1)} %get-tuple-element.31), channel_id=1, source_target_pairs={{0,6},{2,0},{4,2},{6,4},{1,7},{3,1},{5,3},{7,5},{8,14},{10,8},{12,... | collective-permute-start | bytes 589832 | tf_op jit(solution)/shard_map/ppermute | solution.py:89
  76.7 11.8 %copy-start = (f32[8,1536]{1,0:T(8,128)S(1)}, f32[8,1536]{1,0:T(8,128)}, u32[]{:S(2)}) copy-start(f32[8,1536]{1,0:T(8,128)} %get-tuple-element.28) | copy-start | bytes 147460
  76.7 11.9 %copy-start.2 = (f32[8,1536]{1,0:T(8,128)S(1)}, f32[8,1536]{1,0:T(8,128)}, u32[]{:S(2)}) copy-start(f32[8,1536]{1,0:T(8,128)} %get-tuple-element.29) | copy-start | bytes 147460
